TPU v7x, 32 devices: a whole 2x2x4 slice. The times are simulated.
32 devices in a mesh: rows: 16 (over z, y, core), sub: 2 (over x).
Axes of the slice: x: 2, y: 2, z: 4, core: 2. Of those that a mesh axis runs over, the one named last changes fastest.
Arguments:
- features: bfloat16 [131072, 512], P(('rows', 'sub')), may hold values from -16 to 16
- residual: float32 [131072, 128], P(('rows', 'sub')), may hold values from -6 to 6
- coefficients: float32 [131072, 128], P(('rows', 'sub')), may hold values from -6 to 6
- block_owner: int32 [2], replicated, may hold values from 0 to 31
- block_tiles: int32 [2, 4], replicated, may hold values from 0 to 31, as said below
Outputs:
- residual_out: float32 [131072, 128], P(('rows', 'sub'))
- coefficients_out: float32 [131072, 128], P(('rows', 'sub'))
Inputs may be any that keep to these rules, and one draw needn't show every extreme that they name: `block_tiles`: in each step the tile numbers are distinct, and tiles 0 and 31 are among them.
All inputs are finite; a program needn't handle non-finite values.
Results may differ from a plain program's by a relative error of at most 0.0012.
Values may be sent and summed in bfloat16 or wider, within the bound.
No kernel may reach another device: no remote copies, remote signals or barrier semaphores. Data moves between devices by JAX's collectives and lax.ppermute only.
A program may use at most 128 MiB of HBM per device.

v0:
```python
import functools
import math

import jax
import jax.numpy as jnp
from jax import lax
from jax.experimental import pallas as pl
from jax.experimental.pallas import tpu as pltpu
from jax.sharding import PartitionSpec as P

BLOCK = 512
TILE = 128
STEPS = 2
RIDGE = 0.5
AXES = ("rows", "sub")
HIGH = lax.Precision.HIGHEST
NT = (((1,), (1,)), ((), ()))
LOG2E = math.log2(math.e)
VMEM_LIMIT = 16 * 1024 * 1024
SMALL_LIMIT = 12 * 1024 * 1024


def pick_kernel(tiles_ref, core_ref, feat_ref, keep_ref, send_ref, sems):
    per_half = keep_ref.shape[1] // TILE
    copies = []
    for turn, out in enumerate((keep_ref, send_ref)):
        half = core_ref[0] if turn == 0 else 1 - core_ref[0]
        for s in range(STEPS):
            for i in range(per_half):
                source = pl.multiple_of(tiles_ref[s, half * per_half + i] * TILE, TILE)
                copies.append(
                    pltpu.make_async_copy(
                        feat_ref.at[pl.ds(source, TILE), :],
                        out.at[s, pl.ds(i * TILE, TILE), :],
                        sems.at[turn, s, i],
                    )
                )
    for copy in copies:
        copy.start()
    for copy in copies:
        copy.wait()


def pick_halves(features, block_tiles, core):
    width = features.shape[1]
    half = jax.ShapeDtypeStruct((STEPS, BLOCK // 2, width), features.dtype)
    return pl.pallas_call(
        pick_kernel,
        grid_spec=pltpu.PrefetchScalarGridSpec(
            num_scalar_prefetch=2,
            grid=(1,),
            in_specs=[pl.BlockSpec(memory_space=pltpu.HBM)],
            out_specs=[pl.BlockSpec(half.shape, lambda i, *_: (0, 0, 0))] * 2,
            scratch_shapes=[pltpu.SemaphoreType.DMA((2, STEPS, BLOCK // 2 // TILE))],
        ),
        out_shape=(half, half),
        compiler_params=pltpu.CompilerParams(vmem_limit_bytes=SMALL_LIMIT),
        name="pick",
    )(pltpu.with_memory_space_constraint(block_tiles, pltpu.HBM), core, pltpu.with_memory_space_constraint(features, pltpu.HBM))


def swap(value, axes, flip):
    flip_of = flip if callable(flip) else lambda i: flip
    return lax.ppermute(value, axes, [(i, i ^ flip_of(i)) for i in range(lax.axis_size(axes))])


def bit_of(index, mask):
    return ((index & mask) != 0).astype(jnp.int32)


def swap_among(pick, me, axes, low, high):
    place = bit_of(me, low) + 2 * bit_of(me, high)
    flips = [0, low, high, low | high]
    return place, [swap(pick(place ^ c), axes, flips[c]) for c in (1, 2, 3)]


def ordered(parts, me, low, high, axis):
    one, two = (me & low) != 0, (me & high) != 0
    parts = [jnp.where(one, parts[c ^ 1], parts[c]) for c in range(4)]
    return jnp.stack([jnp.where(two, parts[c ^ 2], parts[c]) for c in range(4)], axis=axis)


def fetch_blocks(features, norms, block_owner, block_tiles, me, devices, core):
    width = features.shape[1]
    low, high = 1, 2 * core
    differs = lambda mask: (((block_owner ^ me) & mask) != 0)[:, None, None]
    on_core = (me & core) != 0

    keep, send = pick_halves(features, block_tiles, bit_of(me, core).reshape(1))
    half = jnp.where(differs(core), swap(send, AXES, core), keep)
    quarters = half.reshape(STEPS, 4, BLOCK // 8, width)
    pick = lambda place: lax.dynamic_index_in_dim(quarters, place, 1, False)
    place, got = swap_among(pick, me, AXES, low, high)
    part = jnp.where(
        differs(high),
        jnp.where(differs(low), got[2], got[1]),
        jnp.where(differs(low), got[0], pick(place)),
    )
    far = [1 << b for b in range(devices.bit_length() - 1) if 1 << b not in (core, low, high)]
    hops = []
    for one, two in zip(far[::2], far[1::2]):
        for first, second in ((one, two), (two, one)):
            flip = lambda i, first=first, second=second: second if i & core else first
            hops.append((flip, jnp.where(on_core, second, first)))
    if len(far) % 2:
        hops.append((far[-1], far[-1]))
    for hop, (flip, mask) in enumerate(hops):
        other = swap(part, AXES, flip)
        if hop == len(hops) - 2:
            other, norms = lax.optimization_barrier((other, norms))
        part = jnp.where(differs(mask), other, part)
    _, got = swap_among(lambda place: part, me, AXES, low, high)
    half = ordered([part] + got, me, low, high, 1)
    other = swap(half, AXES, core)
    both = jnp.stack([jnp.where(on_core, other, half), jnp.where(on_core, half, other)], axis=1)
    return both.reshape(STEPS * BLOCK, width), norms


def pack(value, exact):
    high = lax.reduce_precision(value[..., :exact, :], 8, 7)
    low = value[..., :exact, :] - high
    return jnp.concatenate([part.astype(jnp.bfloat16) for part in (high, low, value[..., exact:, :])], axis=-2)


def unpack(value, exact):
    value = value.astype(jnp.float32)
    return jnp.concatenate([value[..., :exact, :] + value[..., exact : 2 * exact, :], value[..., 2 * exact :, :]], axis=-2)


class Spread:
    def __init__(self, axes, core):
        self.axes, self.core = axes, core
        self.me = lax.axis_index(axes).astype(jnp.int32)
        self.near = [1 << b for b in range(3) if 1 << b != core]
        self.far = [1 << b for b in range(3, lax.axis_size(axes).bit_length() - 1)]
        self.count = 8
        self.core_axis = 2 - (core.bit_length() - 1)

    def core_sum(self, value):
        value = value.reshape((2,) * 3 + value.shape[1:])
        zero, one = (lax.index_in_dim(value, i, self.core_axis, False) for i in (0, 1))
        bit = (self.me & self.core) != 0
        value = jnp.where(bit, one, zero) + swap(jnp.where(bit, zero, one), self.axes, self.core)
        return value.reshape((4,) + value.shape[2:])

    def near_sum(self, value, exact):
        packed = pack(value, exact)
        pick = lambda array, place: lax.dynamic_index_in_dim(array, place, 0, False)
        place, got = swap_among(lambda place: pick(packed, place), self.me, self.axes, *self.near)
        return lambda got: pick(value, place) + unpack(got[0], exact) + unpack(got[1], exact) + unpack(got[2], exact), got

    def far_sum(self, value, exact, mask):
        return lambda got: value + unpack(got[0], exact), [swap(pack(value, exact), self.axes, mask)]

    def near_gather(self, value):
        _, got = swap_among(lambda place: value, self.me, self.axes, *self.near)
        return lambda got: ordered([value] + got, self.me, *self.near, 0), got

    def core_gather(self, value):
        rest = value.shape[1:]
        value = value.reshape((2, 2) + rest)
        bit = (self.me & self.core) != 0
        got = swap(value, self.axes, self.core)
        value = jnp.stack([jnp.where(bit, got, value), jnp.where(bit, value, got)], axis=self.core_axis)
        return value.reshape((self.count,) + rest)


def scaled_norm(rows, scale):
    wide = rows.astype(jnp.float32)
    return jnp.sum(wide * wide, axis=1, keepdims=True) * scale


def gram_kernel(scale, core_ref, block_ref, slab_ref, own_ref, cross_ref):
    mine = block_ref[pl.ds(pl.multiple_of(core_ref[0] * BLOCK, BLOCK), BLOCK), :]
    eye = jnp.where(
        lax.broadcasted_iota(jnp.int32, (BLOCK, BLOCK), 0)
        == lax.broadcasted_iota(jnp.int32, (BLOCK, BLOCK), 1),
        RIDGE,
        0.0,
    )
    for left, right, shift, out in (
        (mine, mine, eye, own_ref),
        (block_ref[:BLOCK], block_ref[BLOCK:], 0.0, cross_ref),
    ):
        dots = lax.dot_general(left, right, NT, preferred_element_type=jnp.float32)
        right_norm = scaled_norm(right, scale)
        row = jnp.transpose(jnp.broadcast_to(right_norm, (BLOCK, 128)))[:1]
        value = jnp.exp(dots * (2.0 * scale) - scaled_norm(left, scale) - row)
        out[...] = (value + shift).astype(out.dtype)


def gram(block, core, scale, slab):
    square = (BLOCK, BLOCK)
    vmem = pl.BlockSpec(memory_space=pltpu.VMEM)
    return pl.pallas_call(
        functools.partial(gram_kernel, scale),
        in_specs=[pl.BlockSpec(memory_space=pltpu.SMEM), vmem, vmem],
        out_shape=(jax.ShapeDtypeStruct(square, jnp.float32), jax.ShapeDtypeStruct(square, jnp.bfloat16)),
        compiler_params=pltpu.CompilerParams(vmem_limit_bytes=SMALL_LIMIT),
        cost_estimate=pl.CostEstimate(
            flops=2 * 2 * BLOCK**3, bytes_accessed=4 * BLOCK * BLOCK * 4, transcendentals=2 * BLOCK**2
        ),
        name="gram",
    )(core, block, in_vmem(slab))


def slab_kernel(scale, chunk, block_ref, feat_ref, norm_ref, res_ref, coef_ref, slab_ref, piece_ref, bnorm, grad, cross, ahead_ref):
    scale2 = scale * LOG2E
    norm = scaled_norm(block_ref[...], scale2)
    bnorm[...] = jnp.broadcast_to(norm, bnorm.shape)
    grad[...] = jnp.zeros_like(grad)
    cross[...] = jnp.zeros_like(cross)
    part = BLOCK // 2
    parts = STEPS * BLOCK // part
    chunks = feat_ref.shape[0] // chunk
    rows_of = lambda i: pl.ds(pl.multiple_of(i * chunk, chunk), chunk)
    at_of = lambda p: slice(p * part, (p + 1) * part)

    def product(i, p):
        return lax.dot_general(block_ref[at_of(p)], feat_ref[rows_of(i), :], NT, preferred_element_type=jnp.float32)

    ahead_ref[...] = product(0, 0)

    def body(i, _):
        rows = rows_of(i)
        weighted = (res_ref[rows, :] - RIDGE * coef_ref[rows, :]).astype(jnp.bfloat16)
        norm_row = norm_ref[:, rows] * LOG2E
        dots = ahead_ref[...]
        for p in range(parts):
            ahead = product(i, p + 1) if p + 1 < parts else product(jnp.minimum(i + 1, chunks - 1), 0)
            norm_wide = jnp.concatenate([bnorm[at_of(p)]] * (chunk // bnorm.shape[1]), axis=1)
            slab = jnp.exp2(dots * (2.0 * scale2) - norm_wide - norm_row).astype(jnp.bfloat16)
            slab_ref[at_of(p), rows] = slab
            grad[at_of(p)] += jnp.dot(slab, weighted, preferred_element_type=jnp.float32)
            dots = ahead
        ahead_ref[...] = dots
        cross[...] += lax.dot_general(
            slab_ref[:BLOCK, rows], slab_ref[BLOCK:, rows], NT, preferred_element_type=jnp.float32
        )
        return 0

    lax.fori_loop(0, chunks, body, 0, unroll=2)
    grads = jnp.transpose(grad[...])
    groups = piece_ref.shape[0]
    own, depth = grads.shape[0] // groups, BLOCK // groups
    for d in range(groups):
        for s in range(STEPS):
            piece_ref[d, s * own : (s + 1) * own] = grads[d * own : (d + 1) * own, s * BLOCK : (s + 1) * BLOCK]
        piece_ref[d, STEPS * own :] = cross[d * depth : (d + 1) * depth]


def in_vmem(value):
    return pltpu.with_memory_space_constraint(value, pltpu.VMEM)


def slabs(block, features, norms, residual, coefficients, scale, groups, chunk=512):
    rows, width = features.shape
    targets = residual.shape[1]
    both = STEPS * BLOCK
    piece = (groups, STEPS * targets // groups + BLOCK // groups, BLOCK)
    return pl.pallas_call(
        functools.partial(slab_kernel, scale, chunk),
        out_shape=(pltpu.VMEM((both, rows), jnp.bfloat16), jax.ShapeDtypeStruct(piece, jnp.float32)),
        scratch_shapes=[
            pltpu.VMEM((both, 128), jnp.float32),
            pltpu.VMEM((both, targets), jnp.float32),
            pltpu.VMEM((BLOCK, BLOCK), jnp.float32),
            pltpu.VMEM((BLOCK // 2, chunk), jnp.float32),
        ],
        compiler_params=pltpu.CompilerParams(vmem_limit_bytes=VMEM_LIMIT),
        cost_estimate=pl.CostEstimate(
            flops=2 * rows * both * (width + targets + BLOCK // 2),
            bytes_accessed=rows * (width * 2 + targets * 8 + both * 2),
            transcendentals=rows * both,
        ),
        name="slabs",
    )(block, in_vmem(features), norms, in_vmem(residual), in_vmem(coefficients))


def reciprocal(x):
    guess = pl.reciprocal(x, approx=True)
    return guess * (2.0 - x * guess)


def eliminate(tiles, t, lane, scaled_ref):
    start, shape = 8 * t, tiles[t].shape
    wide = lambda tile, k: jnp.broadcast_to(tile[:, start + k : start + k + 1], shape)
    rows = [jnp.broadcast_to(tiles[t][k : k + 1], shape) for k in range(8)]
    at = {(i, k): wide(rows[i], k) for i in range(8) for k in range(i, 8)}
    units = [jnp.where(lane == start + k, 1.0, 0.0) for k in range(8)]
    rows = [row + unit for row, unit in zip(rows, units)]
    total, lower = [None] * 8, {}
    for r in range(0, 8, 2):
        p, m, q = at[r, r], at[r, r + 1], at[r + 1, r + 1]
        inverse = reciprocal(p * q - m * m)
        p, m, q = p * inverse, m * inverse, q * inverse
        for k in range(r + 2, 8):
            first = q * at[r, k] - m * at[r + 1, k]
            second = p * at[r + 1, k] - m * at[r, k]
            lower[r, k], lower[r + 1, k] = first, second
            for i in range(r + 2, k + 1):
                at[i, k] = at[i, k] - (at[r, i] * first + at[r + 1, i] * second)
            rows[k] = rows[k] - (first * rows[r] + second * rows[r + 1])
        total[r] = q * rows[r] - m * rows[r + 1]
        total[r + 1] = p * rows[r + 1] - m * rows[r]
    for r in (4, 2, 0):
        for k in range(r + 2, 8):
            total[r] = total[r] - lower[r, k] * total[k]
            total[r + 1] = total[r + 1] - lower[r + 1, k] * total[k]
    for k in range(8):
        scaled_ref[start + k : start + k + 1] = total[k][:1] - units[k][:1]
    for u in range(t + 1, len(tiles)):
        parts = [wide(tiles[u], k) * total[k] for k in range(8)]
        while len(parts) > 1:
            parts = [x + y for x, y in zip(parts[::2], parts[1::2])]
        tiles[u] = tiles[u] - parts[0]


def factor_kernel(index, copies, *refs):
    refs = list(refs)
    rest_ref, _ = refs.pop(0), refs.pop(0)
    if copies:
        source, scaled, sem = refs.pop(0), *refs[-2:]
        copy = pltpu.make_async_copy(source, refs[-3], sem)
        copy.start()
    else:
        scaled = refs[-1]
    last = rest_ref.shape[0] == TILE
    factor_ref = refs[0] if last else refs[1]
    here = slice(index * TILE, (index + 1) * TILE)
    row_ids = lax.broadcasted_iota(jnp.int32, (TILE, TILE), 0)
    col_ids = lax.broadcasted_iota(jnp.int32, (TILE, TILE), 1)
    lane = lax.broadcasted_iota(jnp.int32, (8, TILE), 1)
    tiles = [rest_ref[8 * t : 8 * t + 8, here] for t in range(TILE // 8)]
    for t in range(TILE // 8):
        eliminate(tiles, t, lane, scaled)
    start = row_ids - row_ids % 8
    dot = functools.partial(lax.dot_general, precision=HIGH, preferred_element_type=jnp.float32)
    lower = jnp.where(col_ids < start, jnp.concatenate(tiles, axis=0), 0.0)
    lower = lower + jnp.where(col_ids == row_ids, 1.0, 0.0)
    right = jnp.where(col_ids < start + 8, scaled[...], 0.0)
    inv = dot(lower, right, (((0,), (0,)), ((), ())))
    top = rest_ref[:TILE]
    panel = dot(inv, top, (((1,), (0,)), ((), ())))
    inside = lax.broadcasted_iota(jnp.int32, panel.shape, 1) // TILE == index
    panel = jnp.where(inside, jnp.concatenate([inv] * (BLOCK // TILE), axis=1), panel)
    factor_ref[:TILE] = top
    factor_ref[TILE:] = panel
    if not last:
        under = rest_ref[TILE:]
        change = dot(rest_ref[TILE:, here], panel, (((1,), (0,)), ((), ())))
        inside = lax.broadcasted_iota(jnp.int32, under.shape, 1) // TILE == index
        refs[0][...] = jnp.where(inside, 0.0, under) - change
    if copies:
        copy.wait()


def factor_step(rest, index, slab, copied=None):
    left = rest.shape[0] - TILE
    vmem, hbm = pl.BlockSpec(memory_space=pltpu.VMEM), pl.BlockSpec(memory_space=pltpu.HBM)
    out = [jax.ShapeDtypeStruct((left, BLOCK), jnp.float32)] if left else []
    out.append(jax.ShapeDtypeStruct((2 * TILE, BLOCK), jnp.float32))
    inputs, in_specs, out_specs = [rest, in_vmem(slab)], [vmem] * 2, [vmem] * len(out)
    scratch = [pltpu.VMEM((TILE, TILE), jnp.float32)]
    if copied is not None:
        inputs.append(in_vmem(copied))
        in_specs.append(vmem)
        out.append(pltpu.HBM(copied.shape, copied.dtype))
        out_specs.append(hbm)
        scratch.append(pltpu.SemaphoreType.DMA)
    out = pl.pallas_call(
        functools.partial(factor_kernel, index, copied is not None),
        in_specs=in_specs,
        out_specs=tuple(out_specs),
        out_shape=tuple(out),
        scratch_shapes=scratch,
        compiler_params=pltpu.CompilerParams(vmem_limit_bytes=SMALL_LIMIT),
        cost_estimate=pl.CostEstimate(flops=6 * 10**9, bytes_accessed=4 * 1024 * 1024, transcendentals=0),
        name="factor",
    )(*inputs)
    out = list(out)
    below = out.pop(0) if left else None
    return (below,) + tuple(out)


def apply_inverse(value, refs):
    ids = lambda axis: lax.broadcasted_iota(jnp.int32, (TILE, BLOCK), axis)
    lower, right = [], []
    for k in range(BLOCK // TILE):
        rest, panel = refs[k][:TILE], refs[k][TILE:]
        unit = jnp.where(ids(1) == ids(0) + k * TILE, 1.0, 0.0)
        lower.append(jnp.where(ids(1) < k * TILE, rest, unit))
        right.append(jnp.where(ids(1) < (k + 1) * TILE, panel, 0.0))
    lower, right = jnp.concatenate(lower, axis=0), jnp.concatenate(right, axis=0)
    middle = lax.dot_general(value, right, NT, precision=HIGH, preferred_element_type=jnp.float32)
    return jnp.dot(middle, lower, precision=HIGH, preferred_element_type=jnp.float32)


def final_kernel(step_size, chunk, owner_ref, tiles_ref, me_ref, packed_ref, gram_ref, slab_ref, res_ref, coef_ref, base_ref, *refs):
    factors, refs = refs[: 2 * (BLOCK // TILE)], refs[2 * (BLOCK // TILE) :]
    res_out, coef_out, upd_ref, wide_ref, ahead_ref, res_buf, tile_buf, res_sems, tile_sems = refs
    rows, targets = res_ref.shape
    own = targets // packed_ref.shape[0]
    exact = STEPS * own
    count = BLOCK // TILE

    def gradient(s):
        high = packed_ref[:, s * own : (s + 1) * own].astype(jnp.float32)
        low = packed_ref[:, exact + s * own : exact + (s + 1) * own].astype(jnp.float32)
        return (high + low).reshape(targets, BLOCK)

    dot = functools.partial(jnp.dot, preferred_element_type=jnp.float32)
    first = apply_inverse(gradient(0), factors[:count]) * step_size
    high = first.astype(jnp.bfloat16)
    low = (first - high.astype(jnp.float32)).astype(jnp.bfloat16)
    cross = packed_ref[:, 2 * exact :].reshape(BLOCK, BLOCK)
    block_part = dot(high, gram_ref[...]) + dot(low, gram_ref[...])
    again = gradient(1) - dot(high, cross) - RIDGE * block_part
    second = apply_inverse(again, factors[count:]) * step_size
    wide_ref[:, :BLOCK] = first
    wide_ref[:, BLOCK:] = second
    upd_ref[:, :BLOCK] = high
    upd_ref[:, BLOCK:] = second.astype(jnp.bfloat16)

    def change_of(s, k):
        at = s * BLOCK + k * TILE
        return jnp.transpose(wide_ref[:, at : at + TILE])

    def tile_rows(s, k):
        return pl.ds(pl.multiple_of(tiles_ref[s, k] * TILE, TILE), TILE)

    def tile_copy(s, k):
        return pltpu.make_async_copy(tile_buf.at[s, k], coef_out.at[tile_rows(s, k), :], tile_sems.at[s, k])

    owned = [owner_ref[s] == me_ref[0] for s in range(STEPS)]

    def writes(s, k):
        kept = owned[s]
        for later in range(s + 1, STEPS):
            for j in range(count):
                kept = kept & jnp.logical_not(owned[later] & (tiles_ref[later, j] == tiles_ref[s, k]))
        return kept

    for s in range(STEPS):
        for k in range(count):

            @pl.when(writes(s, k))
            def _():
                tile_buf[s, k] = coef_ref[tile_rows(s, k), :] + change_of(s, k)
                for earlier in range(s):
                    for j in range(count):

                        @pl.when(owned[earlier] & (tiles_ref[earlier, j] == tiles_ref[s, k]))
                        def _():
                            tile_buf[s, k] += change_of(earlier, j)

                tile_copy(s, k).start()

    chunks = rows // chunk
    rows_of = lambda i: pl.ds(pl.multiple_of(i * chunk, chunk), chunk)

    def res_copy(i):
        return pltpu.make_async_copy(res_buf.at[rows_of(i), :], res_out.at[rows_of(i), :], res_sems.at[i])

    def product(i):
        return jnp.dot(upd_ref[...], slab_ref[:, rows_of(i)], preferred_element_type=jnp.float32)

    ahead_ref[...] = product(0)

    def body(i, _):
        change = ahead_ref[...]
        ahead = product(jnp.minimum(i + 1, chunks - 1))
        res_buf[rows_of(i), :] = res_ref[rows_of(i), :] - jnp.transpose(change)
        ahead_ref[...] = ahead
        res_copy(i).start()
        return 0

    lax.fori_loop(0, chunks, body, 0)
    for i in range(rows // chunk):
        res_copy(i).wait()
    for s in range(STEPS):
        for k in range(count):

            @pl.when(writes(s, k))
            def _():
                tile_copy(s, k).wait()


def finish(owner, tiles, me, packed, gram12, slab, residual, coefficients, base, factors, step_size, chunk=512):
    rows, targets = residual.shape
    both = STEPS * BLOCK
    count = BLOCK // TILE
    smem, vmem, hbm = (pl.BlockSpec(memory_space=space) for space in (pltpu.SMEM, pltpu.VMEM, pltpu.HBM))
    return pl.pallas_call(
        functools.partial(final_kernel, step_size, chunk),
        in_specs=[smem] * 3 + [vmem] * 5 + [hbm] + [vmem] * len(factors),
        out_specs=(hbm, hbm),
        out_shape=(
            pltpu.HBM(residual.shape, jnp.float32),
            pltpu.HBM(residual.shape, jnp.float32),
        ),
        scratch_shapes=[
            pltpu.VMEM((targets, both), jnp.bfloat16),
            pltpu.VMEM((targets, both), jnp.float32),
            pltpu.VMEM((targets, chunk), jnp.float32),
            pltpu.VMEM((rows, targets), jnp.float32),
            pltpu.VMEM((STEPS, count, TILE, targets), jnp.float32),
            pltpu.SemaphoreType.DMA((rows // chunk,)),
            pltpu.SemaphoreType.DMA((STEPS, count)),
        ],
        input_output_aliases={8: 1},
        compiler_params=pltpu.CompilerParams(vmem_limit_bytes=VMEM_LIMIT),
        cost_estimate=pl.CostEstimate(
            flops=2 * rows * both * targets, bytes_accessed=rows * (both * 2 + targets * 16), transcendentals=0
        ),
        name="finish",
    )(owner, tiles, me, packed, gram12, in_vmem(slab), in_vmem(residual), in_vmem(coefficients), base, *factors)


def local(features, residual, coefficients, block_owner, block_tiles):
    rows_dev, width = features.shape
    targets = residual.shape[1]
    sub_count = lax.axis_size("sub")
    devices = lax.axis_size("rows") * sub_count
    me = lax.axis_index(AXES).astype(jnp.int32)
    scale = 1.0 / width
    step_size = 1.0 / math.sqrt(rows_dev * devices)
    spread = Spread(AXES, sub_count) if devices <= 32 else Spread(("rows",), 1)
    groups = spread.count
    own = targets // groups

    wide = features.astype(jnp.float32)
    norms = (jnp.sum(wide * wide, axis=1) * scale).reshape(1, rows_dev)
    block, norms = fetch_blocks(features, norms, block_owner, block_tiles, me, devices, sub_count)
    slab, pieces = slabs(block, features, norms, residual, coefficients, scale, groups)
    if spread.axes != AXES:
        pieces = lax.psum(pieces, "sub")
    core, on_core = bit_of(me, sub_count), (me & sub_count) != 0
    rest, gram12 = gram(block, core.reshape(1), scale, slab)
    factors, base = ([], []), None

    def beside(hop, index, rest):
        then, got = hop
        below, mine, *copied = factor_step(rest, index, slab, coefficients if index == 0 else None)
        got, below, mine = lax.optimization_barrier((got, below, mine))
        other = swap(mine, AXES, sub_count)
        factors[0].append(jnp.where(on_core, other, mine))
        factors[1].append(jnp.where(on_core, mine, other))
        return then(got), below, copied

    value = spread.core_sum(pieces)
    value, rest, (base,) = beside(spread.near_sum(value, STEPS * own), 0, rest)
    for index, mask in enumerate(spread.far):
        value, rest, _ = beside(spread.far_sum(value, STEPS * own, mask), 1 + index, rest)
    packed, rest, _ = beside(spread.near_gather(pack(value, STEPS * own)), 3, rest)
    packed = spread.core_gather(packed)
    return finish(
        block_owner, block_tiles, me.reshape(1), packed, gram12, slab, residual, coefficients, base,
        factors[0] + factors[1], step_size,
    )


def solution(mesh):
    row_spec = P(AXES, None)
    return jax.shard_map(
        local,
        mesh=mesh,
        in_specs=(row_spec, row_spec, row_spec, P(), P()),
        out_specs=(row_spec, row_spec),
        check_vma=False,
    )
```

profile of v0, /device:TPU:0, one launch (start us, length us, event | category | flops | bytes accessed | tf_op | source)
XLA Modules:
  0.0 103.2 jit_solution(7938832617867009830)
XLA Ops:
  0.6 2.2 %pick.1 = (bf16[2,256,512]{2,1,0:T(8,128)(2,1)S(1)}, bf16[2,256,512]{2,1,0:T(8,128)(2,1)S(1)}) custom-call(s32[2,4]{1,0:T(2,128)} %tiles_ref.3, s32[1]{0:T(128)} %bitcast.1.core_ref, bf16[4096,512]{1,0:T(8,128)(2,1)} %feat_ref.3), custom_call_target="tpu_custom_call" | custom-call | tf_op jit(solution)/shard_map/pick/pallas_call | solution.py:47
  3.4 1.5 %collective-permute-done = bf16[2,256,512]{2,1,0:T(8,128)(2,1)S(1)} collective-permute-done((bf16[2,256,512]{2,1,0:T(8,128)(2,1)S(1)}, bf16[2,256,512]{2,1,0:T(8,128)(2,1)S(1)}, u32[]{:S(2)}, u32[]{:S(2)}) %collective-permute-start) | collective-permute-done | bytes 524320 | tf_op jit(solution)/shard_map/ppermute | solution.py:64
  5.1 3.0 %collective-permute-start.2 = (bf16[2,64,512]{2,1,0:T(8,128)(2,1)S(1)}, bf16[2,64,512]{2,1,0:T(8,128)(2,1)S(1)}, u32[]{:S(2)}, u32[]{:S(2)}) collective-permute-start(bf16[2,64,512]{2,1,0:T(8,128)(2,1)S(1)} %get-tuple-element.89), channel_id=1, source_target_pairs={{0,4},{1,5},{2,6},{3,7},{4,0},{5,1},{6,2},{7,3},{8,12},{9,13},{10,... | collective-permute-start | bytes 393224 | tf_op jit(solution)/shard_map/ppermute | solution.py:64
  8.0 1.5 %collective-permute-start.3 = (bf16[2,64,512]{2,1,0:T(8,128)(2,1)S(1)}, bf16[2,64,512]{2,1,0:T(8,128)(2,1)S(1)}, u32[]{:S(2)}, u32[]{:S(2)}) collective-permute-start(bf16[2,64,512]{2,1,0:T(8,128)(2,1)S(1)} %get-tuple-element.90), channel_id=1, source_target_pairs={{0,1},{1,0},{2,3},{3,2},{4,5},{5,4},{6,7},{7,6},{8,9},{9,8},{10,11... | collective-permute-start | bytes 393224 | tf_op jit(solution)/shard_map/ppermute | solution.py:64
  9.6 3.2 %multiply_reduce_fusion = f32[4096]{0:T(1024)S(1)} fusion(bf16[4096,512]{1,0:T(8,128)(2,1)} %feat_ref.3), kind=kLoop, calls=%fused_computation | loop fusion | flops 6287360 | bytes 4210688 | tf_op jit(solution)/shard_map/reduce_sum | solution.py:533
  12.8 1.6 %collective-permute-done.3 = bf16[2,64,512]{2,1,0:T(8,128)(2,1)S(1)} collective-permute-done((bf16[2,64,512]{2,1,0:T(8,128)(2,1)S(1)}, bf16[2,64,512]{2,1,0:T(8,128)(2,1)S(1)}, u32[]{:S(2)}, u32[]{:S(2)}) %collective-permute-start.3) | collective-permute-done | bytes 131104 | tf_op jit(solution)/shard_map/ppermute | solution.py:64
  14.4 1.5 %collective-permute-done.1 = bf16[2,64,512]{2,1,0:T(8,128)(2,1)S(1)} collective-permute-done((bf16[2,64,512]{2,1,0:T(8,128)(2,1)S(1)}, bf16[2,64,512]{2,1,0:T(8,128)(2,1)S(1)}, u32[]{:S(2)}, u32[]{:S(2)}) %collective-permute-start.1) | collective-permute-done | bytes 131104 | tf_op jit(solution)/shard_map/ppermute | solution.py:64
  16.0 1.8 %collective-permute-start.4 = (bf16[2,64,512]{2,1,0:T(8,128)(2,1)S(1)}, bf16[2,64,512]{2,1,0:T(8,128)(2,1)S(1)}, u32[]{:S(2)}, u32[]{:S(2)}) collective-permute-start(bf16[2,64,512]{2,1,0:T(8,128)(2,1)S(1)} %fusion.5), channel_id=1, source_target_pairs={{0,8},{1,9},{2,18},{3,19},{4,12},{5,13},{6,22},{7,23},{8,0},{9,1},... | collective-permute-start | bytes 393224 | tf_op jit(solution)/shard_map/ppermute | solution.py:64
  17.8 3.7 %collective-permute-done.4 = bf16[2,64,512]{2,1,0:T(8,128)(2,1)S(1)} collective-permute-done((bf16[2,64,512]{2,1,0:T(8,128)(2,1)S(1)}, bf16[2,64,512]{2,1,0:T(8,128)(2,1)S(1)}, u32[]{:S(2)}, u32[]{:S(2)}) %collective-permute-start.4) | collective-permute-done | bytes 131104 | tf_op jit(solution)/shard_map/ppermute | solution.py:64
  21.6 2.7 %collective-permute-start.5 = (bf16[2,64,512]{2,1,0:T(8,128)(2,1)S(1)}, bf16[2,64,512]{2,1,0:T(8,128)(2,1)S(1)}, u32[]{:S(2)}, u32[]{:S(2)}) collective-permute-start(bf16[2,64,512]{2,1,0:T(8,128)(2,1)S(1)} %broadcast_select_fusion.9), channel_id=1, source_target_pairs={{0,16},{1,17},{2,10},{3,11},{4,20},{5,21},{6,14},{7,15},{8,24},{9,... | collective-permute-start | bytes 393224 | tf_op jit(solution)/shard_map/ppermute | solution.py:64
  24.3 3.3 %collective-permute-done.5 = bf16[2,64,512]{2,1,0:T(8,128)(2,1)S(1)} collective-permute-done((bf16[2,64,512]{2,1,0:T(8,128)(2,1)S(1)}, bf16[2,64,512]{2,1,0:T(8,128)(2,1)S(1)}, u32[]{:S(2)}, u32[]{:S(2)}) %collective-permute-start.5) | collective-permute-done | bytes 131104 | tf_op jit(solution)/shard_map/ppermute | solution.py:64
  27.6 1.3 %collective-permute-start.8 = (bf16[2,64,512]{2,1,0:T(8,128)(2,1)S(1)}, bf16[2,64,512]{2,1,0:T(8,128)(2,1)S(1)}, u32[]{:S(2)}, u32[]{:S(2)}) collective-permute-start(bf16[2,64,512]{2,1,0:T(8,128)(2,1)S(1)} %broadcast_select_fusion.10), channel_id=1, source_target_pairs={{0,1},{1,0},{2,3},{3,2},{4,5},{5,4},{6,7},{7,6},{8,9},{9,8},{10,11... | collective-permute-start | bytes 393224 | tf_op jit(solution)/shard_map/ppermute | solution.py:64
  28.9 1.5 %collective-permute-start.7 = (bf16[2,64,512]{2,1,0:T(8,128)(2,1)S(1)}, bf16[2,64,512]{2,1,0:T(8,128)(2,1)S(1)}, u32[]{:S(2)}, u32[]{:S(2)}) collective-permute-start(bf16[2,64,512]{2,1,0:T(8,128)(2,1)S(1)} %broadcast_select_fusion.10), channel_id=1, source_target_pairs={{0,4},{1,5},{2,6},{3,7},{4,0},{5,1},{6,2},{7,3},{8,12},{9,13},{10,... | collective-permute-start | bytes 393224 | tf_op jit(solution)/shard_map/ppermute | solution.py:64
  31.2 2.1 %collective-permute-done.8 = bf16[2,64,512]{2,1,0:T(8,128)(2,1)S(1)} collective-permute-done((bf16[2,64,512]{2,1,0:T(8,128)(2,1)S(1)}, bf16[2,64,512]{2,1,0:T(8,128)(2,1)S(1)}, u32[]{:S(2)}, u32[]{:S(2)}) %collective-permute-start.8) | collective-permute-done | bytes 131104 | tf_op jit(solution)/shard_map/ppermute | solution.py:64
  33.2 1.3 %collective-permute-done.7 = bf16[2,64,512]{2,1,0:T(8,128)(2,1)S(1)} collective-permute-done((bf16[2,64,512]{2,1,0:T(8,128)(2,1)S(1)}, bf16[2,64,512]{2,1,0:T(8,128)(2,1)S(1)}, u32[]{:S(2)}, u32[]{:S(2)}) %collective-permute-start.7) | collective-permute-done | bytes 131104 | tf_op jit(solution)/shard_map/ppermute | solution.py:64
  34.5 1.8 %collective-permute-done.6 = bf16[2,64,512]{2,1,0:T(8,128)(2,1)S(1)} collective-permute-done((bf16[2,64,512]{2,1,0:T(8,128)(2,1)S(1)}, bf16[2,64,512]{2,1,0:T(8,128)(2,1)S(1)}, u32[]{:S(2)}, u32[]{:S(2)}) %collective-permute-start.6) | collective-permute-done | bytes 131104 | tf_op jit(solution)/shard_map/ppermute | solution.py:64
  36.5 1.9 %collective-permute-done.9 = bf16[2,4,64,512]{3,2,1,0:T(8,128)(2,1)S(1)} collective-permute-done((bf16[2,4,64,512]{3,2,1,0:T(8,128)(2,1)S(1)}, bf16[2,4,64,512]{3,2,1,0:T(8,128)(2,1)S(1)}, u32[]{:S(2)}, u32[]{:S(2)}) %collective-permute-start.9) | collective-permute-done | bytes 524320 | tf_op jit(solution)/shard_map/ppermute | solution.py:64
  39.1 10.7 %slabs.1 = (bf16[1024,4096]{1,0:T(8,128)(2,1)S(1)}, f32[8,96,512]{2,1,0:T(8,128)S(1)}) custom-call(bf16[1024,512]{1,0:T(8,128)(2,1)S(1)} %bitcast.81, bf16[4096,512]{1,0:T(8,128)(2,1)S(1)} %copy-done, f32[1,4096]{1,0:T(1,128)S(1)} %bitcast.84, f32[4096,128]{1,0:T(8,128)S(1)} %copy-done.1, f32[4096,128]{1,0:T(8,128)S(1)} %copy-done.2), custom_call_target="tpu_custom_call" | custom-call | flops 7516192768 | bytes 16777216 | tf_op jit(solution)/shard_map/slabs/pallas_call | solution.py:261
  50.1 1.0 gram.1
  51.1 1.3 %collective-permute-done.10 = f32[2,2,96,512]{3,2,1,0:T(8,128)S(1)} collective-permute-done((f32[2,2,96,512]{3,2,1,0:T(8,128)S(1)}, f32[2,2,96,512]{3,2,1,0:T(8,128)S(1)}, u32[]{:S(2)}, u32[]{:S(2)}) %collective-permute-start.10) | collective-permute-done | bytes 786464 | tf_op jit(solution)/shard_map/ppermute | solution.py:64
  52.8 0.8 collective-permute-start.13
  53.6 1.2 %collective-permute-start.12 = (bf16[128,512]{1,0:T(8,128)(2,1)S(1)}, bf16[128,512]{1,0:T(8,128)(2,1)S(1)}, u32[]{:S(2)}, u32[]{:S(2)}) collective-permute-start(bf16[128,512]{1,0:T(8,128)(2,1)S(1)} %get-tuple-element.83), channel_id=1, source_target_pairs={{0,4},{1,5},{2,6},{3,7},{4,0},{5,1},{6,2},{7,3},{8,12},{9,13},{10,... | collective-permute-start | bytes 393224 | tf_op jit(solution)/shard_map/ppermute | solution.py:64
  54.8 1.5 %collective-permute-start.11 = (bf16[128,512]{1,0:T(8,128)(2,1)S(1)}, bf16[128,512]{1,0:T(8,128)(2,1)S(1)}, u32[]{:S(2)}, u32[]{:S(2)}) collective-permute-start(bf16[128,512]{1,0:T(8,128)(2,1)S(1)} %get-tuple-element.84), channel_id=1, source_target_pairs={{0,1},{1,0},{2,3},{3,2},{4,5},{5,4},{6,7},{7,6},{8,9},{9,8},{10,11... | collective-permute-start | bytes 393224 | tf_op jit(solution)/shard_map/ppermute | solution.py:64
  56.3 6.5 %factor.4 = (f32[384,512]{1,0:T(8,128)S(1)}, f32[256,512]{1,0:T(8,128)S(1)}, f32[4096,128]{1,0:T(8,128)}) custom-call(f32[512,512]{1,0:T(8,128)S(1)} %get-tuple-element.38.refs_0_, bf16[1024,4096]{1,0:T(8,128)(2,1)S(1)} %get-tuple-element.37.slab_ref.refs_1_, f32[4096,128]{1,0:T(8,128)S(1)} %copy-done.2), custom_call_target="tpu_custom_call" | custom-call | flops 6000000000 | bytes 4194304 | tf_op jit(solution)/shard_map/factor/pallas_call | solution.py:371
  63.2 2.5 %collective-permute-start.14 = (bf16[128,512]{1,0:T(8,128)(2,1)S(1)}, bf16[128,512]{1,0:T(8,128)(2,1)S(1)}, u32[]{:S(2)}, u32[]{:S(2)}) collective-permute-start(bf16[128,512]{1,0:T(8,128)(2,1)S(1)} %pad_maximum_fusion.5), channel_id=1, source_target_pairs={{0,8},{1,9},{2,10},{3,11},{4,12},{5,13},{6,14},{7,15},{8,0},{9,1},... | collective-permute-start | bytes 393224 | tf_op jit(solution)/shard_map/ppermute | solution.py:64
  65.8 6.3 %factor.5 = (f32[256,512]{1,0:T(8,128)S(1)}, f32[256,512]{1,0:T(8,128)S(1)}) custom-call(f32[384,512]{1,0:T(8,128)S(1)} %get-tuple-element.44.refs_0_, bf16[1024,4096]{1,0:T(8,128)(2,1)S(1)} %get-tuple-element.37.slab_ref.refs_1_), custom_call_target="tpu_custom_call" | custom-call | flops 6000000000 | bytes 4194304 | tf_op jit(solution)/shard_map/factor/pallas_call | solution.py:371
  72.3 3.4 %collective-permute-start.15 = (bf16[128,512]{1,0:T(8,128)(2,1)S(1)}, bf16[128,512]{1,0:T(8,128)(2,1)S(1)}, u32[]{:S(2)}, u32[]{:S(2)}) collective-permute-start(bf16[128,512]{1,0:T(8,128)(2,1)S(1)} %pad_maximum_fusion.6), channel_id=1, source_target_pairs={{0,16},{1,17},{2,18},{3,19},{4,20},{5,21},{6,22},{7,23},{8,24},{9,... | collective-permute-start | bytes 393224 | tf_op jit(solution)/shard_map/ppermute | solution.py:64
  75.7 6.3 %factor.6 = (f32[128,512]{1,0:T(8,128)S(1)}, f32[256,512]{1,0:T(8,128)S(1)}) custom-call(f32[256,512]{1,0:T(8,128)S(1)} %get-tuple-element.48.refs_0_, bf16[1024,4096]{1,0:T(8,128)(2,1)S(1)} %get-tuple-element.37.slab_ref.refs_1_), custom_call_target="tpu_custom_call" | custom-call | flops 6000000000 | bytes 4194304 | tf_op jit(solution)/shard_map/factor/pallas_call | solution.py:371
  83.0 1.5 %collective-permute-start.17 = (bf16[128,512]{1,0:T(8,128)(2,1)S(1)}, bf16[128,512]{1,0:T(8,128)(2,1)S(1)}, u32[]{:S(2)}, u32[]{:S(2)}) collective-permute-start(bf16[128,512]{1,0:T(8,128)(2,1)S(1)} %pad_maximum_fusion.7), channel_id=1, source_target_pairs={{0,4},{1,5},{2,6},{3,7},{4,0},{5,1},{6,2},{7,3},{8,12},{9,13},{10,... | collective-permute-start | bytes 393224 | tf_op jit(solution)/shard_map/ppermute | solution.py:64
  84.5 1.5 %collective-permute-start.16 = (bf16[128,512]{1,0:T(8,128)(2,1)S(1)}, bf16[128,512]{1,0:T(8,128)(2,1)S(1)}, u32[]{:S(2)}, u32[]{:S(2)}) collective-permute-start(bf16[128,512]{1,0:T(8,128)(2,1)S(1)} %pad_maximum_fusion.7), channel_id=1, source_target_pairs={{0,1},{1,0},{2,3},{3,2},{4,5},{5,4},{6,7},{7,6},{8,9},{9,8},{10,11... | collective-permute-start | bytes 393224 | tf_op jit(solution)/shard_map/ppermute | solution.py:64
  86.0 5.8 %factor.7 = f32[256,512]{1,0:T(8,128)S(1)} custom-call(f32[128,512]{1,0:T(8,128)S(1)} %get-tuple-element.52.refs_0_, bf16[1024,4096]{1,0:T(8,128)(2,1)S(1)} %get-tuple-element.37.slab_ref.refs_1_), custom_call_target="tpu_custom_call" | custom-call | flops 6000000000 | bytes 4194304 | tf_op jit(solution)/shard_map/factor/pallas_call | solution.py:371
  95.4 7.6 %finish.1 = (f32[4096,128]{1,0:T(8,128)}, f32[4096,128]{1,0:T(8,128)}) custom-call(s32[2]{0:T(128)S(1)} %copy-done.4, s32[2,4]{1,0:T(2,128)S(1)} %copy-done.3, s32[1]{0:T(128)} %bitcast.me_ref, bf16[8,128,512]{2,1,0:T(8,128)(2,1)S(1)} %bitcast.83, bf16[512,512]{1,0:T(8,128)(2,1)S(1)} %get-tuple-element.56.gram_ref, ...), custom_call_target="tpu_custom_call", output_to_operand_aliasing={{1}: (8, {})} | custom-call | flops 1073741824 | bytes 16777216 | tf_op jit(solution)/shard_map/finish/pallas_call | solution.py:494
  (87 shorter events, 8.1 us)
Async XLA Ops:
  0.6 2.7 %copy-start.4 = (s32[2]{0:T(128)S(1)}, s32[2]{0:T(128)}, u32[]{:S(2)}) copy-start(s32[2]{0:T(128)} %owner_ref.1) | copy-start | bytes 28
  2.8 2.1 %collective-permute-start = (bf16[2,256,512]{2,1,0:T(8,128)(2,1)S(1)}, bf16[2,256,512]{2,1,0:T(8,128)(2,1)S(1)}, u32[]{:S(2)}, u32[]{:S(2)}) collective-permute-start(bf16[2,256,512]{2,1,0:T(8,128)(2,1)S(1)} %get-tuple-element.32), channel_id=1, source_target_pairs={{0,2},{1,3},{2,0},{3,1},{4,6},{5,7},{6,4},{7,5},{8,10},{9,11},{10,... | collective-permute-start | bytes 1572872 | tf_op jit(solution)/shard_map/ppermute | solution.py:64
  5.1 7.7 %collective-permute-start.2 = (bf16[2,64,512]{2,1,0:T(8,128)(2,1)S(1)}, bf16[2,64,512]{2,1,0:T(8,128)(2,1)S(1)}, u32[]{:S(2)}, u32[]{:S(2)}) collective-permute-start(bf16[2,64,512]{2,1,0:T(8,128)(2,1)S(1)} %get-tuple-element.89), channel_id=1, source_target_pairs={{0,4},{1,5},{2,6},{3,7},{4,0},{5,1},{6,2},{7,3},{8,12},{9,13},{10,... | collective-permute-start | bytes 393224 | tf_op jit(solution)/shard_map/ppermute | solution.py:64
  8.0 6.4 %collective-permute-start.3 = (bf16[2,64,512]{2,1,0:T(8,128)(2,1)S(1)}, bf16[2,64,512]{2,1,0:T(8,128)(2,1)S(1)}, u32[]{:S(2)}, u32[]{:S(2)}) collective-permute-start(bf16[2,64,512]{2,1,0:T(8,128)(2,1)S(1)} %get-tuple-element.90), channel_id=1, source_target_pairs={{0,1},{1,0},{2,3},{3,2},{4,5},{5,4},{6,7},{7,6},{8,9},{9,8},{10,11... | collective-permute-start | bytes 393224 | tf_op jit(solution)/shard_map/ppermute | solution.py:64
  9.5 6.4 %collective-permute-start.1 = (bf16[2,64,512]{2,1,0:T(8,128)(2,1)S(1)}, bf16[2,64,512]{2,1,0:T(8,128)(2,1)S(1)}, u32[]{:S(2)}, u32[]{:S(2)}) collective-permute-start(bf16[2,64,512]{2,1,0:T(8,128)(2,1)S(1)} %get-tuple-element.91), channel_id=1, source_target_pairs={{0,5},{1,4},{2,7},{3,6},{4,1},{5,0},{6,3},{7,2},{8,13},{9,12},{10,... | collective-permute-start | bytes 393224 | tf_op jit(solution)/shard_map/ppermute | solution.py:64
  9.6 29.0 %copy-start.2 = (f32[4096,128]{1,0:T(8,128)S(1)}, f32[4096,128]{1,0:T(8,128)}, u32[]{:S(2)}) copy-start(f32[4096,128]{1,0:T(8,128)} %coef_ref.3) | copy-start | bytes 6291460
  16.0 5.5 %collective-permute-start.4 = (bf16[2,64,512]{2,1,0:T(8,128)(2,1)S(1)}, bf16[2,64,512]{2,1,0:T(8,128)(2,1)S(1)}, u32[]{:S(2)}, u32[]{:S(2)}) collective-permute-start(bf16[2,64,512]{2,1,0:T(8,128)(2,1)S(1)} %fusion.5), channel_id=1, source_target_pairs={{0,8},{1,9},{2,18},{3,19},{4,12},{5,13},{6,22},{7,23},{8,0},{9,1},... | collective-permute-start | bytes 393224 | tf_op jit(solution)/shard_map/ppermute | solution.py:64
  21.6 5.9 %collective-permute-start.5 = (bf16[2,64,512]{2,1,0:T(8,128)(2,1)S(1)}, bf16[2,64,512]{2,1,0:T(8,128)(2,1)S(1)}, u32[]{:S(2)}, u32[]{:S(2)}) collective-permute-start(bf16[2,64,512]{2,1,0:T(8,128)(2,1)S(1)} %broadcast_select_fusion.9), channel_id=1, source_target_pairs={{0,16},{1,17},{2,10},{3,11},{4,20},{5,21},{6,14},{7,15},{8,24},{9,... | collective-permute-start | bytes 393224 | tf_op jit(solution)/shard_map/ppermute | solution.py:64
  27.6 5.6 %collective-permute-start.8 = (bf16[2,64,512]{2,1,0:T(8,128)(2,1)S(1)}, bf16[2,64,512]{2,1,0:T(8,128)(2,1)S(1)}, u32[]{:S(2)}, u32[]{:S(2)}) collective-permute-start(bf16[2,64,512]{2,1,0:T(8,128)(2,1)S(1)} %broadcast_select_fusion.10), channel_id=1, source_target_pairs={{0,1},{1,0},{2,3},{3,2},{4,5},{5,4},{6,7},{7,6},{8,9},{9,8},{10,11... | collective-permute-start | bytes 393224 | tf_op jit(solution)/shard_map/ppermute | solution.py:64
  28.9 5.6 %collective-permute-start.7 = (bf16[2,64,512]{2,1,0:T(8,128)(2,1)S(1)}, bf16[2,64,512]{2,1,0:T(8,128)(2,1)S(1)}, u32[]{:S(2)}, u32[]{:S(2)}) collective-permute-start(bf16[2,64,512]{2,1,0:T(8,128)(2,1)S(1)} %broadcast_select_fusion.10), channel_id=1, source_target_pairs={{0,4},{1,5},{2,6},{3,7},{4,0},{5,1},{6,2},{7,3},{8,12},{9,13},{10,... | collective-permute-start | bytes 393224 | tf_op jit(solution)/shard_map/ppermute | solution.py:64
  30.4 5.9 %collective-permute-start.6 = (bf16[2,64,512]{2,1,0:T(8,128)(2,1)S(1)}, bf16[2,64,512]{2,1,0:T(8,128)(2,1)S(1)}, u32[]{:S(2)}, u32[]{:S(2)}) collective-permute-start(bf16[2,64,512]{2,1,0:T(8,128)(2,1)S(1)} %broadcast_select_fusion.10), channel_id=1, source_target_pairs={{0,5},{1,4},{2,7},{3,6},{4,1},{5,0},{6,3},{7,2},{8,13},{9,12},{10,... | collective-permute-start | bytes 393224 | tf_op jit(solution)/shard_map/ppermute | solution.py:64
  36.3 2.3 %copy-start.1 = (f32[4096,128]{1,0:T(8,128)S(1)}, f32[4096,128]{1,0:T(8,128)}, u32[]{:S(2)}) copy-start(f32[4096,128]{1,0:T(8,128)} %res_ref.3) | copy-start | bytes 6291460
  36.4 2.7 %copy-start = (bf16[4096,512]{1,0:T(8,128)(2,1)S(1)}, bf16[4096,512]{1,0:T(8,128)(2,1)}, u32[]{:S(2)}) copy-start(bf16[4096,512]{1,0:T(8,128)(2,1)} %feat_ref.3) | copy-start | bytes 12582916
  36.4 2.0 %collective-permute-start.9 = (bf16[2,4,64,512]{3,2,1,0:T(8,128)(2,1)S(1)}, bf16[2,4,64,512]{3,2,1,0:T(8,128)(2,1)S(1)}, u32[]{:S(2)}, u32[]{:S(2)}) collective-permute-start(bf16[2,4,64,512]{3,2,1,0:T(8,128)(2,1)S(1)} %pad_maximum_fusion.2), channel_id=1, source_target_pairs={{0,2},{1,3},{2,0},{3,1},{4,6},{5,7},{6,4},{7,5},{8,10},{9,11},{10,... | collective-permute-start | bytes 1572872 | tf_op jit(solution)/shard_map/ppermute | solution.py:64
  50.0 2.4 %collective-permute-start.10 = (f32[2,2,96,512]{3,2,1,0:T(8,128)S(1)}, f32[2,2,96,512]{3,2,1,0:T(8,128)S(1)}, u32[]{:S(2)}, u32[]{:S(2)}) collective-permute-start(f32[2,2,96,512]{3,2,1,0:T(8,128)S(1)} %select_bitcast_fusion), channel_id=1, source_target_pairs={{0,2},{1,3},{2,0},{3,1},{4,6},{5,7},{6,4},{7,5},{8,10},{9,11},{10,... | collective-permute-start | bytes 2359304 | tf_op jit(solution)/shard_map/ppermute | solution.py:64
  52.8 10.1 %collective-permute-start.13 = (bf16[128,512]{1,0:T(8,128)(2,1)S(1)}, bf16[128,512]{1,0:T(8,128)(2,1)S(1)}, u32[]{:S(2)}, u32[]{:S(2)}) collective-permute-start(bf16[128,512]{1,0:T(8,128)(2,1)S(1)} %get-tuple-element.82), channel_id=1, source_target_pairs={{0,5},{1,4},{2,7},{3,6},{4,1},{5,0},{6,3},{7,2},{8,13},{9,12},{10,... | collective-permute-start | bytes 393224 | tf_op jit(solution)/shard_map/ppermute | solution.py:64
  53.6 9.3 %collective-permute-start.12 = (bf16[128,512]{1,0:T(8,128)(2,1)S(1)}, bf16[128,512]{1,0:T(8,128)(2,1)S(1)}, u32[]{:S(2)}, u32[]{:S(2)}) collective-permute-start(bf16[128,512]{1,0:T(8,128)(2,1)S(1)} %get-tuple-element.83), channel_id=1, source_target_pairs={{0,4},{1,5},{2,6},{3,7},{4,0},{5,1},{6,2},{7,3},{8,12},{9,13},{10,... | collective-permute-start | bytes 393224 | tf_op jit(solution)/shard_map/ppermute | solution.py:64
  54.8 8.1 %collective-permute-start.11 = (bf16[128,512]{1,0:T(8,128)(2,1)S(1)}, bf16[128,512]{1,0:T(8,128)(2,1)S(1)}, u32[]{:S(2)}, u32[]{:S(2)}) collective-permute-start(bf16[128,512]{1,0:T(8,128)(2,1)S(1)} %get-tuple-element.84), channel_id=1, source_target_pairs={{0,1},{1,0},{2,3},{3,2},{4,5},{5,4},{6,7},{7,6},{8,9},{9,8},{10,11... | collective-permute-start | bytes 393224 | tf_op jit(solution)/shard_map/ppermute | solution.py:64
  63.2 8.9 %collective-permute-start.14 = (bf16[128,512]{1,0:T(8,128)(2,1)S(1)}, bf16[128,512]{1,0:T(8,128)(2,1)S(1)}, u32[]{:S(2)}, u32[]{:S(2)}) collective-permute-start(bf16[128,512]{1,0:T(8,128)(2,1)S(1)} %pad_maximum_fusion.5), channel_id=1, source_target_pairs={{0,8},{1,9},{2,10},{3,11},{4,12},{5,13},{6,14},{7,15},{8,0},{9,1},... | collective-permute-start | bytes 393224 | tf_op jit(solution)/shard_map/ppermute | solution.py:64
  72.1 20.7 %collective-permute-start.20 = (f32[256,512]{1,0:T(8,128)S(1)}, f32[256,512]{1,0:T(8,128)S(1)}, u32[]{:S(2)}, u32[]{:S(2)}) collective-permute-start(f32[256,512]{1,0:T(8,128)S(1)} %get-tuple-element.58), channel_id=1, source_target_pairs={{0,2},{1,3},{2,0},{3,1},{4,6},{5,7},{6,4},{7,5},{8,10},{9,11},{10,... | collective-permute-start | bytes 1572872 | tf_op jit(solution)/shard_map/ppermute | solution.py:64
  72.3 10.0 %collective-permute-start.15 = (bf16[128,512]{1,0:T(8,128)(2,1)S(1)}, bf16[128,512]{1,0:T(8,128)(2,1)S(1)}, u32[]{:S(2)}, u32[]{:S(2)}) collective-permute-start(bf16[128,512]{1,0:T(8,128)(2,1)S(1)} %pad_maximum_fusion.6), channel_id=1, source_target_pairs={{0,16},{1,17},{2,18},{3,19},{4,20},{5,21},{6,22},{7,23},{8,24},{9,... | collective-permute-start | bytes 393224 | tf_op jit(solution)/shard_map/ppermute | solution.py:64
  82.0 10.8 %collective-permute-start.21 = (f32[256,512]{1,0:T(8,128)S(1)}, f32[256,512]{1,0:T(8,128)S(1)}, u32[]{:S(2)}, u32[]{:S(2)}) collective-permute-start(f32[256,512]{1,0:T(8,128)S(1)} %get-tuple-element.59), channel_id=1, source_target_pairs={{0,2},{1,3},{2,0},{3,1},{4,6},{5,7},{6,4},{7,5},{8,10},{9,11},{10,... | collective-permute-start | bytes 1572872 | tf_op jit(solution)/shard_map/ppermute | solution.py:64
  82.5 9.3 %collective-permute-start.18 = (bf16[128,512]{1,0:T(8,128)(2,1)S(1)}, bf16[128,512]{1,0:T(8,128)(2,1)S(1)}, u32[]{:S(2)}, u32[]{:S(2)}) collective-permute-start(bf16[128,512]{1,0:T(8,128)(2,1)S(1)} %pad_maximum_fusion.7), channel_id=1, source_target_pairs={{0,5},{1,4},{2,7},{3,6},{4,1},{5,0},{6,3},{7,2},{8,13},{9,12},{10,... | collective-permute-start | bytes 393224 | tf_op jit(solution)/shard_map/ppermute | solution.py:64
  83.0 8.9 %collective-permute-start.17 = (bf16[128,512]{1,0:T(8,128)(2,1)S(1)}, bf16[128,512]{1,0:T(8,128)(2,1)S(1)}, u32[]{:S(2)}, u32[]{:S(2)}) collective-permute-start(bf16[128,512]{1,0:T(8,128)(2,1)S(1)} %pad_maximum_fusion.7), channel_id=1, source_target_pairs={{0,4},{1,5},{2,6},{3,7},{4,0},{5,1},{6,2},{7,3},{8,12},{9,13},{10,... | collective-permute-start | bytes 393224 | tf_op jit(solution)/shard_map/ppermute | solution.py:64
  84.5 7.4 %collective-permute-start.16 = (bf16[128,512]{1,0:T(8,128)(2,1)S(1)}, bf16[128,512]{1,0:T(8,128)(2,1)S(1)}, u32[]{:S(2)}, u32[]{:S(2)}) collective-permute-start(bf16[128,512]{1,0:T(8,128)(2,1)S(1)} %pad_maximum_fusion.7), channel_id=1, source_target_pairs={{0,1},{1,0},{2,3},{3,2},{4,5},{5,4},{6,7},{7,6},{8,9},{9,8},{10,11... | collective-permute-start | bytes 393224 | tf_op jit(solution)/shard_map/ppermute | solution.py:64
  91.8 2.0 %collective-permute-start.22 = (f32[256,512]{1,0:T(8,128)S(1)}, f32[256,512]{1,0:T(8,128)S(1)}, u32[]{:S(2)}, u32[]{:S(2)}) collective-permute-start(f32[256,512]{1,0:T(8,128)S(1)} %get-tuple-element.60), channel_id=1, source_target_pairs={{0,2},{1,3},{2,0},{3,1},{4,6},{5,7},{6,4},{7,5},{8,10},{9,11},{10,... | collective-permute-start | bytes 1572872 | tf_op jit(solution)/shard_map/ppermute | solution.py:64
  92.1 2.4 %collective-permute-start.19 = (bf16[2,2,128,512]{3,2,1,0:T(8,128)(2,1)S(1)}, bf16[2,2,128,512]{3,2,1,0:T(8,128)(2,1)S(1)}, u32[]{:S(2)}, u32[]{:S(2)}) collective-permute-start(bf16[2,2,128,512]{3,2,1,0:T(8,128)(2,1)S(1)} %bitcast.88), channel_id=1, source_target_pairs={{0,2},{1,3},{2,0},{3,1},{4,6},{5,7},{6,4},{7,5},{8,10},{9,11},{10,... | collective-permute-start | bytes 1572872 | tf_op jit(solution)/shard_map/ppermute | solution.py:64
  92.7 2.6 %collective-permute-start.23 = (f32[256,512]{1,0:T(8,128)S(1)}, f32[256,512]{1,0:T(8,128)S(1)}, u32[]{:S(2)}, u32[]{:S(2)}) collective-permute-start(f32[256,512]{1,0:T(8,128)S(1)} %factor.7), channel_id=1, source_target_pairs={{0,2},{1,3},{2,0},{3,1},{4,6},{5,7},{6,4},{7,5},{8,10},{9,11},{10,... | collective-permute-start | bytes 1572872 | tf_op jit(solution)/shard_map/ppermute | solution.py:64
  94.6 0.8 copy-start.3
where the time goes:
time: 103 us
  Pallas kernels  46.4 us (45%)
  starting transfers between devices  27.2 us (26%)
  waiting for transfers between devices  21.9 us (21%)
  other arithmetic  5.55 us (5%)
  between operations  1.39 us (1%)
    ppermute x24, starting transfers between devices, swap(): lax.ppermute(value, axes, [(i, i ^ flip_of(i)) for i in range(lax.axis_si...  27.2 us
    pallas_call x4, Pallas kernels, factor_step(): pl.pallas_call(functools.partial(factor_kernel, index, copied is not None...  24.9 us
    ppermute x24, waiting for transfers between devices, swap(): lax.ppermute(value, axes, [(i, i ^ flip_of(i)) for i in range(lax.axis_si...  21.9 us
    pallas_call x1, Pallas kernels, slabs(): pl.pallas_call(functools.partial(slab_kernel, scale, chunk), out_shape=(p...  10.7 us
    pallas_call x1, Pallas kernels, finish(): pl.pallas_call(functools.partial(final_kernel, step_size, chunk), in_spec...  7.61 us
    reduce_sum x1, other arithmetic, local(): norms = (jnp.sum(wide * wide, axis=1) * scale).reshape(1, rows_dev)  3.23 us
    pallas_call x1, Pallas kernels, pick_halves(): pl.pallas_call(pick_kernel, grid_spec=pltpu.PrefetchScalarGridSpec(num_sc...  2.18 us
  transfers between devices with their start and end apart: 24, of which 13 were waited for; matrix products, arithmetic and copies ran while one was open for 4% of the time, Pallas kernels for 25%

commit v1 on v0

--- a/solution.py
+++ b/solution.py
@@ -277,12 +277,7 @@
     )(block, in_vmem(features), norms, in_vmem(residual), in_vmem(coefficients))
 
 
-def reciprocal(x):
-    guess = pl.reciprocal(x, approx=True)
-    return guess * (2.0 - x * guess)
-
-
-def eliminate(tiles, t, lane, scaled_ref):
+def eliminate(tiles, t, lane, scaled_ref, waiting):
     start, shape = 8 * t, tiles[t].shape
     wide = lambda tile, k: jnp.broadcast_to(tile[:, start + k : start + k + 1], shape)
     rows = [jnp.broadcast_to(tiles[t][k : k + 1], shape) for k in range(8)]
@@ -290,85 +285,106 @@
     units = [jnp.where(lane == start + k, 1.0, 0.0) for k in range(8)]
     rows = [row + unit for row, unit in zip(rows, units)]
     total, lower = [None] * 8, {}
+    waiting, share = list(waiting), -(-len(waiting) // 4)
     for r in range(0, 8, 2):
         p, m, q = at[r, r], at[r, r + 1], at[r + 1, r + 1]
-        inverse = reciprocal(p * q - m * m)
-        p, m, q = p * inverse, m * inverse, q * inverse
+        det = p * q - m * m
+        guess = pl.reciprocal(det, approx=True)
+        for _ in range(min(share, len(waiting))):
+            waiting.pop(0)()
+        refine = 2.0 - det * guess
+        inverse = guess * refine
         for k in range(r + 2, 8):
             first = q * at[r, k] - m * at[r + 1, k]
             second = p * at[r + 1, k] - m * at[r, k]
-            lower[r, k], lower[r + 1, k] = first, second
+            lower[r, k], lower[r + 1, k] = first * inverse, second * inverse
             for i in range(r + 2, k + 1):
-                at[i, k] = at[i, k] - (at[r, i] * first + at[r + 1, i] * second)
-            rows[k] = rows[k] - (first * rows[r] + second * rows[r + 1])
-        total[r] = q * rows[r] - m * rows[r + 1]
-        total[r + 1] = p * rows[r + 1] - m * rows[r]
+                product = at[r, i] * first + at[r + 1, i] * second
+                change = product * guess * refine if k < r + 4 else product * inverse
+                at[i, k] = at[i, k] - change
+            rows[k] = rows[k] - (first * rows[r] + second * rows[r + 1]) * inverse
+        total[r] = (q * rows[r] - m * rows[r + 1]) * inverse
+        total[r + 1] = (p * rows[r + 1] - m * rows[r]) * inverse
     for r in (4, 2, 0):
-        for k in range(r + 2, 8):
+        for k in range(7, r + 1, -1):
             total[r] = total[r] - lower[r, k] * total[k]
             total[r + 1] = total[r + 1] - lower[r + 1, k] * total[k]
     for k in range(8):
         scaled_ref[start + k : start + k + 1] = total[k][:1] - units[k][:1]
-    for u in range(t + 1, len(tiles)):
+
+    def update(u):
         parts = [wide(tiles[u], k) * total[k] for k in range(8)]
         while len(parts) > 1:
             parts = [x + y for x, y in zip(parts[::2], parts[1::2])]
         tiles[u] = tiles[u] - parts[0]
 
-
-def factor_kernel(index, copies, *refs):
+    if t + 1 < len(tiles):
+        update(t + 1)
+    return [functools.partial(update, u) for u in range(t + 2, len(tiles))]
+
+
+def factor_kernel(index, copied, *refs):
     refs = list(refs)
     rest_ref, _ = refs.pop(0), refs.pop(0)
-    if copies:
-        source, scaled, sem = refs.pop(0), *refs[-2:]
-        copy = pltpu.make_async_copy(source, refs[-3], sem)
+    before_ref = refs.pop(0) if index else None
+    scaled = refs.pop()
+    if copied:
+        sem = refs.pop()
+        copy = pltpu.make_async_copy(refs.pop(0), refs.pop(), sem)
         copy.start()
-    else:
-        scaled = refs[-1]
-    last = rest_ref.shape[0] == TILE
-    factor_ref = refs[0] if last else refs[1]
+    factor_ref = refs[0]
     here = slice(index * TILE, (index + 1) * TILE)
+    dot = functools.partial(lax.dot_general, precision=HIGH, preferred_element_type=jnp.float32)
+    plain = (((1,), (0,)), ((), ()))
+
+    def updated(rows):
+        if not index:
+            return rest_ref[rows]
+        then = slice((index - 1) * TILE, index * TILE)
+        old = rest_ref[rows]
+        inside = lax.broadcasted_iota(jnp.int32, old.shape, 1) // TILE == index - 1
+        return jnp.where(inside, 0.0, old) - dot(rest_ref[rows, then], before_ref[TILE:], plain)
+
+    first = TILE if index == 1 else 0
+    factor_ref[:TILE] = updated(slice(first, first + TILE))
     row_ids = lax.broadcasted_iota(jnp.int32, (TILE, TILE), 0)
     col_ids = lax.broadcasted_iota(jnp.int32, (TILE, TILE), 1)
     lane = lax.broadcasted_iota(jnp.int32, (8, TILE), 1)
-    tiles = [rest_ref[8 * t : 8 * t + 8, here] for t in range(TILE // 8)]
+    tiles = [factor_ref[8 * t : 8 * t + 8, here] for t in range(TILE // 8)]
+    if len(refs) > 1:
+        refs[1][...] = updated(slice(first + TILE, rest_ref.shape[0]))
+    waiting = []
     for t in range(TILE // 8):
-        eliminate(tiles, t, lane, scaled)
+        waiting = eliminate(tiles, t, lane, scaled, waiting)
     start = row_ids - row_ids % 8
-    dot = functools.partial(lax.dot_general, precision=HIGH, preferred_element_type=jnp.float32)
     lower = jnp.where(col_ids < start, jnp.concatenate(tiles, axis=0), 0.0)
     lower = lower + jnp.where(col_ids == row_ids, 1.0, 0.0)
     right = jnp.where(col_ids < start + 8, scaled[...], 0.0)
     inv = dot(lower, right, (((0,), (0,)), ((), ())))
-    top = rest_ref[:TILE]
-    panel = dot(inv, top, (((1,), (0,)), ((), ())))
+    panel = dot(inv, factor_ref[:TILE], plain)
     inside = lax.broadcasted_iota(jnp.int32, panel.shape, 1) // TILE == index
-    panel = jnp.where(inside, jnp.concatenate([inv] * (BLOCK // TILE), axis=1), panel)
-    factor_ref[:TILE] = top
-    factor_ref[TILE:] = panel
-    if not last:
-        under = rest_ref[TILE:]
-        change = dot(rest_ref[TILE:, here], panel, (((1,), (0,)), ((), ())))
-        inside = lax.broadcasted_iota(jnp.int32, under.shape, 1) // TILE == index
-        refs[0][...] = jnp.where(inside, 0.0, under) - change
-    if copies:
+    factor_ref[TILE:] = jnp.where(inside, jnp.concatenate([inv] * (BLOCK // TILE), axis=1), panel)
+    if copied:
         copy.wait()
 
 
-def factor_step(rest, index, slab, copied=None):
-    left = rest.shape[0] - TILE
+def factor_step(rest, index, slab, before=None, copied=None):
+    left = BLOCK - (index + 1) * TILE
     vmem, hbm = pl.BlockSpec(memory_space=pltpu.VMEM), pl.BlockSpec(memory_space=pltpu.HBM)
-    out = [jax.ShapeDtypeStruct((left, BLOCK), jnp.float32)] if left else []
-    out.append(jax.ShapeDtypeStruct((2 * TILE, BLOCK), jnp.float32))
-    inputs, in_specs, out_specs = [rest, in_vmem(slab)], [vmem] * 2, [vmem] * len(out)
-    scratch = [pltpu.VMEM((TILE, TILE), jnp.float32)]
+    out = [jax.ShapeDtypeStruct((2 * TILE, BLOCK), jnp.float32)]
+    inputs, scratch = [rest, in_vmem(slab)], [pltpu.VMEM((TILE, TILE), jnp.float32)]
+    if index:
+        inputs.append(before)
+        if left:
+            out.append(jax.ShapeDtypeStruct((left, BLOCK), jnp.float32))
+    in_specs, out_specs = [vmem] * len(inputs), [vmem] * len(out)
     if copied is not None:
         inputs.append(in_vmem(copied))
         in_specs.append(vmem)
         out.append(pltpu.HBM(copied.shape, copied.dtype))
         out_specs.append(hbm)
-        scratch.append(pltpu.SemaphoreType.DMA)
-    out = pl.pallas_call(
+        scratch.insert(0, pltpu.SemaphoreType.DMA)
+    return pl.pallas_call(
         functools.partial(factor_kernel, index, copied is not None),
         in_specs=in_specs,
         out_specs=tuple(out_specs),
@@ -378,22 +394,21 @@
         cost_estimate=pl.CostEstimate(flops=6 * 10**9, bytes_accessed=4 * 1024 * 1024, transcendentals=0),
         name="factor",
     )(*inputs)
-    out = list(out)
-    below = out.pop(0) if left else None
-    return (below,) + tuple(out)
 
 
 def apply_inverse(value, refs):
-    ids = lambda axis: lax.broadcasted_iota(jnp.int32, (TILE, BLOCK), axis)
-    lower, right = [], []
-    for k in range(BLOCK // TILE):
-        rest, panel = refs[k][:TILE], refs[k][TILE:]
-        unit = jnp.where(ids(1) == ids(0) + k * TILE, 1.0, 0.0)
-        lower.append(jnp.where(ids(1) < k * TILE, rest, unit))
-        right.append(jnp.where(ids(1) < (k + 1) * TILE, panel, 0.0))
-    lower, right = jnp.concatenate(lower, axis=0), jnp.concatenate(right, axis=0)
-    middle = lax.dot_general(value, right, NT, precision=HIGH, preferred_element_type=jnp.float32)
-    return jnp.dot(middle, lower, precision=HIGH, preferred_element_type=jnp.float32)
+    upto = lambda k: slice(0, k * TILE)
+    dot = functools.partial(lax.dot_general, precision=HIGH, preferred_element_type=jnp.float32)
+    count = BLOCK // TILE
+    middle = [dot(value[:, upto(k + 1)], refs[k][TILE:, upto(k + 1)], NT) for k in range(count)]
+    added = {k: dot(middle[k], refs[k][:TILE, upto(k)], (((1,), (0,)), ((), ()))) for k in range(1, count)}
+    out = []
+    for j in range(count):
+        total = middle[j]
+        for k in range(j + 1, count):
+            total = total + added[k][:, j * TILE : (j + 1) * TILE]
+        out.append(total)
+    return jnp.concatenate(out, axis=1)
 
 
 def final_kernel(step_size, chunk, owner_ref, tiles_ref, me_ref, packed_ref, gram_ref, slab_ref, res_ref, coef_ref, base_ref, *refs):
@@ -537,25 +552,29 @@
         pieces = lax.psum(pieces, "sub")
     core, on_core = bit_of(me, sub_count), (me & sub_count) != 0
     rest, gram12 = gram(block, core.reshape(1), scale, slab)
-    factors, base = ([], []), None
+    factors, before, copied = ([], []), None, []
 
     def beside(hop, index, rest):
+        nonlocal before
         then, got = hop
-        below, mine, *copied = factor_step(rest, index, slab, coefficients if index == 0 else None)
-        got, below, mine = lax.optimization_barrier((got, below, mine))
+        mine, *given = factor_step(rest, index, slab, before, None if index else coefficients)
+        if not index:
+            copied.append(given.pop())
+        got, mine, given = lax.optimization_barrier((got, mine, given))
+        before = mine
         other = swap(mine, AXES, sub_count)
         factors[0].append(jnp.where(on_core, other, mine))
         factors[1].append(jnp.where(on_core, mine, other))
-        return then(got), below, copied
+        return then(got), given[0] if given else rest
 
     value = spread.core_sum(pieces)
-    value, rest, (base,) = beside(spread.near_sum(value, STEPS * own), 0, rest)
+    value, rest = beside(spread.near_sum(value, STEPS * own), 0, rest)
     for index, mask in enumerate(spread.far):
-        value, rest, _ = beside(spread.far_sum(value, STEPS * own, mask), 1 + index, rest)
-    packed, rest, _ = beside(spread.near_gather(pack(value, STEPS * own)), 3, rest)
+        value, rest = beside(spread.far_sum(value, STEPS * own, mask), 1 + index, rest)
+    packed, rest = beside(spread.near_gather(pack(value, STEPS * own)), 3, rest)
     packed = spread.core_gather(packed)
     return finish(
-        block_owner, block_tiles, me.reshape(1), packed, gram12, slab, residual, coefficients, base,
+        block_owner, block_tiles, me.reshape(1), packed, gram12, slab, residual, coefficients, copied[0],
         factors[0] + factors[1], step_size,
     )
 

time: 103 us -> 101 us (0.981)
  Pallas kernels: 46.4 us -> 43.7 us
    pallas_call x4, Pallas kernels: 24.9 us -> 22.3 us  [factor_step(): pl.pallas_call(functools.partial(factor_kernel, index, copied is not None...]
  transfers between devices with their start and end apart: 24 -> 24, of which waited for: 13 -> 14; matrix products, arithmetic and copies ran while one was open for 4% -> 4% of each run, Pallas kernels for 25% -> 23%
where the time goes in v1:
time: 101 us
  Pallas kernels  43.7 us (43%)
  starting transfers between devices  27.2 us (27%)
  waiting for transfers between devices  22.4 us (22%)
  other arithmetic  5.55 us (5%)
  between operations  1.39 us (1%)
    ppermute x24, starting transfers between devices, swap(): lax.ppermute(value, axes, [(i, i ^ flip_of(i)) for i in range(lax.axis_si...  27.2 us
    ppermute x24, waiting for transfers between devices, swap(): lax.ppermute(value, axes, [(i, i ^ flip_of(i)) for i in range(lax.axis_si...  22.4 us
    pallas_call x4, Pallas kernels, factor_step(): pl.pallas_call(functools.partial(factor_kernel, index, copied is not None...  22.3 us
    pallas_call x1, Pallas kernels, slabs(): pl.pallas_call(functools.partial(slab_kernel, scale, chunk), out_shape=(p...  10.7 us
    pallas_call x1, Pallas kernels, finish(): pl.pallas_call(functools.partial(final_kernel, step_size, chunk), in_spec...  7.52 us
    reduce_sum x1, other arithmetic, local(): norms = (jnp.sum(wide * wide, axis=1) * scale).reshape(1, rows_dev)  3.23 us
    pallas_call x1, Pallas kernels, pick_halves(): pl.pallas_call(pick_kernel, grid_spec=pltpu.PrefetchScalarGridSpec(num_sc...  2.18 us
  transfers between devices with their start and end apart: 24, of which 14 were waited for; matrix products, arithmetic and copies ran while one was open for 4% of the time, Pallas kernels for 23%

profile of v1, /device:TPU:0, one launch (start us, length us, event | category | flops | bytes accessed | tf_op | source)
XLA Modules:
  0.0 100.9 jit_solution(16841617307174385354)
XLA Ops:
  0.6 2.2 %pick.1 = (bf16[2,256,512]{2,1,0:T(8,128)(2,1)S(1)}, bf16[2,256,512]{2,1,0:T(8,128)(2,1)S(1)}) custom-call(s32[2,4]{1,0:T(2,128)} %tiles_ref.3, s32[1]{0:T(128)} %bitcast.1.core_ref, bf16[4096,512]{1,0:T(8,128)(2,1)} %feat_ref.3), custom_call_target="tpu_custom_call" | custom-call | tf_op jit(solution)/shard_map/pick/pallas_call | solution.py:47
  3.4 1.5 %collective-permute-done = bf16[2,256,512]{2,1,0:T(8,128)(2,1)S(1)} collective-permute-done((bf16[2,256,512]{2,1,0:T(8,128)(2,1)S(1)}, bf16[2,256,512]{2,1,0:T(8,128)(2,1)S(1)}, u32[]{:S(2)}, u32[]{:S(2)}) %collective-permute-start) | collective-permute-done | bytes 524320 | tf_op jit(solution)/shard_map/ppermute | solution.py:64
  5.1 3.0 %collective-permute-start.2 = (bf16[2,64,512]{2,1,0:T(8,128)(2,1)S(1)}, bf16[2,64,512]{2,1,0:T(8,128)(2,1)S(1)}, u32[]{:S(2)}, u32[]{:S(2)}) collective-permute-start(bf16[2,64,512]{2,1,0:T(8,128)(2,1)S(1)} %get-tuple-element.85), channel_id=1, source_target_pairs={{0,4},{1,5},{2,6},{3,7},{4,0},{5,1},{6,2},{7,3},{8,12},{9,13},{10,... | collective-permute-start | bytes 393224 | tf_op jit(solution)/shard_map/ppermute | solution.py:64
  8.0 1.5 %collective-permute-start.3 = (bf16[2,64,512]{2,1,0:T(8,128)(2,1)S(1)}, bf16[2,64,512]{2,1,0:T(8,128)(2,1)S(1)}, u32[]{:S(2)}, u32[]{:S(2)}) collective-permute-start(bf16[2,64,512]{2,1,0:T(8,128)(2,1)S(1)} %get-tuple-element.86), channel_id=1, source_target_pairs={{0,1},{1,0},{2,3},{3,2},{4,5},{5,4},{6,7},{7,6},{8,9},{9,8},{10,11... | collective-permute-start | bytes 393224 | tf_op jit(solution)/shard_map/ppermute | solution.py:64
  9.6 3.2 %multiply_reduce_fusion = f32[4096]{0:T(1024)S(1)} fusion(bf16[4096,512]{1,0:T(8,128)(2,1)} %feat_ref.3), kind=kLoop, calls=%fused_computation | loop fusion | flops 6287360 | bytes 4210688 | tf_op jit(solution)/shard_map/reduce_sum | solution.py:548
  12.8 1.6 %collective-permute-done.3 = bf16[2,64,512]{2,1,0:T(8,128)(2,1)S(1)} collective-permute-done((bf16[2,64,512]{2,1,0:T(8,128)(2,1)S(1)}, bf16[2,64,512]{2,1,0:T(8,128)(2,1)S(1)}, u32[]{:S(2)}, u32[]{:S(2)}) %collective-permute-start.3) | collective-permute-done | bytes 131104 | tf_op jit(solution)/shard_map/ppermute | solution.py:64
  14.4 1.5 %collective-permute-done.1 = bf16[2,64,512]{2,1,0:T(8,128)(2,1)S(1)} collective-permute-done((bf16[2,64,512]{2,1,0:T(8,128)(2,1)S(1)}, bf16[2,64,512]{2,1,0:T(8,128)(2,1)S(1)}, u32[]{:S(2)}, u32[]{:S(2)}) %collective-permute-start.1) | collective-permute-done | bytes 131104 | tf_op jit(solution)/shard_map/ppermute | solution.py:64
  16.0 1.8 %collective-permute-start.4 = (bf16[2,64,512]{2,1,0:T(8,128)(2,1)S(1)}, bf16[2,64,512]{2,1,0:T(8,128)(2,1)S(1)}, u32[]{:S(2)}, u32[]{:S(2)}) collective-permute-start(bf16[2,64,512]{2,1,0:T(8,128)(2,1)S(1)} %fusion.5), channel_id=1, source_target_pairs={{0,8},{1,9},{2,18},{3,19},{4,12},{5,13},{6,22},{7,23},{8,0},{9,1},... | collective-permute-start | bytes 393224 | tf_op jit(solution)/shard_map/ppermute | solution.py:64
  17.8 3.7 %collective-permute-done.4 = bf16[2,64,512]{2,1,0:T(8,128)(2,1)S(1)} collective-permute-done((bf16[2,64,512]{2,1,0:T(8,128)(2,1)S(1)}, bf16[2,64,512]{2,1,0:T(8,128)(2,1)S(1)}, u32[]{:S(2)}, u32[]{:S(2)}) %collective-permute-start.4) | collective-permute-done | bytes 131104 | tf_op jit(solution)/shard_map/ppermute | solution.py:64
  21.6 2.7 %collective-permute-start.5 = (bf16[2,64,512]{2,1,0:T(8,128)(2,1)S(1)}, bf16[2,64,512]{2,1,0:T(8,128)(2,1)S(1)}, u32[]{:S(2)}, u32[]{:S(2)}) collective-permute-start(bf16[2,64,512]{2,1,0:T(8,128)(2,1)S(1)} %broadcast_select_fusion.9), channel_id=1, source_target_pairs={{0,16},{1,17},{2,10},{3,11},{4,20},{5,21},{6,14},{7,15},{8,24},{9,... | collective-permute-start | bytes 393224 | tf_op jit(solution)/shard_map/ppermute | solution.py:64
  24.3 3.3 %collective-permute-done.5 = bf16[2,64,512]{2,1,0:T(8,128)(2,1)S(1)} collective-permute-done((bf16[2,64,512]{2,1,0:T(8,128)(2,1)S(1)}, bf16[2,64,512]{2,1,0:T(8,128)(2,1)S(1)}, u32[]{:S(2)}, u32[]{:S(2)}) %collective-permute-start.5) | collective-permute-done | bytes 131104 | tf_op jit(solution)/shard_map/ppermute | solution.py:64
  27.6 1.3 %collective-permute-start.8 = (bf16[2,64,512]{2,1,0:T(8,128)(2,1)S(1)}, bf16[2,64,512]{2,1,0:T(8,128)(2,1)S(1)}, u32[]{:S(2)}, u32[]{:S(2)}) collective-permute-start(bf16[2,64,512]{2,1,0:T(8,128)(2,1)S(1)} %broadcast_select_fusion.10), channel_id=1, source_target_pairs={{0,1},{1,0},{2,3},{3,2},{4,5},{5,4},{6,7},{7,6},{8,9},{9,8},{10,11... | collective-permute-start | bytes 393224 | tf_op jit(solution)/shard_map/ppermute | solution.py:64
  28.9 1.5 %collective-permute-start.7 = (bf16[2,64,512]{2,1,0:T(8,128)(2,1)S(1)}, bf16[2,64,512]{2,1,0:T(8,128)(2,1)S(1)}, u32[]{:S(2)}, u32[]{:S(2)}) collective-permute-start(bf16[2,64,512]{2,1,0:T(8,128)(2,1)S(1)} %broadcast_select_fusion.10), channel_id=1, source_target_pairs={{0,4},{1,5},{2,6},{3,7},{4,0},{5,1},{6,2},{7,3},{8,12},{9,13},{10,... | collective-permute-start | bytes 393224 | tf_op jit(solution)/shard_map/ppermute | solution.py:64
  31.2 2.1 %collective-permute-done.8 = bf16[2,64,512]{2,1,0:T(8,128)(2,1)S(1)} collective-permute-done((bf16[2,64,512]{2,1,0:T(8,128)(2,1)S(1)}, bf16[2,64,512]{2,1,0:T(8,128)(2,1)S(1)}, u32[]{:S(2)}, u32[]{:S(2)}) %collective-permute-start.8) | collective-permute-done | bytes 131104 | tf_op jit(solution)/shard_map/ppermute | solution.py:64
  33.2 1.3 %collective-permute-done.7 = bf16[2,64,512]{2,1,0:T(8,128)(2,1)S(1)} collective-permute-done((bf16[2,64,512]{2,1,0:T(8,128)(2,1)S(1)}, bf16[2,64,512]{2,1,0:T(8,128)(2,1)S(1)}, u32[]{:S(2)}, u32[]{:S(2)}) %collective-permute-start.7) | collective-permute-done | bytes 131104 | tf_op jit(solution)/shard_map/ppermute | solution.py:64
  34.5 1.8 %collective-permute-done.6 = bf16[2,64,512]{2,1,0:T(8,128)(2,1)S(1)} collective-permute-done((bf16[2,64,512]{2,1,0:T(8,128)(2,1)S(1)}, bf16[2,64,512]{2,1,0:T(8,128)(2,1)S(1)}, u32[]{:S(2)}, u32[]{:S(2)}) %collective-permute-start.6) | collective-permute-done | bytes 131104 | tf_op jit(solution)/shard_map/ppermute | solution.py:64
  36.5 1.9 %collective-permute-done.9 = bf16[2,4,64,512]{3,2,1,0:T(8,128)(2,1)S(1)} collective-permute-done((bf16[2,4,64,512]{3,2,1,0:T(8,128)(2,1)S(1)}, bf16[2,4,64,512]{3,2,1,0:T(8,128)(2,1)S(1)}, u32[]{:S(2)}, u32[]{:S(2)}) %collective-permute-start.9) | collective-permute-done | bytes 524320 | tf_op jit(solution)/shard_map/ppermute | solution.py:64
  39.1 10.7 %slabs.1 = (bf16[1024,4096]{1,0:T(8,128)(2,1)S(1)}, f32[8,96,512]{2,1,0:T(8,128)S(1)}) custom-call(bf16[1024,512]{1,0:T(8,128)(2,1)S(1)} %bitcast.81, bf16[4096,512]{1,0:T(8,128)(2,1)S(1)} %copy-done, f32[1,4096]{1,0:T(1,128)S(1)} %bitcast.84, f32[4096,128]{1,0:T(8,128)S(1)} %copy-done.1, f32[4096,128]{1,0:T(8,128)S(1)} %copy-done.2), custom_call_target="tpu_custom_call" | custom-call | flops 7516192768 | bytes 16777216 | tf_op jit(solution)/shard_map/slabs/pallas_call | solution.py:261
  50.1 1.0 gram.1
  51.1 1.3 %collective-permute-done.10 = f32[2,2,96,512]{3,2,1,0:T(8,128)S(1)} collective-permute-done((f32[2,2,96,512]{3,2,1,0:T(8,128)S(1)}, f32[2,2,96,512]{3,2,1,0:T(8,128)S(1)}, u32[]{:S(2)}, u32[]{:S(2)}) %collective-permute-start.10) | collective-permute-done | bytes 786464 | tf_op jit(solution)/shard_map/ppermute | solution.py:64
  52.8 0.8 collective-permute-start.13
  53.6 1.2 %collective-permute-start.12 = (bf16[128,512]{1,0:T(8,128)(2,1)S(1)}, bf16[128,512]{1,0:T(8,128)(2,1)S(1)}, u32[]{:S(2)}, u32[]{:S(2)}) collective-permute-start(bf16[128,512]{1,0:T(8,128)(2,1)S(1)} %get-tuple-element.79), channel_id=1, source_target_pairs={{0,4},{1,5},{2,6},{3,7},{4,0},{5,1},{6,2},{7,3},{8,12},{9,13},{10,... | collective-permute-start | bytes 393224 | tf_op jit(solution)/shard_map/ppermute | solution.py:64
  54.8 1.5 %collective-permute-start.11 = (bf16[128,512]{1,0:T(8,128)(2,1)S(1)}, bf16[128,512]{1,0:T(8,128)(2,1)S(1)}, u32[]{:S(2)}, u32[]{:S(2)}) collective-permute-start(bf16[128,512]{1,0:T(8,128)(2,1)S(1)} %get-tuple-element.80), channel_id=1, source_target_pairs={{0,1},{1,0},{2,3},{3,2},{4,5},{5,4},{6,7},{7,6},{8,9},{9,8},{10,11... | collective-permute-start | bytes 393224 | tf_op jit(solution)/shard_map/ppermute | solution.py:64
  56.3 5.8 %factor.4 = (f32[256,512]{1,0:T(8,128)S(1)}, f32[4096,128]{1,0:T(8,128)}) custom-call(f32[512,512]{1,0:T(8,128)S(1)} %get-tuple-element.36.refs_0_, bf16[1024,4096]{1,0:T(8,128)(2,1)S(1)} %get-tuple-element.35.slab_ref.refs_1_, f32[4096,128]{1,0:T(8,128)S(1)} %copy-done.2), custom_call_target="tpu_custom_call" | custom-call | flops 6000000000 | bytes 4194304 | tf_op jit(solution)/shard_map/factor/pallas_call | solution.py:387
  62.5 2.5 %collective-permute-start.14 = (bf16[128,512]{1,0:T(8,128)(2,1)S(1)}, bf16[128,512]{1,0:T(8,128)(2,1)S(1)}, u32[]{:S(2)}, u32[]{:S(2)}) collective-permute-start(bf16[128,512]{1,0:T(8,128)(2,1)S(1)} %pad_maximum_fusion.5), channel_id=1, source_target_pairs={{0,8},{1,9},{2,10},{3,11},{4,12},{5,13},{6,14},{7,15},{8,0},{9,1},... | collective-permute-start | bytes 393224 | tf_op jit(solution)/shard_map/ppermute | solution.py:64
  65.0 5.4 %factor.5 = (f32[256,512]{1,0:T(8,128)S(1)}, f32[256,512]{1,0:T(8,128)S(1)}) custom-call(f32[512,512]{1,0:T(8,128)S(1)} %get-tuple-element.36.refs_0_, bf16[1024,4096]{1,0:T(8,128)(2,1)S(1)} %get-tuple-element.35.slab_ref.refs_1_, f32[256,512]{1,0:T(8,128)S(1)} %get-tuple-element.41.refs_2_), custom_call_target="tpu_custom_call" | custom-call | flops 6000000000 | bytes 4194304 | tf_op jit(solution)/shard_map/factor/pallas_call | solution.py:387
  70.7 3.4 %collective-permute-start.15 = (bf16[128,512]{1,0:T(8,128)(2,1)S(1)}, bf16[128,512]{1,0:T(8,128)(2,1)S(1)}, u32[]{:S(2)}, u32[]{:S(2)}) collective-permute-start(bf16[128,512]{1,0:T(8,128)(2,1)S(1)} %pad_maximum_fusion.6), channel_id=1, source_target_pairs={{0,16},{1,17},{2,18},{3,19},{4,20},{5,21},{6,22},{7,23},{8,24},{9,... | collective-permute-start | bytes 393224 | tf_op jit(solution)/shard_map/ppermute | solution.py:64
  74.3 5.7 %factor.6 = (f32[256,512]{1,0:T(8,128)S(1)}, f32[128,512]{1,0:T(8,128)S(1)}) custom-call(f32[256,512]{1,0:T(8,128)S(1)} %get-tuple-element.45.refs_0_, bf16[1024,4096]{1,0:T(8,128)(2,1)S(1)} %get-tuple-element.35.slab_ref.refs_1_, f32[256,512]{1,0:T(8,128)S(1)} %get-tuple-element.46.refs_2_), custom_call_target="tpu_custom_call" | custom-call | flops 6000000000 | bytes 4194304 | tf_op jit(solution)/shard_map/factor/pallas_call | solution.py:387
  81.2 1.5 %collective-permute-start.17 = (bf16[128,512]{1,0:T(8,128)(2,1)S(1)}, bf16[128,512]{1,0:T(8,128)(2,1)S(1)}, u32[]{:S(2)}, u32[]{:S(2)}) collective-permute-start(bf16[128,512]{1,0:T(8,128)(2,1)S(1)} %pad_maximum_fusion.7), channel_id=1, source_target_pairs={{0,4},{1,5},{2,6},{3,7},{4,0},{5,1},{6,2},{7,3},{8,12},{9,13},{10,... | collective-permute-start | bytes 393224 | tf_op jit(solution)/shard_map/ppermute | solution.py:64
  82.7 1.5 %collective-permute-start.16 = (bf16[128,512]{1,0:T(8,128)(2,1)S(1)}, bf16[128,512]{1,0:T(8,128)(2,1)S(1)}, u32[]{:S(2)}, u32[]{:S(2)}) collective-permute-start(bf16[128,512]{1,0:T(8,128)(2,1)S(1)} %pad_maximum_fusion.7), channel_id=1, source_target_pairs={{0,1},{1,0},{2,3},{3,2},{4,5},{5,4},{6,7},{7,6},{8,9},{9,8},{10,11... | collective-permute-start | bytes 393224 | tf_op jit(solution)/shard_map/ppermute | solution.py:64
  84.2 5.4 %factor.7 = f32[256,512]{1,0:T(8,128)S(1)} custom-call(f32[128,512]{1,0:T(8,128)S(1)} %get-tuple-element.50.refs_0_, bf16[1024,4096]{1,0:T(8,128)(2,1)S(1)} %get-tuple-element.35.slab_ref.refs_1_, f32[256,512]{1,0:T(8,128)S(1)} %get-tuple-element.51.refs_2_), custom_call_target="tpu_custom_call" | custom-call | flops 6000000000 | bytes 4194304 | tf_op jit(solution)/shard_map/factor/pallas_call | solution.py:387
  93.2 7.5 %finish.1 = (f32[4096,128]{1,0:T(8,128)}, f32[4096,128]{1,0:T(8,128)}) custom-call(s32[2]{0:T(128)S(1)} %copy-done.4, s32[2,4]{1,0:T(2,128)S(1)} %copy-done.3, s32[1]{0:T(128)} %bitcast.me_ref, bf16[8,128,512]{2,1,0:T(8,128)(2,1)S(1)} %bitcast.83, bf16[512,512]{1,0:T(8,128)(2,1)S(1)} %get-tuple-element.55.gram_ref, ...), custom_call_target="tpu_custom_call", output_to_operand_aliasing={{1}: (8, {})} | custom-call | flops 1073741824 | bytes 16777216 | tf_op jit(solution)/shard_map/finish/pallas_call | solution.py:509
  (87 shorter events, 8.6 us)
Async XLA Ops:
  0.6 2.7 %copy-start.4 = (s32[2]{0:T(128)S(1)}, s32[2]{0:T(128)}, u32[]{:S(2)}) copy-start(s32[2]{0:T(128)} %owner_ref.1) | copy-start | bytes 28
  2.8 2.1 %collective-permute-start = (bf16[2,256,512]{2,1,0:T(8,128)(2,1)S(1)}, bf16[2,256,512]{2,1,0:T(8,128)(2,1)S(1)}, u32[]{:S(2)}, u32[]{:S(2)}) collective-permute-start(bf16[2,256,512]{2,1,0:T(8,128)(2,1)S(1)} %get-tuple-element.30), channel_id=1, source_target_pairs={{0,2},{1,3},{2,0},{3,1},{4,6},{5,7},{6,4},{7,5},{8,10},{9,11},{10,... | collective-permute-start | bytes 1572872 | tf_op jit(solution)/shard_map/ppermute | solution.py:64
  5.1 7.7 %collective-permute-start.2 = (bf16[2,64,512]{2,1,0:T(8,128)(2,1)S(1)}, bf16[2,64,512]{2,1,0:T(8,128)(2,1)S(1)}, u32[]{:S(2)}, u32[]{:S(2)}) collective-permute-start(bf16[2,64,512]{2,1,0:T(8,128)(2,1)S(1)} %get-tuple-element.85), channel_id=1, source_target_pairs={{0,4},{1,5},{2,6},{3,7},{4,0},{5,1},{6,2},{7,3},{8,12},{9,13},{10,... | collective-permute-start | bytes 393224 | tf_op jit(solution)/shard_map/ppermute | solution.py:64
  8.0 6.4 %collective-permute-start.3 = (bf16[2,64,512]{2,1,0:T(8,128)(2,1)S(1)}, bf16[2,64,512]{2,1,0:T(8,128)(2,1)S(1)}, u32[]{:S(2)}, u32[]{:S(2)}) collective-permute-start(bf16[2,64,512]{2,1,0:T(8,128)(2,1)S(1)} %get-tuple-element.86), channel_id=1, source_target_pairs={{0,1},{1,0},{2,3},{3,2},{4,5},{5,4},{6,7},{7,6},{8,9},{9,8},{10,11... | collective-permute-start | bytes 393224 | tf_op jit(solution)/shard_map/ppermute | solution.py:64
  9.5 6.4 %collective-permute-start.1 = (bf16[2,64,512]{2,1,0:T(8,128)(2,1)S(1)}, bf16[2,64,512]{2,1,0:T(8,128)(2,1)S(1)}, u32[]{:S(2)}, u32[]{:S(2)}) collective-permute-start(bf16[2,64,512]{2,1,0:T(8,128)(2,1)S(1)} %get-tuple-element.87), channel_id=1, source_target_pairs={{0,5},{1,4},{2,7},{3,6},{4,1},{5,0},{6,3},{7,2},{8,13},{9,12},{10,... | collective-permute-start | bytes 393224 | tf_op jit(solution)/shard_map/ppermute | solution.py:64
  9.6 29.0 %copy-start.2 = (f32[4096,128]{1,0:T(8,128)S(1)}, f32[4096,128]{1,0:T(8,128)}, u32[]{:S(2)}) copy-start(f32[4096,128]{1,0:T(8,128)} %coef_ref.3) | copy-start | bytes 6291460
  16.0 5.5 %collective-permute-start.4 = (bf16[2,64,512]{2,1,0:T(8,128)(2,1)S(1)}, bf16[2,64,512]{2,1,0:T(8,128)(2,1)S(1)}, u32[]{:S(2)}, u32[]{:S(2)}) collective-permute-start(bf16[2,64,512]{2,1,0:T(8,128)(2,1)S(1)} %fusion.5), channel_id=1, source_target_pairs={{0,8},{1,9},{2,18},{3,19},{4,12},{5,13},{6,22},{7,23},{8,0},{9,1},... | collective-permute-start | bytes 393224 | tf_op jit(solution)/shard_map/ppermute | solution.py:64
  21.6 5.9 %collective-permute-start.5 = (bf16[2,64,512]{2,1,0:T(8,128)(2,1)S(1)}, bf16[2,64,512]{2,1,0:T(8,128)(2,1)S(1)}, u32[]{:S(2)}, u32[]{:S(2)}) collective-permute-start(bf16[2,64,512]{2,1,0:T(8,128)(2,1)S(1)} %broadcast_select_fusion.9), channel_id=1, source_target_pairs={{0,16},{1,17},{2,10},{3,11},{4,20},{5,21},{6,14},{7,15},{8,24},{9,... | collective-permute-start | bytes 393224 | tf_op jit(solution)/shard_map/ppermute | solution.py:64
  27.6 5.6 %collective-permute-start.8 = (bf16[2,64,512]{2,1,0:T(8,128)(2,1)S(1)}, bf16[2,64,512]{2,1,0:T(8,128)(2,1)S(1)}, u32[]{:S(2)}, u32[]{:S(2)}) collective-permute-start(bf16[2,64,512]{2,1,0:T(8,128)(2,1)S(1)} %broadcast_select_fusion.10), channel_id=1, source_target_pairs={{0,1},{1,0},{2,3},{3,2},{4,5},{5,4},{6,7},{7,6},{8,9},{9,8},{10,11... | collective-permute-start | bytes 393224 | tf_op jit(solution)/shard_map/ppermute | solution.py:64
  28.9 5.6 %collective-permute-start.7 = (bf16[2,64,512]{2,1,0:T(8,128)(2,1)S(1)}, bf16[2,64,512]{2,1,0:T(8,128)(2,1)S(1)}, u32[]{:S(2)}, u32[]{:S(2)}) collective-permute-start(bf16[2,64,512]{2,1,0:T(8,128)(2,1)S(1)} %broadcast_select_fusion.10), channel_id=1, source_target_pairs={{0,4},{1,5},{2,6},{3,7},{4,0},{5,1},{6,2},{7,3},{8,12},{9,13},{10,... | collective-permute-start | bytes 393224 | tf_op jit(solution)/shard_map/ppermute | solution.py:64
  30.4 5.9 %collective-permute-start.6 = (bf16[2,64,512]{2,1,0:T(8,128)(2,1)S(1)}, bf16[2,64,512]{2,1,0:T(8,128)(2,1)S(1)}, u32[]{:S(2)}, u32[]{:S(2)}) collective-permute-start(bf16[2,64,512]{2,1,0:T(8,128)(2,1)S(1)} %broadcast_select_fusion.10), channel_id=1, source_target_pairs={{0,5},{1,4},{2,7},{3,6},{4,1},{5,0},{6,3},{7,2},{8,13},{9,12},{10,... | collective-permute-start | bytes 393224 | tf_op jit(solution)/shard_map/ppermute | solution.py:64
  36.3 2.3 %copy-start.1 = (f32[4096,128]{1,0:T(8,128)S(1)}, f32[4096,128]{1,0:T(8,128)}, u32[]{:S(2)}) copy-start(f32[4096,128]{1,0:T(8,128)} %res_ref.3) | copy-start | bytes 6291460
  36.4 2.7 %copy-start = (bf16[4096,512]{1,0:T(8,128)(2,1)S(1)}, bf16[4096,512]{1,0:T(8,128)(2,1)}, u32[]{:S(2)}) copy-start(bf16[4096,512]{1,0:T(8,128)(2,1)} %feat_ref.3) | copy-start | bytes 12582916
  36.4 2.0 %collective-permute-start.9 = (bf16[2,4,64,512]{3,2,1,0:T(8,128)(2,1)S(1)}, bf16[2,4,64,512]{3,2,1,0:T(8,128)(2,1)S(1)}, u32[]{:S(2)}, u32[]{:S(2)}) collective-permute-start(bf16[2,4,64,512]{3,2,1,0:T(8,128)(2,1)S(1)} %pad_maximum_fusion.2), channel_id=1, source_target_pairs={{0,2},{1,3},{2,0},{3,1},{4,6},{5,7},{6,4},{7,5},{8,10},{9,11},{10,... | collective-permute-start | bytes 1572872 | tf_op jit(solution)/shard_map/ppermute | solution.py:64
  50.0 2.4 %collective-permute-start.10 = (f32[2,2,96,512]{3,2,1,0:T(8,128)S(1)}, f32[2,2,96,512]{3,2,1,0:T(8,128)S(1)}, u32[]{:S(2)}, u32[]{:S(2)}) collective-permute-start(f32[2,2,96,512]{3,2,1,0:T(8,128)S(1)} %select_bitcast_fusion), channel_id=1, source_target_pairs={{0,2},{1,3},{2,0},{3,1},{4,6},{5,7},{6,4},{7,5},{8,10},{9,11},{10,... | collective-permute-start | bytes 2359304 | tf_op jit(solution)/shard_map/ppermute | solution.py:64
  52.8 9.3 %collective-permute-start.13 = (bf16[128,512]{1,0:T(8,128)(2,1)S(1)}, bf16[128,512]{1,0:T(8,128)(2,1)S(1)}, u32[]{:S(2)}, u32[]{:S(2)}) collective-permute-start(bf16[128,512]{1,0:T(8,128)(2,1)S(1)} %get-tuple-element.78), channel_id=1, source_target_pairs={{0,5},{1,4},{2,7},{3,6},{4,1},{5,0},{6,3},{7,2},{8,13},{9,12},{10,... | collective-permute-start | bytes 393224 | tf_op jit(solution)/shard_map/ppermute | solution.py:64
  53.6 8.5 %collective-permute-start.12 = (bf16[128,512]{1,0:T(8,128)(2,1)S(1)}, bf16[128,512]{1,0:T(8,128)(2,1)S(1)}, u32[]{:S(2)}, u32[]{:S(2)}) collective-permute-start(bf16[128,512]{1,0:T(8,128)(2,1)S(1)} %get-tuple-element.79), channel_id=1, source_target_pairs={{0,4},{1,5},{2,6},{3,7},{4,0},{5,1},{6,2},{7,3},{8,12},{9,13},{10,... | collective-permute-start | bytes 393224 | tf_op jit(solution)/shard_map/ppermute | solution.py:64
  54.8 7.3 %collective-permute-start.11 = (bf16[128,512]{1,0:T(8,128)(2,1)S(1)}, bf16[128,512]{1,0:T(8,128)(2,1)S(1)}, u32[]{:S(2)}, u32[]{:S(2)}) collective-permute-start(bf16[128,512]{1,0:T(8,128)(2,1)S(1)} %get-tuple-element.80), channel_id=1, source_target_pairs={{0,1},{1,0},{2,3},{3,2},{4,5},{5,4},{6,7},{7,6},{8,9},{9,8},{10,11... | collective-permute-start | bytes 393224 | tf_op jit(solution)/shard_map/ppermute | solution.py:64
  62.5 8.0 %collective-permute-start.14 = (bf16[128,512]{1,0:T(8,128)(2,1)S(1)}, bf16[128,512]{1,0:T(8,128)(2,1)S(1)}, u32[]{:S(2)}, u32[]{:S(2)}) collective-permute-start(bf16[128,512]{1,0:T(8,128)(2,1)S(1)} %pad_maximum_fusion.5), channel_id=1, source_target_pairs={{0,8},{1,9},{2,10},{3,11},{4,12},{5,13},{6,14},{7,15},{8,0},{9,1},... | collective-permute-start | bytes 393224 | tf_op jit(solution)/shard_map/ppermute | solution.py:64
  70.4 20.1 %collective-permute-start.20 = (f32[256,512]{1,0:T(8,128)S(1)}, f32[256,512]{1,0:T(8,128)S(1)}, u32[]{:S(2)}, u32[]{:S(2)}) collective-permute-start(f32[256,512]{1,0:T(8,128)S(1)} %get-tuple-element.41.refs_2_), channel_id=1, source_target_pairs={{0,2},{1,3},{2,0},{3,1},{4,6},{5,7},{6,4},{7,5},{8,10},{9,11},{10,... | collective-permute-start | bytes 1572872 | tf_op jit(solution)/shard_map/ppermute | solution.py:64
  70.7 9.8 %collective-permute-start.15 = (bf16[128,512]{1,0:T(8,128)(2,1)S(1)}, bf16[128,512]{1,0:T(8,128)(2,1)S(1)}, u32[]{:S(2)}, u32[]{:S(2)}) collective-permute-start(bf16[128,512]{1,0:T(8,128)(2,1)S(1)} %pad_maximum_fusion.6), channel_id=1, source_target_pairs={{0,16},{1,17},{2,18},{3,19},{4,20},{5,21},{6,22},{7,23},{8,24},{9,... | collective-permute-start | bytes 393224 | tf_op jit(solution)/shard_map/ppermute | solution.py:64
  74.1 16.6 %collective-permute-start.21 = (f32[256,512]{1,0:T(8,128)S(1)}, f32[256,512]{1,0:T(8,128)S(1)}, u32[]{:S(2)}, u32[]{:S(2)}) collective-permute-start(f32[256,512]{1,0:T(8,128)S(1)} %get-tuple-element.46.refs_2_), channel_id=1, source_target_pairs={{0,2},{1,3},{2,0},{3,1},{4,6},{5,7},{6,4},{7,5},{8,10},{9,11},{10,... | collective-permute-start | bytes 1572872 | tf_op jit(solution)/shard_map/ppermute | solution.py:64
  80.6 9.0 %collective-permute-start.18 = (bf16[128,512]{1,0:T(8,128)(2,1)S(1)}, bf16[128,512]{1,0:T(8,128)(2,1)S(1)}, u32[]{:S(2)}, u32[]{:S(2)}) collective-permute-start(bf16[128,512]{1,0:T(8,128)(2,1)S(1)} %pad_maximum_fusion.7), channel_id=1, source_target_pairs={{0,5},{1,4},{2,7},{3,6},{4,1},{5,0},{6,3},{7,2},{8,13},{9,12},{10,... | collective-permute-start | bytes 393224 | tf_op jit(solution)/shard_map/ppermute | solution.py:64
  81.2 8.5 %collective-permute-start.17 = (bf16[128,512]{1,0:T(8,128)(2,1)S(1)}, bf16[128,512]{1,0:T(8,128)(2,1)S(1)}, u32[]{:S(2)}, u32[]{:S(2)}) collective-permute-start(bf16[128,512]{1,0:T(8,128)(2,1)S(1)} %pad_maximum_fusion.7), channel_id=1, source_target_pairs={{0,4},{1,5},{2,6},{3,7},{4,0},{5,1},{6,2},{7,3},{8,12},{9,13},{10,... | collective-permute-start | bytes 393224 | tf_op jit(solution)/shard_map/ppermute | solution.py:64
  82.7 7.0 %collective-permute-start.16 = (bf16[128,512]{1,0:T(8,128)(2,1)S(1)}, bf16[128,512]{1,0:T(8,128)(2,1)S(1)}, u32[]{:S(2)}, u32[]{:S(2)}) collective-permute-start(bf16[128,512]{1,0:T(8,128)(2,1)S(1)} %pad_maximum_fusion.7), channel_id=1, source_target_pairs={{0,1},{1,0},{2,3},{3,2},{4,5},{5,4},{6,7},{7,6},{8,9},{9,8},{10,11... | collective-permute-start | bytes 393224 | tf_op jit(solution)/shard_map/ppermute | solution.py:64
  89.6 2.0 %collective-permute-start.22 = (f32[256,512]{1,0:T(8,128)S(1)}, f32[256,512]{1,0:T(8,128)S(1)}, u32[]{:S(2)}, u32[]{:S(2)}) collective-permute-start(f32[256,512]{1,0:T(8,128)S(1)} %get-tuple-element.51.refs_2_), channel_id=1, source_target_pairs={{0,2},{1,3},{2,0},{3,1},{4,6},{5,7},{6,4},{7,5},{8,10},{9,11},{10,... | collective-permute-start | bytes 1572872 | tf_op jit(solution)/shard_map/ppermute | solution.py:64
  89.9 2.4 %collective-permute-start.19 = (bf16[2,2,128,512]{3,2,1,0:T(8,128)(2,1)S(1)}, bf16[2,2,128,512]{3,2,1,0:T(8,128)(2,1)S(1)}, u32[]{:S(2)}, u32[]{:S(2)}) collective-permute-start(bf16[2,2,128,512]{3,2,1,0:T(8,128)(2,1)S(1)} %bitcast.88), channel_id=1, source_target_pairs={{0,2},{1,3},{2,0},{3,1},{4,6},{5,7},{6,4},{7,5},{8,10},{9,11},{10,... | collective-permute-start | bytes 1572872 | tf_op jit(solution)/shard_map/ppermute | solution.py:64
  90.5 2.6 %collective-permute-start.23 = (f32[256,512]{1,0:T(8,128)S(1)}, f32[256,512]{1,0:T(8,128)S(1)}, u32[]{:S(2)}, u32[]{:S(2)}) collective-permute-start(f32[256,512]{1,0:T(8,128)S(1)} %factor.7), channel_id=1, source_target_pairs={{0,2},{1,3},{2,0},{3,1},{4,6},{5,7},{6,4},{7,5},{8,10},{9,11},{10,... | collective-permute-start | bytes 1572872 | tf_op jit(solution)/shard_map/ppermute | solution.py:64
  92.4 0.8 copy-start.3

commit v2 on v1

--- a/solution.py
+++ b/solution.py
@@ -136,11 +136,12 @@
         self.count = 8
         self.core_axis = 2 - (core.bit_length() - 1)
 
-    def core_sum(self, value):
-        value = value.reshape((2,) * 3 + value.shape[1:])
-        zero, one = (lax.index_in_dim(value, i, self.core_axis, False) for i in (0, 1))
+    def core_sum(self, packed, exact):
+        packed = packed.reshape((2,) * 3 + packed.shape[1:])
+        zero, one = (lax.index_in_dim(packed, i, self.core_axis, False) for i in (0, 1))
         bit = (self.me & self.core) != 0
-        value = jnp.where(bit, one, zero) + swap(jnp.where(bit, zero, one), self.axes, self.core)
+        got = swap(jnp.where(bit, zero, one), self.axes, self.core)
+        value = unpack(jnp.where(bit, one, zero), exact) + unpack(got, exact)
         return value.reshape((4,) + value.shape[2:])
 
     def near_sum(self, value, exact):
@@ -149,8 +150,10 @@
         place, got = swap_among(lambda place: pick(packed, place), self.me, self.axes, *self.near)
         return lambda got: pick(value, place) + unpack(got[0], exact) + unpack(got[1], exact) + unpack(got[2], exact), got
 
-    def far_sum(self, value, exact, mask):
-        return lambda got: value + unpack(got[0], exact), [swap(pack(value, exact), self.axes, mask)]
+    def far_sum(self, value, exact):
+        packed = pack(value, exact)
+        _, got = swap_among(lambda place: packed, self.me, self.axes, *self.far)
+        return lambda got: value + unpack(got[0], exact) + unpack(got[1], exact) + unpack(got[2], exact), got
 
     def near_gather(self, value):
         _, got = swap_among(lambda place: value, self.me, self.axes, *self.near)
@@ -170,35 +173,27 @@
     return jnp.sum(wide * wide, axis=1, keepdims=True) * scale
 
 
-def gram_kernel(scale, core_ref, block_ref, slab_ref, own_ref, cross_ref):
+def kernel_of(left, right, scale):
+    dots = lax.dot_general(left, right, NT, preferred_element_type=jnp.float32)
+    row = jnp.transpose(jnp.broadcast_to(scaled_norm(right, scale), (BLOCK, 128)))[:1]
+    return jnp.exp(dots * (2.0 * scale) - scaled_norm(left, scale) - row)
+
+
+def gram_kernel(scale, core_ref, block_ref, slab_ref, own_ref):
     mine = block_ref[pl.ds(pl.multiple_of(core_ref[0] * BLOCK, BLOCK), BLOCK), :]
-    eye = jnp.where(
-        lax.broadcasted_iota(jnp.int32, (BLOCK, BLOCK), 0)
-        == lax.broadcasted_iota(jnp.int32, (BLOCK, BLOCK), 1),
-        RIDGE,
-        0.0,
-    )
-    for left, right, shift, out in (
-        (mine, mine, eye, own_ref),
-        (block_ref[:BLOCK], block_ref[BLOCK:], 0.0, cross_ref),
-    ):
-        dots = lax.dot_general(left, right, NT, preferred_element_type=jnp.float32)
-        right_norm = scaled_norm(right, scale)
-        row = jnp.transpose(jnp.broadcast_to(right_norm, (BLOCK, 128)))[:1]
-        value = jnp.exp(dots * (2.0 * scale) - scaled_norm(left, scale) - row)
-        out[...] = (value + shift).astype(out.dtype)
+    diagonal = lax.broadcasted_iota(jnp.int32, (BLOCK, BLOCK), 0) == lax.broadcasted_iota(jnp.int32, (BLOCK, BLOCK), 1)
+    own_ref[...] = kernel_of(mine, mine, scale) + jnp.where(diagonal, RIDGE, 0.0)
 
 
 def gram(block, core, scale, slab):
-    square = (BLOCK, BLOCK)
     vmem = pl.BlockSpec(memory_space=pltpu.VMEM)
     return pl.pallas_call(
         functools.partial(gram_kernel, scale),
         in_specs=[pl.BlockSpec(memory_space=pltpu.SMEM), vmem, vmem],
-        out_shape=(jax.ShapeDtypeStruct(square, jnp.float32), jax.ShapeDtypeStruct(square, jnp.bfloat16)),
+        out_shape=jax.ShapeDtypeStruct((BLOCK, BLOCK), jnp.float32),
         compiler_params=pltpu.CompilerParams(vmem_limit_bytes=SMALL_LIMIT),
         cost_estimate=pl.CostEstimate(
-            flops=2 * 2 * BLOCK**3, bytes_accessed=4 * BLOCK * BLOCK * 4, transcendentals=2 * BLOCK**2
+            flops=2 * BLOCK**3, bytes_accessed=4 * BLOCK * BLOCK * 2, transcendentals=BLOCK**2
         ),
         name="gram",
     )(core, block, in_vmem(slab))
@@ -231,22 +226,27 @@
             norm_wide = jnp.concatenate([bnorm[at_of(p)]] * (chunk // bnorm.shape[1]), axis=1)
             slab = jnp.exp2(dots * (2.0 * scale2) - norm_wide - norm_row).astype(jnp.bfloat16)
             slab_ref[at_of(p), rows] = slab
-            grad[at_of(p)] += jnp.dot(slab, weighted, preferred_element_type=jnp.float32)
+            if p < parts // 2:
+                grad[at_of(p)] += jnp.dot(slab, weighted, preferred_element_type=jnp.float32)
             dots = ahead
         ahead_ref[...] = dots
-        cross[...] += lax.dot_general(
-            slab_ref[:BLOCK, rows], slab_ref[BLOCK:, rows], NT, preferred_element_type=jnp.float32
-        )
+        left = jnp.concatenate([slab_ref[:BLOCK, rows], jnp.transpose(weighted)], axis=0)
+        cross[...] += lax.dot_general(left, slab_ref[BLOCK:, rows], NT, preferred_element_type=jnp.float32)
         return 0
 
     lax.fori_loop(0, chunks, body, 0, unroll=2)
-    grads = jnp.transpose(grad[...])
+    grads = jnp.concatenate([jnp.transpose(grad[...]), cross[BLOCK:]], axis=1)
     groups = piece_ref.shape[0]
     own, depth = grads.shape[0] // groups, BLOCK // groups
+    exact = STEPS * own
+    high = grads.astype(jnp.bfloat16)
+    low = (grads - high.astype(jnp.float32)).astype(jnp.bfloat16)
     for d in range(groups):
         for s in range(STEPS):
-            piece_ref[d, s * own : (s + 1) * own] = grads[d * own : (d + 1) * own, s * BLOCK : (s + 1) * BLOCK]
-        piece_ref[d, STEPS * own :] = cross[d * depth : (d + 1) * depth]
+            there = (slice(d * own, (d + 1) * own), slice(s * BLOCK, (s + 1) * BLOCK))
+            piece_ref[d, s * own : (s + 1) * own] = high[there]
+            piece_ref[d, exact + s * own : exact + (s + 1) * own] = low[there]
+        piece_ref[d, 2 * exact :] = cross[d * depth : (d + 1) * depth].astype(jnp.bfloat16)
 
 
 def in_vmem(value):
@@ -257,14 +257,14 @@
     rows, width = features.shape
     targets = residual.shape[1]
     both = STEPS * BLOCK
-    piece = (groups, STEPS * targets // groups + BLOCK // groups, BLOCK)
+    piece = (groups, 2 * STEPS * targets // groups + BLOCK // groups, BLOCK)
     return pl.pallas_call(
         functools.partial(slab_kernel, scale, chunk),
-        out_shape=(pltpu.VMEM((both, rows), jnp.bfloat16), jax.ShapeDtypeStruct(piece, jnp.float32)),
+        out_shape=(pltpu.VMEM((both, rows), jnp.bfloat16), jax.ShapeDtypeStruct(piece, jnp.bfloat16)),
         scratch_shapes=[
             pltpu.VMEM((both, 128), jnp.float32),
-            pltpu.VMEM((both, targets), jnp.float32),
-            pltpu.VMEM((BLOCK, BLOCK), jnp.float32),
+            pltpu.VMEM((BLOCK, targets), jnp.float32),
+            pltpu.VMEM((BLOCK + targets, BLOCK), jnp.float32),
             pltpu.VMEM((BLOCK // 2, chunk), jnp.float32),
         ],
         compiler_params=pltpu.CompilerParams(vmem_limit_bytes=VMEM_LIMIT),
@@ -323,7 +323,7 @@
     return [functools.partial(update, u) for u in range(t + 2, len(tiles))]
 
 
-def factor_kernel(index, copied, *refs):
+def factor_kernel(index, copied, scale, *refs):
     refs = list(refs)
     rest_ref, _ = refs.pop(0), refs.pop(0)
     before_ref = refs.pop(0) if index else None
@@ -332,6 +332,9 @@
         sem = refs.pop()
         copy = pltpu.make_async_copy(refs.pop(0), refs.pop(), sem)
         copy.start()
+    if index == 1:
+        block_ref, cross_ref = refs.pop(0), refs.pop()
+        cross_ref[...] = kernel_of(block_ref[:BLOCK], block_ref[BLOCK:], scale).astype(cross_ref.dtype)
     factor_ref = refs[0]
     here = slice(index * TILE, (index + 1) * TILE)
     dot = functools.partial(lax.dot_general, precision=HIGH, preferred_element_type=jnp.float32)
@@ -368,7 +371,7 @@
         copy.wait()
 
 
-def factor_step(rest, index, slab, before=None, copied=None):
+def factor_step(rest, index, slab, before=None, copied=None, block=None, scale=None):
     left = BLOCK - (index + 1) * TILE
     vmem, hbm = pl.BlockSpec(memory_space=pltpu.VMEM), pl.BlockSpec(memory_space=pltpu.HBM)
     out = [jax.ShapeDtypeStruct((2 * TILE, BLOCK), jnp.float32)]
@@ -377,6 +380,9 @@
         inputs.append(before)
         if left:
             out.append(jax.ShapeDtypeStruct((left, BLOCK), jnp.float32))
+    if block is not None:
+        inputs.append(block)
+        out.append(jax.ShapeDtypeStruct((BLOCK, BLOCK), jnp.bfloat16))
     in_specs, out_specs = [vmem] * len(inputs), [vmem] * len(out)
     if copied is not None:
         inputs.append(in_vmem(copied))
@@ -385,7 +391,7 @@
         out_specs.append(hbm)
         scratch.insert(0, pltpu.SemaphoreType.DMA)
     return pl.pallas_call(
-        functools.partial(factor_kernel, index, copied is not None),
+        functools.partial(factor_kernel, index, copied is not None, scale),
         in_specs=in_specs,
         out_specs=tuple(out_specs),
         out_shape=tuple(out),
@@ -413,7 +419,7 @@
 
 def final_kernel(step_size, chunk, owner_ref, tiles_ref, me_ref, packed_ref, gram_ref, slab_ref, res_ref, coef_ref, base_ref, *refs):
     factors, refs = refs[: 2 * (BLOCK // TILE)], refs[2 * (BLOCK // TILE) :]
-    res_out, coef_out, upd_ref, wide_ref, ahead_ref, res_buf, tile_buf, res_sems, tile_sems = refs
+    res_out, coef_out, upd_ref, wide_ref, part_ref, ahead_ref, res_buf, tile_buf, res_sems, tile_sems = refs
     rows, targets = res_ref.shape
     own = targets // packed_ref.shape[0]
     exact = STEPS * own
@@ -428,14 +434,16 @@
     first = apply_inverse(gradient(0), factors[:count]) * step_size
     high = first.astype(jnp.bfloat16)
     low = (first - high.astype(jnp.float32)).astype(jnp.bfloat16)
+    for i in range(rows // chunk):
+        at = slice(i * chunk, (i + 1) * chunk)
+        part_ref[:, at] = dot(high, slab_ref[:BLOCK, at])
     cross = packed_ref[:, 2 * exact :].reshape(BLOCK, BLOCK)
     block_part = dot(high, gram_ref[...]) + dot(low, gram_ref[...])
     again = gradient(1) - dot(high, cross) - RIDGE * block_part
     second = apply_inverse(again, factors[count:]) * step_size
     wide_ref[:, :BLOCK] = first
     wide_ref[:, BLOCK:] = second
-    upd_ref[:, :BLOCK] = high
-    upd_ref[:, BLOCK:] = second.astype(jnp.bfloat16)
+    upd_ref[...] = second.astype(jnp.bfloat16)
 
     def change_of(s, k):
         at = s * BLOCK + k * TILE
@@ -478,7 +486,8 @@
         return pltpu.make_async_copy(res_buf.at[rows_of(i), :], res_out.at[rows_of(i), :], res_sems.at[i])
 
     def product(i):
-        return jnp.dot(upd_ref[...], slab_ref[:, rows_of(i)], preferred_element_type=jnp.float32)
+        change = jnp.dot(upd_ref[...], slab_ref[BLOCK:, rows_of(i)], preferred_element_type=jnp.float32)
+        return part_ref[:, rows_of(i)] + change
 
     ahead_ref[...] = product(0)
 
@@ -515,8 +524,9 @@
             pltpu.HBM(residual.shape, jnp.float32),
         ),
         scratch_shapes=[
-            pltpu.VMEM((targets, both), jnp.bfloat16),
+            pltpu.VMEM((targets, BLOCK), jnp.bfloat16),
             pltpu.VMEM((targets, both), jnp.float32),
+            pltpu.VMEM((targets, rows), jnp.float32),
             pltpu.VMEM((targets, chunk), jnp.float32),
             pltpu.VMEM((rows, targets), jnp.float32),
             pltpu.VMEM((STEPS, count, TILE, targets), jnp.float32),
@@ -548,33 +558,37 @@
     norms = (jnp.sum(wide * wide, axis=1) * scale).reshape(1, rows_dev)
     block, norms = fetch_blocks(features, norms, block_owner, block_tiles, me, devices, sub_count)
     slab, pieces = slabs(block, features, norms, residual, coefficients, scale, groups)
+    exact = STEPS * own
     if spread.axes != AXES:
-        pieces = lax.psum(pieces, "sub")
+        pieces = pack(lax.psum(unpack(pieces, exact), "sub"), exact)
     core, on_core = bit_of(me, sub_count), (me & sub_count) != 0
-    rest, gram12 = gram(block, core.reshape(1), scale, slab)
-    factors, before, copied = ([], []), None, []
-
-    def beside(hop, index, rest):
-        nonlocal before
+    rest = gram(block, core.reshape(1), scale, slab)
+    factors, before, extra = ([], []), None, []
+
+    def beside(hop, indices):
+        nonlocal before, rest
         then, got = hop
-        mine, *given = factor_step(rest, index, slab, before, None if index else coefficients)
-        if not index:
-            copied.append(given.pop())
-        got, mine, given = lax.optimization_barrier((got, mine, given))
-        before = mine
-        other = swap(mine, AXES, sub_count)
-        factors[0].append(jnp.where(on_core, other, mine))
-        factors[1].append(jnp.where(on_core, mine, other))
-        return then(got), given[0] if given else rest
-
-    value = spread.core_sum(pieces)
-    value, rest = beside(spread.near_sum(value, STEPS * own), 0, rest)
-    for index, mask in enumerate(spread.far):
-        value, rest = beside(spread.far_sum(value, STEPS * own, mask), 1 + index, rest)
-    packed, rest = beside(spread.near_gather(pack(value, STEPS * own)), 3, rest)
+        for index in indices:
+            args = {0: {"copied": coefficients}, 1: {"block": block, "scale": scale}}.get(index, {})
+            mine, *given = factor_step(rest, index, slab, before, **args)
+            if args:
+                extra.append(given.pop())
+            if index == indices[-1]:
+                got, mine, given = lax.optimization_barrier((got, mine, given))
+            before, rest = mine, given[0] if given else rest
+            other = swap(mine, AXES, sub_count)
+            factors[0].append(jnp.where(on_core, other, mine))
+            factors[1].append(jnp.where(on_core, mine, other))
+        return then(got)
+
+    value = spread.core_sum(pieces, exact)
+    value = beside(spread.near_sum(value, exact), [0])
+    value = beside(spread.far_sum(value, exact), [1, 2])
+    packed = beside(spread.near_gather(pack(value, exact)), [3])
+    base, gram12 = extra
     packed = spread.core_gather(packed)
     return finish(
-        block_owner, block_tiles, me.reshape(1), packed, gram12, slab, residual, coefficients, copied[0],
+        block_owner, block_tiles, me.reshape(1), packed, gram12, slab, residual, coefficients, base,
         factors[0] + factors[1], step_size,
     )
 

time: 101 us -> 101 us (level)
  local copies, waits for them, and re-layouts: 0.73 us -> 1.9 us
  Pallas kernels: 43.7 us -> 42.6 us
    unnamed x10 -> x12, local copies, waits for them, and re-layouts: 0.53 us -> 1.62 us
    ppermute x24 -> x25, waiting for transfers between devices: 22.4 us -> 21.8 us  [swap(): lax.ppermute(value, axes, [(i, i ^ flip_of(i)) for i in range(lax.axis_si...]
    ppermute x24 -> x25, starting transfers between devices: 27.2 us -> 27.6 us  [swap(): lax.ppermute(value, axes, [(i, i ^ flip_of(i)) for i in range(lax.axis_si...]
  transfers between devices with their start and end apart: 24 -> 25, of which waited for: 14 -> 13; matrix products, arithmetic and copies ran while one was open for 4% -> 4% of each run, Pallas kernels for 23% -> 23%
where the time goes in v2:
time: 101 us
  Pallas kernels  42.6 us (42%)
  starting transfers between devices  27.6 us (27%)
  waiting for transfers between devices  21.8 us (22%)
  other arithmetic  5.45 us (5%)
  local copies, waits for them, and re-layouts  1.9 us (2%)
  between operations  1.45 us (1%)
    ppermute x25, starting transfers between devices, swap(): lax.ppermute(value, axes, [(i, i ^ flip_of(i)) for i in range(lax.axis_si...  27.6 us
    pallas_call x4, Pallas kernels, factor_step(): pl.pallas_call(functools.partial(factor_kernel, index, copied is not None...  22.7 us
    ppermute x25, waiting for transfers between devices, swap(): lax.ppermute(value, axes, [(i, i ^ flip_of(i)) for i in range(lax.axis_si...  21.8 us
    pallas_call x1, Pallas kernels, slabs(): pl.pallas_call(functools.partial(slab_kernel, scale, chunk), out_shape=(p...  9.97 us
    pallas_call x1, Pallas kernels, finish(): pl.pallas_call(functools.partial(final_kernel, step_size, chunk), in_spec...  7.32 us
    reduce_sum x1, other arithmetic, local(): norms = (jnp.sum(wide * wide, axis=1) * scale).reshape(1, rows_dev)  3.08 us
    pallas_call x1, Pallas kernels, pick_halves(): pl.pallas_call(pick_kernel, grid_spec=pltpu.PrefetchScalarGridSpec(num_sc...  2.05 us
  transfers between devices with their start and end apart: 25, of which 13 were waited for; matrix products, arithmetic and copies ran while one was open for 4% of the time, Pallas kernels for 23%

profile of v2, /device:TPU:0, one launch (start us, length us, event | category | flops | bytes accessed | tf_op | source)
XLA Modules:
  0.0 100.8 jit_solution(10336810860848251742)
XLA Ops:
  0.6 2.0 %pick.1 = (bf16[2,256,512]{2,1,0:T(8,128)(2,1)S(1)}, bf16[2,256,512]{2,1,0:T(8,128)(2,1)S(1)}) custom-call(s32[2,4]{1,0:T(2,128)} %tiles_ref.3, s32[1]{0:T(128)} %bitcast.1.core_ref, bf16[4096,512]{1,0:T(8,128)(2,1)} %feat_ref.3), custom_call_target="tpu_custom_call" | custom-call | tf_op jit(solution)/shard_map/pick/pallas_call | solution.py:47
  3.3 1.5 %collective-permute-done = bf16[2,256,512]{2,1,0:T(8,128)(2,1)S(1)} collective-permute-done((bf16[2,256,512]{2,1,0:T(8,128)(2,1)S(1)}, bf16[2,256,512]{2,1,0:T(8,128)(2,1)S(1)}, u32[]{:S(2)}, u32[]{:S(2)}) %collective-permute-start) | collective-permute-done | bytes 524320 | tf_op jit(solution)/shard_map/ppermute | solution.py:64
  4.9 3.0 %collective-permute-start.2 = (bf16[2,64,512]{2,1,0:T(8,128)(2,1)S(1)}, bf16[2,64,512]{2,1,0:T(8,128)(2,1)S(1)}, u32[]{:S(2)}, u32[]{:S(2)}) collective-permute-start(bf16[2,64,512]{2,1,0:T(8,128)(2,1)S(1)} %get-tuple-element.83), channel_id=1, source_target_pairs={{0,4},{1,5},{2,6},{3,7},{4,0},{5,1},{6,2},{7,3},{8,12},{9,13},{10,... | collective-permute-start | bytes 393224 | tf_op jit(solution)/shard_map/ppermute | solution.py:64
  7.9 1.5 %collective-permute-start.3 = (bf16[2,64,512]{2,1,0:T(8,128)(2,1)S(1)}, bf16[2,64,512]{2,1,0:T(8,128)(2,1)S(1)}, u32[]{:S(2)}, u32[]{:S(2)}) collective-permute-start(bf16[2,64,512]{2,1,0:T(8,128)(2,1)S(1)} %get-tuple-element.84), channel_id=1, source_target_pairs={{0,1},{1,0},{2,3},{3,2},{4,5},{5,4},{6,7},{7,6},{8,9},{9,8},{10,11... | collective-permute-start | bytes 393224 | tf_op jit(solution)/shard_map/ppermute | solution.py:64
  9.4 3.1 %multiply_reduce_fusion = f32[4096]{0:T(1024)S(1)} fusion(bf16[4096,512]{1,0:T(8,128)(2,1)} %feat_ref.3), kind=kLoop, calls=%fused_computation | loop fusion | flops 6287360 | bytes 4210688 | tf_op jit(solution)/shard_map/reduce_sum | solution.py:558
  12.5 1.7 %collective-permute-done.3 = bf16[2,64,512]{2,1,0:T(8,128)(2,1)S(1)} collective-permute-done((bf16[2,64,512]{2,1,0:T(8,128)(2,1)S(1)}, bf16[2,64,512]{2,1,0:T(8,128)(2,1)S(1)}, u32[]{:S(2)}, u32[]{:S(2)}) %collective-permute-start.3) | collective-permute-done | bytes 131104 | tf_op jit(solution)/shard_map/ppermute | solution.py:64
  14.3 1.5 %collective-permute-done.1 = bf16[2,64,512]{2,1,0:T(8,128)(2,1)S(1)} collective-permute-done((bf16[2,64,512]{2,1,0:T(8,128)(2,1)S(1)}, bf16[2,64,512]{2,1,0:T(8,128)(2,1)S(1)}, u32[]{:S(2)}, u32[]{:S(2)}) %collective-permute-start.1) | collective-permute-done | bytes 131104 | tf_op jit(solution)/shard_map/ppermute | solution.py:64
  15.8 1.8 %collective-permute-start.4 = (bf16[2,64,512]{2,1,0:T(8,128)(2,1)S(1)}, bf16[2,64,512]{2,1,0:T(8,128)(2,1)S(1)}, u32[]{:S(2)}, u32[]{:S(2)}) collective-permute-start(bf16[2,64,512]{2,1,0:T(8,128)(2,1)S(1)} %fusion.5), channel_id=1, source_target_pairs={{0,8},{1,9},{2,18},{3,19},{4,12},{5,13},{6,22},{7,23},{8,0},{9,1},... | collective-permute-start | bytes 393224 | tf_op jit(solution)/shard_map/ppermute | solution.py:64
  17.6 3.7 %collective-permute-done.4 = bf16[2,64,512]{2,1,0:T(8,128)(2,1)S(1)} collective-permute-done((bf16[2,64,512]{2,1,0:T(8,128)(2,1)S(1)}, bf16[2,64,512]{2,1,0:T(8,128)(2,1)S(1)}, u32[]{:S(2)}, u32[]{:S(2)}) %collective-permute-start.4) | collective-permute-done | bytes 131104 | tf_op jit(solution)/shard_map/ppermute | solution.py:64
  21.4 2.7 %collective-permute-start.5 = (bf16[2,64,512]{2,1,0:T(8,128)(2,1)S(1)}, bf16[2,64,512]{2,1,0:T(8,128)(2,1)S(1)}, u32[]{:S(2)}, u32[]{:S(2)}) collective-permute-start(bf16[2,64,512]{2,1,0:T(8,128)(2,1)S(1)} %broadcast_select_fusion.9), channel_id=1, source_target_pairs={{0,16},{1,17},{2,10},{3,11},{4,20},{5,21},{6,14},{7,15},{8,24},{9,... | collective-permute-start | bytes 393224 | tf_op jit(solution)/shard_map/ppermute | solution.py:64
  24.1 3.3 %collective-permute-done.5 = bf16[2,64,512]{2,1,0:T(8,128)(2,1)S(1)} collective-permute-done((bf16[2,64,512]{2,1,0:T(8,128)(2,1)S(1)}, bf16[2,64,512]{2,1,0:T(8,128)(2,1)S(1)}, u32[]{:S(2)}, u32[]{:S(2)}) %collective-permute-start.5) | collective-permute-done | bytes 131104 | tf_op jit(solution)/shard_map/ppermute | solution.py:64
  27.5 1.3 %collective-permute-start.8 = (bf16[2,64,512]{2,1,0:T(8,128)(2,1)S(1)}, bf16[2,64,512]{2,1,0:T(8,128)(2,1)S(1)}, u32[]{:S(2)}, u32[]{:S(2)}) collective-permute-start(bf16[2,64,512]{2,1,0:T(8,128)(2,1)S(1)} %broadcast_select_fusion.10), channel_id=1, source_target_pairs={{0,1},{1,0},{2,3},{3,2},{4,5},{5,4},{6,7},{7,6},{8,9},{9,8},{10,11... | collective-permute-start | bytes 393224 | tf_op jit(solution)/shard_map/ppermute | solution.py:64
  28.7 1.5 %collective-permute-start.7 = (bf16[2,64,512]{2,1,0:T(8,128)(2,1)S(1)}, bf16[2,64,512]{2,1,0:T(8,128)(2,1)S(1)}, u32[]{:S(2)}, u32[]{:S(2)}) collective-permute-start(bf16[2,64,512]{2,1,0:T(8,128)(2,1)S(1)} %broadcast_select_fusion.10), channel_id=1, source_target_pairs={{0,4},{1,5},{2,6},{3,7},{4,0},{5,1},{6,2},{7,3},{8,12},{9,13},{10,... | collective-permute-start | bytes 393224 | tf_op jit(solution)/shard_map/ppermute | solution.py:64
  31.0 2.1 %collective-permute-done.8 = bf16[2,64,512]{2,1,0:T(8,128)(2,1)S(1)} collective-permute-done((bf16[2,64,512]{2,1,0:T(8,128)(2,1)S(1)}, bf16[2,64,512]{2,1,0:T(8,128)(2,1)S(1)}, u32[]{:S(2)}, u32[]{:S(2)}) %collective-permute-start.8) | collective-permute-done | bytes 131104 | tf_op jit(solution)/shard_map/ppermute | solution.py:64
  33.1 1.3 %collective-permute-done.7 = bf16[2,64,512]{2,1,0:T(8,128)(2,1)S(1)} collective-permute-done((bf16[2,64,512]{2,1,0:T(8,128)(2,1)S(1)}, bf16[2,64,512]{2,1,0:T(8,128)(2,1)S(1)}, u32[]{:S(2)}, u32[]{:S(2)}) %collective-permute-start.7) | collective-permute-done | bytes 131104 | tf_op jit(solution)/shard_map/ppermute | solution.py:64
  34.3 1.8 %collective-permute-done.6 = bf16[2,64,512]{2,1,0:T(8,128)(2,1)S(1)} collective-permute-done((bf16[2,64,512]{2,1,0:T(8,128)(2,1)S(1)}, bf16[2,64,512]{2,1,0:T(8,128)(2,1)S(1)}, u32[]{:S(2)}, u32[]{:S(2)}) %collective-permute-start.6) | collective-permute-done | bytes 131104 | tf_op jit(solution)/shard_map/ppermute | solution.py:64
  36.3 1.9 %collective-permute-done.9 = bf16[2,4,64,512]{3,2,1,0:T(8,128)(2,1)S(1)} collective-permute-done((bf16[2,4,64,512]{3,2,1,0:T(8,128)(2,1)S(1)}, bf16[2,4,64,512]{3,2,1,0:T(8,128)(2,1)S(1)}, u32[]{:S(2)}, u32[]{:S(2)}) %collective-permute-start.9) | collective-permute-done | bytes 524320 | tf_op jit(solution)/shard_map/ppermute | solution.py:64
  38.5 1.6 %copy-done.2 = f32[4096,128]{1,0:T(8,128)S(1)} copy-done((f32[4096,128]{1,0:T(8,128)S(1)}, f32[4096,128]{1,0:T(8,128)}, u32[]{:S(2)}) %copy-start.2) | copy-done | bytes 2097176
  40.0 10.0 %slabs.1 = (bf16[1024,4096]{1,0:T(8,128)(2,1)S(1)}, bf16[8,128,512]{2,1,0:T(8,128)(2,1)S(1)}) custom-call(bf16[1024,512]{1,0:T(8,128)(2,1)S(1)} %bitcast.69, bf16[4096,512]{1,0:T(8,128)(2,1)S(1)} %copy-done, f32[1,4096]{1,0:T(1,128)S(1)} %bitcast.74, f32[4096,128]{1,0:T(8,128)S(1)} %copy-done.1, f32[4096,128]{1,0:T(8,128)S(1)} %copy-done.2), custom_call_target="tpu_custom_call" | custom-call | flops 7516192768 | bytes 16777216 | tf_op jit(solution)/shard_map/slabs/pallas_call | solution.py:261
  51.0 1.1 %collective-permute-done.10 = bf16[2,2,128,512]{3,2,1,0:T(8,128)(2,1)S(1)} collective-permute-done((bf16[2,2,128,512]{3,2,1,0:T(8,128)(2,1)S(1)}, bf16[2,2,128,512]{3,2,1,0:T(8,128)(2,1)S(1)}, u32[]{:S(2)}, u32[]{:S(2)}) %collective-permute-start.10) | collective-permute-done | bytes 524320 | tf_op jit(solution)/shard_map/ppermute | solution.py:64
  52.7 0.8 collective-permute-start.13
  53.5 1.2 %collective-permute-start.12 = (bf16[128,512]{1,0:T(8,128)(2,1)S(1)}, bf16[128,512]{1,0:T(8,128)(2,1)S(1)}, u32[]{:S(2)}, u32[]{:S(2)}) collective-permute-start(bf16[128,512]{1,0:T(8,128)(2,1)S(1)} %get-tuple-element.77), channel_id=1, source_target_pairs={{0,4},{1,5},{2,6},{3,7},{4,0},{5,1},{6,2},{7,3},{8,12},{9,13},{10,... | collective-permute-start | bytes 393224 | tf_op jit(solution)/shard_map/ppermute | solution.py:64
  54.7 1.5 %collective-permute-start.11 = (bf16[128,512]{1,0:T(8,128)(2,1)S(1)}, bf16[128,512]{1,0:T(8,128)(2,1)S(1)}, u32[]{:S(2)}, u32[]{:S(2)}) collective-permute-start(bf16[128,512]{1,0:T(8,128)(2,1)S(1)} %get-tuple-element.78), channel_id=1, source_target_pairs={{0,1},{1,0},{2,3},{3,2},{4,5},{5,4},{6,7},{7,6},{8,9},{9,8},{10,11... | collective-permute-start | bytes 393224 | tf_op jit(solution)/shard_map/ppermute | solution.py:64
  56.2 5.8 %factor.4 = (f32[256,512]{1,0:T(8,128)S(1)}, f32[4096,128]{1,0:T(8,128)}) custom-call(f32[512,512]{1,0:T(8,128)S(1)} %gram.1.refs_0_, bf16[1024,4096]{1,0:T(8,128)(2,1)S(1)} %get-tuple-element.33.slab_ref.refs_1_, f32[4096,128]{1,0:T(8,128)S(1)} %copy-done.3), custom_call_target="tpu_custom_call" | custom-call | flops 6000000000 | bytes 4194304 | tf_op jit(solution)/shard_map/factor/pallas_call | solution.py:393
  62.4 5.3 %collective-permute-start.16 = (bf16[128,512]{1,0:T(8,128)(2,1)S(1)}, bf16[128,512]{1,0:T(8,128)(2,1)S(1)}, u32[]{:S(2)}, u32[]{:S(2)}) collective-permute-start(bf16[128,512]{1,0:T(8,128)(2,1)S(1)} %pad_maximum_fusion.5), channel_id=1, source_target_pairs={{0,24},{1,25},{2,26},{3,27},{4,28},{5,29},{6,30},{7,31},{8,16},{9,... | collective-permute-start | bytes 393224 | tf_op jit(solution)/shard_map/ppermute | solution.py:64
  68.3 5.8 %factor.5 = (f32[256,512]{1,0:T(8,128)S(1)}, f32[256,512]{1,0:T(8,128)S(1)}, bf16[512,512]{1,0:T(8,128)(2,1)S(1)}) custom-call(f32[512,512]{1,0:T(8,128)S(1)} %gram.1.refs_0_, bf16[1024,4096]{1,0:T(8,128)(2,1)S(1)} %get-tuple-element.33.slab_ref.refs_1_, f32[256,512]{1,0:T(8,128)S(1)} %get-tuple-element.38.refs_2_, bf16[1024,512]{1,0:T(8,128)(2,1)S(1)} %bitcast.71), custom_call_target="tpu_custom_call" | custom-call | flops 6000000000 | bytes 4194304 | tf_op jit(solution)/shard_map/factor/pallas_call | solution.py:393
  74.7 5.7 %factor.6 = (f32[256,512]{1,0:T(8,128)S(1)}, f32[128,512]{1,0:T(8,128)S(1)}) custom-call(f32[256,512]{1,0:T(8,128)S(1)} %get-tuple-element.39.refs_0_, bf16[1024,4096]{1,0:T(8,128)(2,1)S(1)} %get-tuple-element.33.slab_ref.refs_1_, f32[256,512]{1,0:T(8,128)S(1)} %get-tuple-element.40.refs_2_), custom_call_target="tpu_custom_call" | custom-call | flops 6000000000 | bytes 4194304 | tf_op jit(solution)/shard_map/factor/pallas_call | solution.py:393
  81.3 1.5 %collective-permute-start.18 = (bf16[128,512]{1,0:T(8,128)(2,1)S(1)}, bf16[128,512]{1,0:T(8,128)(2,1)S(1)}, u32[]{:S(2)}, u32[]{:S(2)}) collective-permute-start(bf16[128,512]{1,0:T(8,128)(2,1)S(1)} %pad_maximum_fusion.6), channel_id=1, source_target_pairs={{0,4},{1,5},{2,6},{3,7},{4,0},{5,1},{6,2},{7,3},{8,12},{9,13},{10,... | collective-permute-start | bytes 393224 | tf_op jit(solution)/shard_map/ppermute | solution.py:64
  82.8 1.5 %collective-permute-start.17 = (bf16[128,512]{1,0:T(8,128)(2,1)S(1)}, bf16[128,512]{1,0:T(8,128)(2,1)S(1)}, u32[]{:S(2)}, u32[]{:S(2)}) collective-permute-start(bf16[128,512]{1,0:T(8,128)(2,1)S(1)} %pad_maximum_fusion.6), channel_id=1, source_target_pairs={{0,1},{1,0},{2,3},{3,2},{4,5},{5,4},{6,7},{7,6},{8,9},{9,8},{10,11... | collective-permute-start | bytes 393224 | tf_op jit(solution)/shard_map/ppermute | solution.py:64
  84.3 5.4 %factor.7 = f32[256,512]{1,0:T(8,128)S(1)} custom-call(f32[128,512]{1,0:T(8,128)S(1)} %get-tuple-element.46.refs_0_, bf16[1024,4096]{1,0:T(8,128)(2,1)S(1)} %get-tuple-element.33.slab_ref.refs_1_, f32[256,512]{1,0:T(8,128)S(1)} %get-tuple-element.47.refs_2_), custom_call_target="tpu_custom_call" | custom-call | flops 6000000000 | bytes 4194304 | tf_op jit(solution)/shard_map/factor/pallas_call | solution.py:393
  90.9 0.8 collective-permute-done.23
  93.3 7.3 %finish.1 = (f32[4096,128]{1,0:T(8,128)}, f32[4096,128]{1,0:T(8,128)}) custom-call(s32[2]{0:T(128)S(1)} %copy-done.5, s32[2,4]{1,0:T(2,128)S(1)} %copy-done.4, s32[1]{0:T(128)} %bitcast.me_ref, bf16[8,128,512]{2,1,0:T(8,128)(2,1)S(1)} %bitcast.72, bf16[512,512]{1,0:T(8,128)(2,1)S(1)} %get-tuple-element.51.gram_ref, ...), custom_call_target="tpu_custom_call", output_to_operand_aliasing={{1}: (8, {})} | custom-call | flops 1073741824 | bytes 16777216 | tf_op jit(solution)/shard_map/finish/pallas_call | solution.py:518
  (95 shorter events, 8.6 us)
Async XLA Ops:
  0.6 2.6 %copy-start.5 = (s32[2]{0:T(128)S(1)}, s32[2]{0:T(128)}, u32[]{:S(2)}) copy-start(s32[2]{0:T(128)} %owner_ref.1) | copy-start | bytes 28
  2.7 2.1 %collective-permute-start = (bf16[2,256,512]{2,1,0:T(8,128)(2,1)S(1)}, bf16[2,256,512]{2,1,0:T(8,128)(2,1)S(1)}, u32[]{:S(2)}, u32[]{:S(2)}) collective-permute-start(bf16[2,256,512]{2,1,0:T(8,128)(2,1)S(1)} %get-tuple-element.28), channel_id=1, source_target_pairs={{0,2},{1,3},{2,0},{3,1},{4,6},{5,7},{6,4},{7,5},{8,10},{9,11},{10,... | collective-permute-start | bytes 1572872 | tf_op jit(solution)/shard_map/ppermute | solution.py:64
  4.9 7.6 %collective-permute-start.2 = (bf16[2,64,512]{2,1,0:T(8,128)(2,1)S(1)}, bf16[2,64,512]{2,1,0:T(8,128)(2,1)S(1)}, u32[]{:S(2)}, u32[]{:S(2)}) collective-permute-start(bf16[2,64,512]{2,1,0:T(8,128)(2,1)S(1)} %get-tuple-element.83), channel_id=1, source_target_pairs={{0,4},{1,5},{2,6},{3,7},{4,0},{5,1},{6,2},{7,3},{8,12},{9,13},{10,... | collective-permute-start | bytes 393224 | tf_op jit(solution)/shard_map/ppermute | solution.py:64
  7.9 6.4 %collective-permute-start.3 = (bf16[2,64,512]{2,1,0:T(8,128)(2,1)S(1)}, bf16[2,64,512]{2,1,0:T(8,128)(2,1)S(1)}, u32[]{:S(2)}, u32[]{:S(2)}) collective-permute-start(bf16[2,64,512]{2,1,0:T(8,128)(2,1)S(1)} %get-tuple-element.84), channel_id=1, source_target_pairs={{0,1},{1,0},{2,3},{3,2},{4,5},{5,4},{6,7},{7,6},{8,9},{9,8},{10,11... | collective-permute-start | bytes 393224 | tf_op jit(solution)/shard_map/ppermute | solution.py:64
  9.4 6.4 %collective-permute-start.1 = (bf16[2,64,512]{2,1,0:T(8,128)(2,1)S(1)}, bf16[2,64,512]{2,1,0:T(8,128)(2,1)S(1)}, u32[]{:S(2)}, u32[]{:S(2)}) collective-permute-start(bf16[2,64,512]{2,1,0:T(8,128)(2,1)S(1)} %get-tuple-element.85), channel_id=1, source_target_pairs={{0,5},{1,4},{2,7},{3,6},{4,1},{5,0},{6,3},{7,2},{8,13},{9,12},{10,... | collective-permute-start | bytes 393224 | tf_op jit(solution)/shard_map/ppermute | solution.py:64
  12.5 25.9 %copy-start.1 = (f32[4096,128]{1,0:T(8,128)S(1)}, f32[4096,128]{1,0:T(8,128)}, u32[]{:S(2)}) copy-start(f32[4096,128]{1,0:T(8,128)} %res_ref.3) | copy-start | bytes 6291460
  12.5 25.9 %copy-start = (bf16[4096,512]{1,0:T(8,128)(2,1)S(1)}, bf16[4096,512]{1,0:T(8,128)(2,1)}, u32[]{:S(2)}) copy-start(bf16[4096,512]{1,0:T(8,128)(2,1)} %feat_ref.3) | copy-start | bytes 12582916
  15.8 5.5 %collective-permute-start.4 = (bf16[2,64,512]{2,1,0:T(8,128)(2,1)S(1)}, bf16[2,64,512]{2,1,0:T(8,128)(2,1)S(1)}, u32[]{:S(2)}, u32[]{:S(2)}) collective-permute-start(bf16[2,64,512]{2,1,0:T(8,128)(2,1)S(1)} %fusion.5), channel_id=1, source_target_pairs={{0,8},{1,9},{2,18},{3,19},{4,12},{5,13},{6,22},{7,23},{8,0},{9,1},... | collective-permute-start | bytes 393224 | tf_op jit(solution)/shard_map/ppermute | solution.py:64
  21.4 5.9 %collective-permute-start.5 = (bf16[2,64,512]{2,1,0:T(8,128)(2,1)S(1)}, bf16[2,64,512]{2,1,0:T(8,128)(2,1)S(1)}, u32[]{:S(2)}, u32[]{:S(2)}) collective-permute-start(bf16[2,64,512]{2,1,0:T(8,128)(2,1)S(1)} %broadcast_select_fusion.9), channel_id=1, source_target_pairs={{0,16},{1,17},{2,10},{3,11},{4,20},{5,21},{6,14},{7,15},{8,24},{9,... | collective-permute-start | bytes 393224 | tf_op jit(solution)/shard_map/ppermute | solution.py:64
  27.5 5.6 %collective-permute-start.8 = (bf16[2,64,512]{2,1,0:T(8,128)(2,1)S(1)}, bf16[2,64,512]{2,1,0:T(8,128)(2,1)S(1)}, u32[]{:S(2)}, u32[]{:S(2)}) collective-permute-start(bf16[2,64,512]{2,1,0:T(8,128)(2,1)S(1)} %broadcast_select_fusion.10), channel_id=1, source_target_pairs={{0,1},{1,0},{2,3},{3,2},{4,5},{5,4},{6,7},{7,6},{8,9},{9,8},{10,11... | collective-permute-start | bytes 393224 | tf_op jit(solution)/shard_map/ppermute | solution.py:64
  28.7 5.6 %collective-permute-start.7 = (bf16[2,64,512]{2,1,0:T(8,128)(2,1)S(1)}, bf16[2,64,512]{2,1,0:T(8,128)(2,1)S(1)}, u32[]{:S(2)}, u32[]{:S(2)}) collective-permute-start(bf16[2,64,512]{2,1,0:T(8,128)(2,1)S(1)} %broadcast_select_fusion.10), channel_id=1, source_target_pairs={{0,4},{1,5},{2,6},{3,7},{4,0},{5,1},{6,2},{7,3},{8,12},{9,13},{10,... | collective-permute-start | bytes 393224 | tf_op jit(solution)/shard_map/ppermute | solution.py:64
  30.3 5.9 %collective-permute-start.6 = (bf16[2,64,512]{2,1,0:T(8,128)(2,1)S(1)}, bf16[2,64,512]{2,1,0:T(8,128)(2,1)S(1)}, u32[]{:S(2)}, u32[]{:S(2)}) collective-permute-start(bf16[2,64,512]{2,1,0:T(8,128)(2,1)S(1)} %broadcast_select_fusion.10), channel_id=1, source_target_pairs={{0,5},{1,4},{2,7},{3,6},{4,1},{5,0},{6,3},{7,2},{8,13},{9,12},{10,... | collective-permute-start | bytes 393224 | tf_op jit(solution)/shard_map/ppermute | solution.py:64
  36.2 2.0 %collective-permute-start.9 = (bf16[2,4,64,512]{3,2,1,0:T(8,128)(2,1)S(1)}, bf16[2,4,64,512]{3,2,1,0:T(8,128)(2,1)S(1)}, u32[]{:S(2)}, u32[]{:S(2)}) collective-permute-start(bf16[2,4,64,512]{3,2,1,0:T(8,128)(2,1)S(1)} %pad_maximum_fusion.2), channel_id=1, source_target_pairs={{0,2},{1,3},{2,0},{3,1},{4,6},{5,7},{6,4},{7,5},{8,10},{9,11},{10,... | collective-permute-start | bytes 1572872 | tf_op jit(solution)/shard_map/ppermute | solution.py:64
  38.4 1.6 %copy-start.2 = (f32[4096,128]{1,0:T(8,128)S(1)}, f32[4096,128]{1,0:T(8,128)}, u32[]{:S(2)}) copy-start(f32[4096,128]{1,0:T(8,128)} %coef_ref.3) | copy-start | bytes 6291460
  50.1 2.0 %collective-permute-start.10 = (bf16[2,2,128,512]{3,2,1,0:T(8,128)(2,1)S(1)}, bf16[2,2,128,512]{3,2,1,0:T(8,128)(2,1)S(1)}, u32[]{:S(2)}, u32[]{:S(2)}) collective-permute-start(bf16[2,2,128,512]{3,2,1,0:T(8,128)(2,1)S(1)} %get-tuple-element.66), channel_id=1, source_target_pairs={{0,2},{1,3},{2,0},{3,1},{4,6},{5,7},{6,4},{7,5},{8,10},{9,11},{10,... | collective-permute-start | bytes 1572872 | tf_op jit(solution)/shard_map/ppermute | solution.py:64
  51.0 5.2 %copy-start.3 = (f32[4096,128]{1,0:T(8,128)S(1)}, f32[4096,128]{1,0:T(8,128)}, u32[]{:S(2)}) copy-start(f32[4096,128]{1,0:T(8,128)} %coef_ref.3) | copy-start | bytes 6291460
  52.7 9.3 %collective-permute-start.13 = (bf16[128,512]{1,0:T(8,128)(2,1)S(1)}, bf16[128,512]{1,0:T(8,128)(2,1)S(1)}, u32[]{:S(2)}, u32[]{:S(2)}) collective-permute-start(bf16[128,512]{1,0:T(8,128)(2,1)S(1)} %get-tuple-element.76), channel_id=1, source_target_pairs={{0,5},{1,4},{2,7},{3,6},{4,1},{5,0},{6,3},{7,2},{8,13},{9,12},{10,... | collective-permute-start | bytes 393224 | tf_op jit(solution)/shard_map/ppermute | solution.py:64
  53.5 8.5 %collective-permute-start.12 = (bf16[128,512]{1,0:T(8,128)(2,1)S(1)}, bf16[128,512]{1,0:T(8,128)(2,1)S(1)}, u32[]{:S(2)}, u32[]{:S(2)}) collective-permute-start(bf16[128,512]{1,0:T(8,128)(2,1)S(1)} %get-tuple-element.77), channel_id=1, source_target_pairs={{0,4},{1,5},{2,6},{3,7},{4,0},{5,1},{6,2},{7,3},{8,12},{9,13},{10,... | collective-permute-start | bytes 393224 | tf_op jit(solution)/shard_map/ppermute | solution.py:64
  54.7 7.3 %collective-permute-start.11 = (bf16[128,512]{1,0:T(8,128)(2,1)S(1)}, bf16[128,512]{1,0:T(8,128)(2,1)S(1)}, u32[]{:S(2)}, u32[]{:S(2)}) collective-permute-start(bf16[128,512]{1,0:T(8,128)(2,1)S(1)} %get-tuple-element.78), channel_id=1, source_target_pairs={{0,1},{1,0},{2,3},{3,2},{4,5},{5,4},{6,7},{7,6},{8,9},{9,8},{10,11... | collective-permute-start | bytes 393224 | tf_op jit(solution)/shard_map/ppermute | solution.py:64
  62.4 18.0 %collective-permute-start.16 = (bf16[128,512]{1,0:T(8,128)(2,1)S(1)}, bf16[128,512]{1,0:T(8,128)(2,1)S(1)}, u32[]{:S(2)}, u32[]{:S(2)}) collective-permute-start(bf16[128,512]{1,0:T(8,128)(2,1)S(1)} %pad_maximum_fusion.5), channel_id=1, source_target_pairs={{0,24},{1,25},{2,26},{3,27},{4,28},{5,29},{6,30},{7,31},{8,16},{9,... | collective-permute-start | bytes 393224 | tf_op jit(solution)/shard_map/ppermute | solution.py:64
  67.6 12.7 %collective-permute-start.15 = (bf16[128,512]{1,0:T(8,128)(2,1)S(1)}, bf16[128,512]{1,0:T(8,128)(2,1)S(1)}, u32[]{:S(2)}, u32[]{:S(2)}) collective-permute-start(bf16[128,512]{1,0:T(8,128)(2,1)S(1)} %pad_maximum_fusion.5), channel_id=1, source_target_pairs={{0,16},{1,17},{2,18},{3,19},{4,20},{5,21},{6,22},{7,23},{8,24},{9,... | collective-permute-start | bytes 393224 | tf_op jit(solution)/shard_map/ppermute | solution.py:64
  67.6 12.8 %collective-permute-start.14 = (bf16[128,512]{1,0:T(8,128)(2,1)S(1)}, bf16[128,512]{1,0:T(8,128)(2,1)S(1)}, u32[]{:S(2)}, u32[]{:S(2)}) collective-permute-start(bf16[128,512]{1,0:T(8,128)(2,1)S(1)} %pad_maximum_fusion.5), channel_id=1, source_target_pairs={{0,8},{1,9},{2,10},{3,11},{4,12},{5,13},{6,14},{7,15},{8,0},{9,1},... | collective-permute-start | bytes 393224 | tf_op jit(solution)/shard_map/ppermute | solution.py:64
  74.1 16.6 %collective-permute-start.21 = (f32[256,512]{1,0:T(8,128)S(1)}, f32[256,512]{1,0:T(8,128)S(1)}, u32[]{:S(2)}, u32[]{:S(2)}) collective-permute-start(f32[256,512]{1,0:T(8,128)S(1)} %get-tuple-element.38.refs_2_), channel_id=1, source_target_pairs={{0,2},{1,3},{2,0},{3,1},{4,6},{5,7},{6,4},{7,5},{8,10},{9,11},{10,... | collective-permute-start | bytes 1572872 | tf_op jit(solution)/shard_map/ppermute | solution.py:64
  74.2 16.5 %collective-permute-start.22 = (f32[256,512]{1,0:T(8,128)S(1)}, f32[256,512]{1,0:T(8,128)S(1)}, u32[]{:S(2)}, u32[]{:S(2)}) collective-permute-start(f32[256,512]{1,0:T(8,128)S(1)} %get-tuple-element.40.refs_2_), channel_id=1, source_target_pairs={{0,2},{1,3},{2,0},{3,1},{4,6},{5,7},{6,4},{7,5},{8,10},{9,11},{10,... | collective-permute-start | bytes 1572872 | tf_op jit(solution)/shard_map/ppermute | solution.py:64
  80.7 9.0 %collective-permute-start.19 = (bf16[128,512]{1,0:T(8,128)(2,1)S(1)}, bf16[128,512]{1,0:T(8,128)(2,1)S(1)}, u32[]{:S(2)}, u32[]{:S(2)}) collective-permute-start(bf16[128,512]{1,0:T(8,128)(2,1)S(1)} %pad_maximum_fusion.6), channel_id=1, source_target_pairs={{0,5},{1,4},{2,7},{3,6},{4,1},{5,0},{6,3},{7,2},{8,13},{9,12},{10,... | collective-permute-start | bytes 393224 | tf_op jit(solution)/shard_map/ppermute | solution.py:64
  81.3 8.5 %collective-permute-start.18 = (bf16[128,512]{1,0:T(8,128)(2,1)S(1)}, bf16[128,512]{1,0:T(8,128)(2,1)S(1)}, u32[]{:S(2)}, u32[]{:S(2)}) collective-permute-start(bf16[128,512]{1,0:T(8,128)(2,1)S(1)} %pad_maximum_fusion.6), channel_id=1, source_target_pairs={{0,4},{1,5},{2,6},{3,7},{4,0},{5,1},{6,2},{7,3},{8,12},{9,13},{10,... | collective-permute-start | bytes 393224 | tf_op jit(solution)/shard_map/ppermute | solution.py:64
  82.8 7.0 %collective-permute-start.17 = (bf16[128,512]{1,0:T(8,128)(2,1)S(1)}, bf16[128,512]{1,0:T(8,128)(2,1)S(1)}, u32[]{:S(2)}, u32[]{:S(2)}) collective-permute-start(bf16[128,512]{1,0:T(8,128)(2,1)S(1)} %pad_maximum_fusion.6), channel_id=1, source_target_pairs={{0,1},{1,0},{2,3},{3,2},{4,5},{5,4},{6,7},{7,6},{8,9},{9,8},{10,11... | collective-permute-start | bytes 393224 | tf_op jit(solution)/shard_map/ppermute | solution.py:64
  89.7 2.0 %collective-permute-start.23 = (f32[256,512]{1,0:T(8,128)S(1)}, f32[256,512]{1,0:T(8,128)S(1)}, u32[]{:S(2)}, u32[]{:S(2)}) collective-permute-start(f32[256,512]{1,0:T(8,128)S(1)} %get-tuple-element.47.refs_2_), channel_id=1, source_target_pairs={{0,2},{1,3},{2,0},{3,1},{4,6},{5,7},{6,4},{7,5},{8,10},{9,11},{10,... | collective-permute-start | bytes 1572872 | tf_op jit(solution)/shard_map/ppermute | solution.py:64
  90.0 2.4 %collective-permute-start.20 = (bf16[2,2,128,512]{3,2,1,0:T(8,128)(2,1)S(1)}, bf16[2,2,128,512]{3,2,1,0:T(8,128)(2,1)S(1)}, u32[]{:S(2)}, u32[]{:S(2)}) collective-permute-start(bf16[2,2,128,512]{3,2,1,0:T(8,128)(2,1)S(1)} %bitcast.75), channel_id=1, source_target_pairs={{0,2},{1,3},{2,0},{3,1},{4,6},{5,7},{6,4},{7,5},{8,10},{9,11},{10,... | collective-permute-start | bytes 1572872 | tf_op jit(solution)/shard_map/ppermute | solution.py:64
  90.6 2.6 %collective-permute-start.24 = (f32[256,512]{1,0:T(8,128)S(1)}, f32[256,512]{1,0:T(8,128)S(1)}, u32[]{:S(2)}, u32[]{:S(2)}) collective-permute-start(f32[256,512]{1,0:T(8,128)S(1)} %factor.7), channel_id=1, source_target_pairs={{0,2},{1,3},{2,0},{3,1},{4,6},{5,7},{6,4},{7,5},{8,10},{9,11},{10,... | collective-permute-start | bytes 1572872 | tf_op jit(solution)/shard_map/ppermute | solution.py:64
  90.9 2.4 %copy-start.4 = (s32[2,4]{1,0:T(2,128)S(1)}, s32[2,4]{1,0:T(2,128)}, u32[]{:S(2)}) copy-start(s32[2,4]{1,0:T(2,128)} %tiles_ref.3) | copy-start | bytes 100

commit v3 on v2

--- a/solution.py
+++ b/solution.py
@@ -80,12 +80,11 @@
     return jnp.stack([jnp.where(two, parts[c ^ 2], parts[c]) for c in range(4)], axis=axis)
 
 
-def fetch_blocks(features, norms, block_owner, block_tiles, me, devices, core):
+def fetch_blocks(features, prepared, block_owner, block_tiles, me, devices, core):
     width = features.shape[1]
     low, high = 1, 2 * core
     differs = lambda mask: (((block_owner ^ me) & mask) != 0)[:, None, None]
     on_core = (me & core) != 0
-
     keep, send = pick_halves(features, block_tiles, bit_of(me, core).reshape(1))
     half = jnp.where(differs(core), swap(send, AXES, core), keep)
     quarters = half.reshape(STEPS, 4, BLOCK // 8, width)
@@ -107,13 +106,18 @@
     for hop, (flip, mask) in enumerate(hops):
         other = swap(part, AXES, flip)
         if hop == len(hops) - 2:
-            other, norms = lax.optimization_barrier((other, norms))
+            other, prepared = lax.optimization_barrier((other, prepared))
         part = jnp.where(differs(mask), other, part)
     _, got = swap_among(lambda place: part, me, AXES, low, high)
     half = ordered([part] + got, me, low, high, 1)
-    other = swap(half, AXES, core)
+    half = half.reshape(BLOCK, width)
+    return half, swap(half, AXES, core), prepared
+
+
+def both_halves(half, other, on_core):
+    half, other = (value.reshape(STEPS, BLOCK // 2, value.shape[1]) for value in (half, other))
     both = jnp.stack([jnp.where(on_core, other, half), jnp.where(on_core, half, other)], axis=1)
-    return both.reshape(STEPS * BLOCK, width), norms
+    return both.reshape(STEPS * BLOCK, half.shape[2])
 
 
 def pack(value, exact):
@@ -179,7 +183,7 @@
     return jnp.exp(dots * (2.0 * scale) - scaled_norm(left, scale) - row)
 
 
-def gram_kernel(scale, core_ref, block_ref, slab_ref, own_ref):
+def gram_kernel(scale, core_ref, block_ref, slab0_ref, slab1_ref, own_ref):
     mine = block_ref[pl.ds(pl.multiple_of(core_ref[0] * BLOCK, BLOCK), BLOCK), :]
     diagonal = lax.broadcasted_iota(jnp.int32, (BLOCK, BLOCK), 0) == lax.broadcasted_iota(jnp.int32, (BLOCK, BLOCK), 1)
     own_ref[...] = kernel_of(mine, mine, scale) + jnp.where(diagonal, RIDGE, 0.0)
@@ -189,30 +193,36 @@
     vmem = pl.BlockSpec(memory_space=pltpu.VMEM)
     return pl.pallas_call(
         functools.partial(gram_kernel, scale),
-        in_specs=[pl.BlockSpec(memory_space=pltpu.SMEM), vmem, vmem],
+        in_specs=[pl.BlockSpec(memory_space=pltpu.SMEM)] + [vmem] * 3,
         out_shape=jax.ShapeDtypeStruct((BLOCK, BLOCK), jnp.float32),
         compiler_params=pltpu.CompilerParams(vmem_limit_bytes=SMALL_LIMIT),
         cost_estimate=pl.CostEstimate(
             flops=2 * BLOCK**3, bytes_accessed=4 * BLOCK * BLOCK * 2, transcendentals=BLOCK**2
         ),
         name="gram",
-    )(core, block, in_vmem(slab))
-
-
-def slab_kernel(scale, chunk, block_ref, feat_ref, norm_ref, res_ref, coef_ref, slab_ref, piece_ref, bnorm, grad, cross, ahead_ref):
+    )(core, block, *map(in_vmem, slab))
+
+
+def slab_kernel(scale, chunk, *refs):
+    refs = list(refs)
+    ahead_ref, bnorm, grad = refs[-3], refs[-2], refs[-1]
+    second = len(refs) > 10
+    half_ref, feat_ref, norm_ref, res_ref, coef_ref = refs[:5]
+    if second:
+        core_ref, first_slab, first_grad, slab_ref, piece_ref, grads, cross = refs[5:12]
+        cross[...] = jnp.zeros_like(cross)
+    else:
+        slab_ref = refs[5]
     scale2 = scale * LOG2E
-    norm = scaled_norm(block_ref[...], scale2)
-    bnorm[...] = jnp.broadcast_to(norm, bnorm.shape)
+    part = BLOCK // 2
+    bnorm[...] = jnp.broadcast_to(scaled_norm(half_ref[...], scale2), bnorm.shape)
     grad[...] = jnp.zeros_like(grad)
-    cross[...] = jnp.zeros_like(cross)
-    part = BLOCK // 2
-    parts = STEPS * BLOCK // part
     chunks = feat_ref.shape[0] // chunk
     rows_of = lambda i: pl.ds(pl.multiple_of(i * chunk, chunk), chunk)
     at_of = lambda p: slice(p * part, (p + 1) * part)
 
     def product(i, p):
-        return lax.dot_general(block_ref[at_of(p)], feat_ref[rows_of(i), :], NT, preferred_element_type=jnp.float32)
+        return lax.dot_general(half_ref[at_of(p)], feat_ref[rows_of(i), :], NT, preferred_element_type=jnp.float32)
 
     ahead_ref[...] = product(0, 0)
 
@@ -221,60 +231,90 @@
         weighted = (res_ref[rows, :] - RIDGE * coef_ref[rows, :]).astype(jnp.bfloat16)
         norm_row = norm_ref[:, rows] * LOG2E
         dots = ahead_ref[...]
-        for p in range(parts):
-            ahead = product(i, p + 1) if p + 1 < parts else product(jnp.minimum(i + 1, chunks - 1), 0)
+        for p in range(STEPS):
+            ahead = product(i, p + 1) if p + 1 < STEPS else product(jnp.minimum(i + 1, chunks - 1), 0)
             norm_wide = jnp.concatenate([bnorm[at_of(p)]] * (chunk // bnorm.shape[1]), axis=1)
             slab = jnp.exp2(dots * (2.0 * scale2) - norm_wide - norm_row).astype(jnp.bfloat16)
             slab_ref[at_of(p), rows] = slab
-            if p < parts // 2:
-                grad[at_of(p)] += jnp.dot(slab, weighted, preferred_element_type=jnp.float32)
+            if p == 0:
+                grad[...] += jnp.dot(slab, weighted, preferred_element_type=jnp.float32)
             dots = ahead
         ahead_ref[...] = dots
-        left = jnp.concatenate([slab_ref[:BLOCK, rows], jnp.transpose(weighted)], axis=0)
-        cross[...] += lax.dot_general(left, slab_ref[BLOCK:, rows], NT, preferred_element_type=jnp.float32)
+        if second:
+            left = [first_slab[at_of(0), rows], slab_ref[at_of(0), rows], jnp.transpose(weighted)]
+            right = [first_slab[at_of(1), rows], slab_ref[at_of(1), rows]]
+            cross[...] += lax.dot_general(
+                jnp.concatenate(left, axis=0), jnp.concatenate(right, axis=0), NT, preferred_element_type=jnp.float32
+            )
         return 0
 
     lax.fori_loop(0, chunks, body, 0, unroll=2)
-    grads = jnp.concatenate([jnp.transpose(grad[...]), cross[BLOCK:]], axis=1)
+    if not second:
+        refs[6][...] = grad[...]
+        return
+    grads[:, at_of(0)] = jnp.transpose(first_grad[...])
+    grads[:, at_of(1)] = jnp.transpose(grad[...])
+    grads[:, BLOCK:] = cross[BLOCK:]
     groups = piece_ref.shape[0]
     own, depth = grads.shape[0] // groups, BLOCK // groups
     exact = STEPS * own
-    high = grads.astype(jnp.bfloat16)
-    low = (grads - high.astype(jnp.float32)).astype(jnp.bfloat16)
-    for d in range(groups):
+    place = lambda h: ((1 - core_ref[0]) if h else core_ref[0]) * part
+    lanes = lambda base, h: pl.ds(pl.multiple_of(base + place(h), part), part)
+    for h in range(2):
+        to = at_of(h)
         for s in range(STEPS):
-            there = (slice(d * own, (d + 1) * own), slice(s * BLOCK, (s + 1) * BLOCK))
-            piece_ref[d, s * own : (s + 1) * own] = high[there]
-            piece_ref[d, exact + s * own : exact + (s + 1) * own] = low[there]
-        piece_ref[d, 2 * exact :] = cross[d * depth : (d + 1) * depth].astype(jnp.bfloat16)
+            value = grads[:, lanes(s * BLOCK, h)]
+            high = value.astype(jnp.bfloat16)
+            low = (value - high.astype(jnp.float32)).astype(jnp.bfloat16)
+            for d in range(groups):
+                here = slice(d * own, (d + 1) * own)
+                piece_ref[d, s * own : (s + 1) * own, to] = high[here]
+                piece_ref[d, exact + s * own : exact + (s + 1) * own, to] = low[here]
+        for d in range(groups):
+            row = place(d * depth // part) + d * depth % part
+            value = cross[pl.ds(pl.multiple_of(row, depth), depth), lanes(0, h)]
+            piece_ref[d, 2 * exact :, to] = value.astype(jnp.bfloat16)
 
 
 def in_vmem(value):
     return pltpu.with_memory_space_constraint(value, pltpu.VMEM)
 
 
-def slabs(block, features, norms, residual, coefficients, scale, groups, chunk=512):
+def slabs(half, features, norms, residual, coefficients, scale, groups=0, core=None, first=(), chunk=512):
     rows, width = features.shape
     targets = residual.shape[1]
-    both = STEPS * BLOCK
-    piece = (groups, 2 * STEPS * targets // groups + BLOCK // groups, BLOCK)
+    vmem = pl.BlockSpec(memory_space=pltpu.VMEM)
+    slab = pltpu.VMEM((BLOCK, rows), jnp.bfloat16)
+    inputs = [half, in_vmem(features), norms, in_vmem(residual), in_vmem(coefficients)]
+    in_specs = [vmem] * 5
+    scratch = [
+        pltpu.VMEM((BLOCK // 2, chunk), jnp.float32),
+        pltpu.VMEM((BLOCK, 128), jnp.float32),
+        pltpu.VMEM((BLOCK // 2, targets), jnp.float32),
+    ]
+    out = jax.ShapeDtypeStruct((BLOCK // 2, targets), jnp.float32)
+    if first:
+        piece = (groups, 2 * STEPS * targets // groups + BLOCK // groups, BLOCK)
+        out = jax.ShapeDtypeStruct(piece, jnp.bfloat16)
+        inputs += [core, in_vmem(first[0]), first[1]]
+        in_specs += [pl.BlockSpec(memory_space=pltpu.SMEM), vmem, vmem]
+        scratch = [
+            pltpu.VMEM((targets, STEPS * BLOCK), jnp.float32),
+            pltpu.VMEM((BLOCK + targets, BLOCK), jnp.float32),
+        ] + scratch
     return pl.pallas_call(
         functools.partial(slab_kernel, scale, chunk),
-        out_shape=(pltpu.VMEM((both, rows), jnp.bfloat16), jax.ShapeDtypeStruct(piece, jnp.bfloat16)),
-        scratch_shapes=[
-            pltpu.VMEM((both, 128), jnp.float32),
-            pltpu.VMEM((BLOCK, targets), jnp.float32),
-            pltpu.VMEM((BLOCK + targets, BLOCK), jnp.float32),
-            pltpu.VMEM((BLOCK // 2, chunk), jnp.float32),
-        ],
+        in_specs=in_specs,
+        out_shape=(slab, out),
+        scratch_shapes=scratch,
         compiler_params=pltpu.CompilerParams(vmem_limit_bytes=VMEM_LIMIT),
         cost_estimate=pl.CostEstimate(
-            flops=2 * rows * both * (width + targets + BLOCK // 2),
-            bytes_accessed=rows * (width * 2 + targets * 8 + both * 2),
-            transcendentals=rows * both,
+            flops=2 * rows * BLOCK * (width + targets + (BLOCK if first else 0)),
+            bytes_accessed=rows * (width * 2 + targets * 8 + BLOCK * 2),
+            transcendentals=rows * BLOCK,
         ),
         name="slabs",
-    )(block, in_vmem(features), norms, in_vmem(residual), in_vmem(coefficients))
+    )(*inputs)
 
 
 def eliminate(tiles, t, lane, scaled_ref, waiting):
@@ -325,7 +365,7 @@
 
 def factor_kernel(index, copied, scale, *refs):
     refs = list(refs)
-    rest_ref, _ = refs.pop(0), refs.pop(0)
+    rest_ref, _, _ = refs.pop(0), refs.pop(0), refs.pop(0)
     before_ref = refs.pop(0) if index else None
     scaled = refs.pop()
     if copied:
@@ -375,7 +415,7 @@
     left = BLOCK - (index + 1) * TILE
     vmem, hbm = pl.BlockSpec(memory_space=pltpu.VMEM), pl.BlockSpec(memory_space=pltpu.HBM)
     out = [jax.ShapeDtypeStruct((2 * TILE, BLOCK), jnp.float32)]
-    inputs, scratch = [rest, in_vmem(slab)], [pltpu.VMEM((TILE, TILE), jnp.float32)]
+    inputs, scratch = [rest, *map(in_vmem, slab)], [pltpu.VMEM((TILE, TILE), jnp.float32)]
     if index:
         inputs.append(before)
         if left:
@@ -417,7 +457,7 @@
     return jnp.concatenate(out, axis=1)
 
 
-def final_kernel(step_size, chunk, owner_ref, tiles_ref, me_ref, packed_ref, gram_ref, slab_ref, res_ref, coef_ref, base_ref, *refs):
+def final_kernel(step_size, chunk, owner_ref, tiles_ref, me_ref, core_ref, packed_ref, gram_ref, slab0_ref, slab1_ref, res_ref, coef_ref, base_ref, *refs):
     factors, refs = refs[: 2 * (BLOCK // TILE)], refs[2 * (BLOCK // TILE) :]
     res_out, coef_out, upd_ref, wide_ref, part_ref, ahead_ref, res_buf, tile_buf, res_sems, tile_sems = refs
     rows, targets = res_ref.shape
@@ -434,9 +474,13 @@
     first = apply_inverse(gradient(0), factors[:count]) * step_size
     high = first.astype(jnp.bfloat16)
     low = (first - high.astype(jnp.float32)).astype(jnp.bfloat16)
+    half = BLOCK // 2
+    upd_ref[...] = high
+    mine, theirs = (pl.ds(pl.multiple_of(c * half, half), half) for c in (core_ref[0], 1 - core_ref[0]))
+    mine_high, theirs_high = upd_ref[:, mine], upd_ref[:, theirs]
     for i in range(rows // chunk):
         at = slice(i * chunk, (i + 1) * chunk)
-        part_ref[:, at] = dot(high, slab_ref[:BLOCK, at])
+        part_ref[:, at] = dot(mine_high, slab0_ref[:half, at]) + dot(theirs_high, slab1_ref[:half, at])
     cross = packed_ref[:, 2 * exact :].reshape(BLOCK, BLOCK)
     block_part = dot(high, gram_ref[...]) + dot(low, gram_ref[...])
     again = gradient(1) - dot(high, cross) - RIDGE * block_part
@@ -486,8 +530,8 @@
         return pltpu.make_async_copy(res_buf.at[rows_of(i), :], res_out.at[rows_of(i), :], res_sems.at[i])
 
     def product(i):
-        change = jnp.dot(upd_ref[...], slab_ref[BLOCK:, rows_of(i)], preferred_element_type=jnp.float32)
-        return part_ref[:, rows_of(i)] + change
+        change = dot(upd_ref[:, mine], slab0_ref[half:, rows_of(i)])
+        return part_ref[:, rows_of(i)] + change + dot(upd_ref[:, theirs], slab1_ref[half:, rows_of(i)])
 
     ahead_ref[...] = product(0)
 
@@ -510,14 +554,14 @@
                 tile_copy(s, k).wait()
 
 
-def finish(owner, tiles, me, packed, gram12, slab, residual, coefficients, base, factors, step_size, chunk=512):
+def finish(owner, tiles, me, core, packed, gram12, slab, residual, coefficients, base, factors, step_size, chunk=512):
     rows, targets = residual.shape
     both = STEPS * BLOCK
     count = BLOCK // TILE
     smem, vmem, hbm = (pl.BlockSpec(memory_space=space) for space in (pltpu.SMEM, pltpu.VMEM, pltpu.HBM))
     return pl.pallas_call(
         functools.partial(final_kernel, step_size, chunk),
-        in_specs=[smem] * 3 + [vmem] * 5 + [hbm] + [vmem] * len(factors),
+        in_specs=[smem] * 4 + [vmem] * 6 + [hbm] + [vmem] * len(factors),
         out_specs=(hbm, hbm),
         out_shape=(
             pltpu.HBM(residual.shape, jnp.float32),
@@ -533,13 +577,13 @@
             pltpu.SemaphoreType.DMA((rows // chunk,)),
             pltpu.SemaphoreType.DMA((STEPS, count)),
         ],
-        input_output_aliases={8: 1},
+        input_output_aliases={10: 1},
         compiler_params=pltpu.CompilerParams(vmem_limit_bytes=VMEM_LIMIT),
         cost_estimate=pl.CostEstimate(
             flops=2 * rows * both * targets, bytes_accessed=rows * (both * 2 + targets * 16), transcendentals=0
         ),
         name="finish",
-    )(owner, tiles, me, packed, gram12, in_vmem(slab), in_vmem(residual), in_vmem(coefficients), base, *factors)
+    )(owner, tiles, me, core, packed, gram12, *map(in_vmem, slab), in_vmem(residual), in_vmem(coefficients), base, *factors)
 
 
 def local(features, residual, coefficients, block_owner, block_tiles):
@@ -556,13 +600,17 @@
 
     wide = features.astype(jnp.float32)
     norms = (jnp.sum(wide * wide, axis=1) * scale).reshape(1, rows_dev)
-    block, norms = fetch_blocks(features, norms, block_owner, block_tiles, me, devices, sub_count)
-    slab, pieces = slabs(block, features, norms, residual, coefficients, scale, groups)
+    half, other, norms = fetch_blocks(features, norms, block_owner, block_tiles, me, devices, sub_count)
+    core, on_core = bit_of(me, sub_count).reshape(1), (me & sub_count) != 0
+    first = slabs(half, features, norms, residual, coefficients, scale)
+    other, first = lax.optimization_barrier((other, first))
+    last = slabs(other, features, norms, residual, coefficients, scale, groups, core, first)
+    slab, pieces = (first[0], last[0]), last[1]
+    block = both_halves(half, other, on_core)
     exact = STEPS * own
     if spread.axes != AXES:
         pieces = pack(lax.psum(unpack(pieces, exact), "sub"), exact)
-    core, on_core = bit_of(me, sub_count), (me & sub_count) != 0
-    rest = gram(block, core.reshape(1), scale, slab)
+    rest = gram(block, core, scale, slab)
     factors, before, extra = ([], []), None, []
 
     def beside(hop, indices):
@@ -588,7 +636,7 @@
     base, gram12 = extra
     packed = spread.core_gather(packed)
     return finish(
-        block_owner, block_tiles, me.reshape(1), packed, gram12, slab, residual, coefficients, base,
+        block_owner, block_tiles, me.reshape(1), core, packed, gram12, slab, residual, coefficients, base,
         factors[0] + factors[1], step_size,
     )
 

time: 101 us -> 103 us (1.020)
  waiting for transfers between devices: 21.8 us -> 19.5 us
  local copies, waits for them, and re-layouts: 1.9 us -> 4.08 us
  Pallas kernels: 42.6 us -> 44 us
    ppermute x25, waiting for transfers between devices: 21.8 us -> 19.5 us  [swap(): lax.ppermute(value, axes, [(i, i ^ flip_of(i)) for i in range(lax.axis_si...]
    unnamed x12 -> x14, local copies, waits for them, and re-layouts: 1.62 us -> 3.8 us
    pallas_call x1 -> x2, Pallas kernels: 9.97 us -> 11.3 us  [slabs(): pl.pallas_call(functools.partial(slab_kernel, scale, chunk), in_specs=in_...]
  transfers between devices with their start and end apart: 25 -> 25, of which waited for: 13 -> 12; matrix products, arithmetic and copies ran while one was open for 4% -> 4% of each run, Pallas kernels for 23% -> 27%
where the time goes in v3:
time: 103 us; the launch traced here: 102 us
  Pallas kernels  44 us (43%)
  starting transfers between devices  28 us (27%)
  waiting for transfers between devices  19.5 us (19%)
  other arithmetic  5.42 us (5%)
  local copies, waits for them, and re-layouts  4.08 us (4%)
  between operations  1.47 us (1%)
    ppermute x25, starting transfers between devices, swap(): lax.ppermute(value, axes, [(i, i ^ flip_of(i)) for i in range(lax.axis_si...  28 us
    pallas_call x4, Pallas kernels, factor_step(): pl.pallas_call(functools.partial(factor_kernel, index, copied is not None...  22.7 us
    ppermute x25, waiting for transfers between devices, swap(): lax.ppermute(value, axes, [(i, i ^ flip_of(i)) for i in range(lax.axis_si...  19.5 us
    pallas_call x2, Pallas kernels, slabs(): pl.pallas_call(functools.partial(slab_kernel, scale, chunk), in_specs=in_...  11.3 us
    pallas_call x1, Pallas kernels, finish(): pl.pallas_call(functools.partial(final_kernel, step_size, chunk), in_spec...  7.37 us
    unnamed x14, local copies, waits for them, and re-layouts  3.8 us
    reduce_sum x1, other arithmetic, local(): norms = (jnp.sum(wide * wide, axis=1) * scale).reshape(1, rows_dev)  3.08 us
  transfers between devices with their start and end apart: 25, of which 12 were waited for; matrix products, arithmetic and copies ran while one was open for 4% of the time, Pallas kernels for 27%

profile of v3, /device:TPU:0, one launch (start us, length us, event | category | flops | bytes accessed | tf_op | source)
XLA Modules:
  0.0 102.5 jit_solution(1077079451707709373)
XLA Ops:
  0.6 2.0 %pick.1 = (bf16[2,256,512]{2,1,0:T(8,128)(2,1)S(1)}, bf16[2,256,512]{2,1,0:T(8,128)(2,1)S(1)}) custom-call(s32[2,4]{1,0:T(2,128)} %tiles_ref.3, s32[1]{0:T(128)} %bitcast.1.core_ref.refs_5_, bf16[4096,512]{1,0:T(8,128)(2,1)} %refs_1_.3), custom_call_target="tpu_custom_call" | custom-call | tf_op jit(solution)/shard_map/pick/pallas_call | solution.py:47
  3.3 1.5 %collective-permute-done = bf16[2,256,512]{2,1,0:T(8,128)(2,1)S(1)} collective-permute-done((bf16[2,256,512]{2,1,0:T(8,128)(2,1)S(1)}, bf16[2,256,512]{2,1,0:T(8,128)(2,1)S(1)}, u32[]{:S(2)}, u32[]{:S(2)}) %collective-permute-start) | collective-permute-done | bytes 524320 | tf_op jit(solution)/shard_map/ppermute | solution.py:64
  4.9 3.0 %collective-permute-start.2 = (bf16[2,64,512]{2,1,0:T(8,128)(2,1)S(1)}, bf16[2,64,512]{2,1,0:T(8,128)(2,1)S(1)}, u32[]{:S(2)}, u32[]{:S(2)}) collective-permute-start(bf16[2,64,512]{2,1,0:T(8,128)(2,1)S(1)} %get-tuple-element.93), channel_id=1, source_target_pairs={{0,4},{1,5},{2,6},{3,7},{4,0},{5,1},{6,2},{7,3},{8,12},{9,13},{10,... | collective-permute-start | bytes 393224 | tf_op jit(solution)/shard_map/ppermute | solution.py:64
  7.9 1.5 %collective-permute-start.3 = (bf16[2,64,512]{2,1,0:T(8,128)(2,1)S(1)}, bf16[2,64,512]{2,1,0:T(8,128)(2,1)S(1)}, u32[]{:S(2)}, u32[]{:S(2)}) collective-permute-start(bf16[2,64,512]{2,1,0:T(8,128)(2,1)S(1)} %get-tuple-element.94), channel_id=1, source_target_pairs={{0,1},{1,0},{2,3},{3,2},{4,5},{5,4},{6,7},{7,6},{8,9},{9,8},{10,11... | collective-permute-start | bytes 393224 | tf_op jit(solution)/shard_map/ppermute | solution.py:64
  9.4 3.1 %multiply_reduce_fusion = f32[4096]{0:T(1024)S(1)} fusion(bf16[4096,512]{1,0:T(8,128)(2,1)} %refs_1_.3), kind=kLoop, calls=%fused_computation | loop fusion | flops 6287360 | bytes 4210688 | tf_op jit(solution)/shard_map/reduce_sum | solution.py:602
  12.5 1.7 %collective-permute-done.3 = bf16[2,64,512]{2,1,0:T(8,128)(2,1)S(1)} collective-permute-done((bf16[2,64,512]{2,1,0:T(8,128)(2,1)S(1)}, bf16[2,64,512]{2,1,0:T(8,128)(2,1)S(1)}, u32[]{:S(2)}, u32[]{:S(2)}) %collective-permute-start.3) | collective-permute-done | bytes 131104 | tf_op jit(solution)/shard_map/ppermute | solution.py:64
  14.3 1.5 %collective-permute-done.1 = bf16[2,64,512]{2,1,0:T(8,128)(2,1)S(1)} collective-permute-done((bf16[2,64,512]{2,1,0:T(8,128)(2,1)S(1)}, bf16[2,64,512]{2,1,0:T(8,128)(2,1)S(1)}, u32[]{:S(2)}, u32[]{:S(2)}) %collective-permute-start.1) | collective-permute-done | bytes 131104 | tf_op jit(solution)/shard_map/ppermute | solution.py:64
  15.8 1.8 %collective-permute-start.4 = (bf16[2,64,512]{2,1,0:T(8,128)(2,1)S(1)}, bf16[2,64,512]{2,1,0:T(8,128)(2,1)S(1)}, u32[]{:S(2)}, u32[]{:S(2)}) collective-permute-start(bf16[2,64,512]{2,1,0:T(8,128)(2,1)S(1)} %fusion.5), channel_id=1, source_target_pairs={{0,8},{1,9},{2,18},{3,19},{4,12},{5,13},{6,22},{7,23},{8,0},{9,1},... | collective-permute-start | bytes 393224 | tf_op jit(solution)/shard_map/ppermute | solution.py:64
  17.6 3.7 %collective-permute-done.4 = bf16[2,64,512]{2,1,0:T(8,128)(2,1)S(1)} collective-permute-done((bf16[2,64,512]{2,1,0:T(8,128)(2,1)S(1)}, bf16[2,64,512]{2,1,0:T(8,128)(2,1)S(1)}, u32[]{:S(2)}, u32[]{:S(2)}) %collective-permute-start.4) | collective-permute-done | bytes 131104 | tf_op jit(solution)/shard_map/ppermute | solution.py:64
  21.5 2.7 %collective-permute-start.5 = (bf16[2,64,512]{2,1,0:T(8,128)(2,1)S(1)}, bf16[2,64,512]{2,1,0:T(8,128)(2,1)S(1)}, u32[]{:S(2)}, u32[]{:S(2)}) collective-permute-start(bf16[2,64,512]{2,1,0:T(8,128)(2,1)S(1)} %broadcast_select_fusion.9), channel_id=1, source_target_pairs={{0,16},{1,17},{2,10},{3,11},{4,20},{5,21},{6,14},{7,15},{8,24},{9,... | collective-permute-start | bytes 393224 | tf_op jit(solution)/shard_map/ppermute | solution.py:64
  24.1 3.3 %collective-permute-done.5 = bf16[2,64,512]{2,1,0:T(8,128)(2,1)S(1)} collective-permute-done((bf16[2,64,512]{2,1,0:T(8,128)(2,1)S(1)}, bf16[2,64,512]{2,1,0:T(8,128)(2,1)S(1)}, u32[]{:S(2)}, u32[]{:S(2)}) %collective-permute-start.5) | collective-permute-done | bytes 131104 | tf_op jit(solution)/shard_map/ppermute | solution.py:64
  27.5 1.3 %collective-permute-start.8 = (bf16[2,64,512]{2,1,0:T(8,128)(2,1)S(1)}, bf16[2,64,512]{2,1,0:T(8,128)(2,1)S(1)}, u32[]{:S(2)}, u32[]{:S(2)}) collective-permute-start(bf16[2,64,512]{2,1,0:T(8,128)(2,1)S(1)} %broadcast_select_fusion.10), channel_id=1, source_target_pairs={{0,1},{1,0},{2,3},{3,2},{4,5},{5,4},{6,7},{7,6},{8,9},{9,8},{10,11... | collective-permute-start | bytes 393224 | tf_op jit(solution)/shard_map/ppermute | solution.py:64
  28.7 1.5 %collective-permute-start.7 = (bf16[2,64,512]{2,1,0:T(8,128)(2,1)S(1)}, bf16[2,64,512]{2,1,0:T(8,128)(2,1)S(1)}, u32[]{:S(2)}, u32[]{:S(2)}) collective-permute-start(bf16[2,64,512]{2,1,0:T(8,128)(2,1)S(1)} %broadcast_select_fusion.10), channel_id=1, source_target_pairs={{0,4},{1,5},{2,6},{3,7},{4,0},{5,1},{6,2},{7,3},{8,12},{9,13},{10,... | collective-permute-start | bytes 393224 | tf_op jit(solution)/shard_map/ppermute | solution.py:64
  31.0 2.1 %collective-permute-done.8 = bf16[2,64,512]{2,1,0:T(8,128)(2,1)S(1)} collective-permute-done((bf16[2,64,512]{2,1,0:T(8,128)(2,1)S(1)}, bf16[2,64,512]{2,1,0:T(8,128)(2,1)S(1)}, u32[]{:S(2)}, u32[]{:S(2)}) %collective-permute-start.8) | collective-permute-done | bytes 131104 | tf_op jit(solution)/shard_map/ppermute | solution.py:64
  33.1 1.3 %collective-permute-done.7 = bf16[2,64,512]{2,1,0:T(8,128)(2,1)S(1)} collective-permute-done((bf16[2,64,512]{2,1,0:T(8,128)(2,1)S(1)}, bf16[2,64,512]{2,1,0:T(8,128)(2,1)S(1)}, u32[]{:S(2)}, u32[]{:S(2)}) %collective-permute-start.7) | collective-permute-done | bytes 131104 | tf_op jit(solution)/shard_map/ppermute | solution.py:64
  34.4 1.8 %collective-permute-done.6 = bf16[2,64,512]{2,1,0:T(8,128)(2,1)S(1)} collective-permute-done((bf16[2,64,512]{2,1,0:T(8,128)(2,1)S(1)}, bf16[2,64,512]{2,1,0:T(8,128)(2,1)S(1)}, u32[]{:S(2)}, u32[]{:S(2)}) %collective-permute-start.6) | collective-permute-done | bytes 131104 | tf_op jit(solution)/shard_map/ppermute | solution.py:64
  36.4 2.2 %copy-done = bf16[4096,512]{1,0:T(8,128)(2,1)S(1)} copy-done((bf16[4096,512]{1,0:T(8,128)(2,1)S(1)}, bf16[4096,512]{1,0:T(8,128)(2,1)}, u32[]{:S(2)}) %copy-start) | copy-done | bytes 4194328
  38.5 1.6 %copy-done.3 = f32[4096,128]{1,0:T(8,128)S(1)} copy-done((f32[4096,128]{1,0:T(8,128)S(1)}, f32[4096,128]{1,0:T(8,128)}, u32[]{:S(2)}) %copy-start.3) | copy-done | bytes 2097176
  40.1 3.9 %slabs.2 = (bf16[512,4096]{1,0:T(8,128)(2,1)S(1)}, f32[256,128]{1,0:T(8,128)S(1)}) custom-call(bf16[512,512]{1,0:T(8,128)(2,1)S(1)} %bitcast.75, bf16[4096,512]{1,0:T(8,128)(2,1)S(1)} %copy-done, f32[1,4096]{1,0:T(1,128)S(1)} %bitcast.79, f32[4096,128]{1,0:T(8,128)S(1)} %copy-done.2, f32[4096,128]{1,0:T(8,128)S(1)} %copy-done.3), custom_call_target="tpu_custom_call" | custom-call | flops 2684354560 | bytes 12582912 | tf_op jit(solution)/shard_map/slabs/pallas_call | solution.py:305
  44.1 7.4 %slabs.3 = (bf16[512,4096]{1,0:T(8,128)(2,1)S(1)}, bf16[8,128,512]{2,1,0:T(8,128)(2,1)S(1)}) custom-call(bf16[512,512]{1,0:T(8,128)(2,1)S(1)} %collective-permute-done.9.refs_0_, bf16[4096,512]{1,0:T(8,128)(2,1)S(1)} %copy-done.1, f32[1,4096]{1,0:T(1,128)S(1)} %bitcast.80, f32[4096,128]{1,0:T(8,128)S(1)} %copy-done.2, f32[4096,128]{1,0:T(8,128)S(1)} %copy-done.4, ...), custom_call_target="tpu_custom_call" | custom-call | flops 4831838208 | bytes 12582912 | tf_op jit(solution)/shard_map/slabs/pallas_call | solution.py:305
  54.3 0.8 collective-permute-start.13
  55.1 1.2 %collective-permute-start.12 = (bf16[128,512]{1,0:T(8,128)(2,1)S(1)}, bf16[128,512]{1,0:T(8,128)(2,1)S(1)}, u32[]{:S(2)}, u32[]{:S(2)}) collective-permute-start(bf16[128,512]{1,0:T(8,128)(2,1)S(1)} %get-tuple-element.87), channel_id=1, source_target_pairs={{0,4},{1,5},{2,6},{3,7},{4,0},{5,1},{6,2},{7,3},{8,12},{9,13},{10,... | collective-permute-start | bytes 393224 | tf_op jit(solution)/shard_map/ppermute | solution.py:64
  56.3 1.5 %collective-permute-start.11 = (bf16[128,512]{1,0:T(8,128)(2,1)S(1)}, bf16[128,512]{1,0:T(8,128)(2,1)S(1)}, u32[]{:S(2)}, u32[]{:S(2)}) collective-permute-start(bf16[128,512]{1,0:T(8,128)(2,1)S(1)} %get-tuple-element.88), channel_id=1, source_target_pairs={{0,1},{1,0},{2,3},{3,2},{4,5},{5,4},{6,7},{7,6},{8,9},{9,8},{10,11... | collective-permute-start | bytes 393224 | tf_op jit(solution)/shard_map/ppermute | solution.py:64
  57.8 5.8 %factor.4 = (f32[256,512]{1,0:T(8,128)S(1)}, f32[4096,128]{1,0:T(8,128)}) custom-call(f32[512,512]{1,0:T(8,128)S(1)} %gram.1.refs_0_, bf16[512,4096]{1,0:T(8,128)(2,1)S(1)} %get-tuple-element.40.refs_6_.slab0_ref.refs_1_, bf16[512,4096]{1,0:T(8,128)(2,1)S(1)} %get-tuple-element.43.slab1_ref.refs_2_, f32[4096,128]{1,0:T(8,128)S(1)} %copy-done.4), custom_call_target="tpu_custom_call" | custom-call | flops 6000000000 | bytes 4194304 | tf_op jit(solution)/shard_map/factor/pallas_call | solution.py:433
  64.0 5.3 %collective-permute-start.16 = (bf16[128,512]{1,0:T(8,128)(2,1)S(1)}, bf16[128,512]{1,0:T(8,128)(2,1)S(1)}, u32[]{:S(2)}, u32[]{:S(2)}) collective-permute-start(bf16[128,512]{1,0:T(8,128)(2,1)S(1)} %pad_maximum_fusion.5), channel_id=1, source_target_pairs={{0,24},{1,25},{2,26},{3,27},{4,28},{5,29},{6,30},{7,31},{8,16},{9,... | collective-permute-start | bytes 393224 | tf_op jit(solution)/shard_map/ppermute | solution.py:64
  69.9 5.8 %factor.5 = (f32[256,512]{1,0:T(8,128)S(1)}, f32[256,512]{1,0:T(8,128)S(1)}, bf16[512,512]{1,0:T(8,128)(2,1)S(1)}) custom-call(f32[512,512]{1,0:T(8,128)S(1)} %gram.1.refs_0_, bf16[512,4096]{1,0:T(8,128)(2,1)S(1)} %get-tuple-element.40.refs_6_.slab0_ref.refs_1_, bf16[512,4096]{1,0:T(8,128)(2,1)S(1)} %get-tuple-element.43.slab1_ref.refs_2_, ...), custom_call_target="tpu_custom_call" | custom-call | flops 6000000000 | bytes 4194304 | tf_op jit(solution)/shard_map/factor/pallas_call | solution.py:433
  76.3 5.7 %factor.6 = (f32[256,512]{1,0:T(8,128)S(1)}, f32[128,512]{1,0:T(8,128)S(1)}) custom-call(f32[256,512]{1,0:T(8,128)S(1)} %get-tuple-element.49.refs_0_, bf16[512,4096]{1,0:T(8,128)(2,1)S(1)} %get-tuple-element.40.refs_6_.slab0_ref.refs_1_, bf16[512,4096]{1,0:T(8,128)(2,1)S(1)} %get-tuple-element.43.slab1_ref.refs_2_, f32[256,512]{1,0:T(8,128)S(1)} %get-tuple-element.50.refs_3_), custom_call_target="tpu_custom_call" | custom-call | flops 6000000000 | bytes 4194304 | tf_op jit(solution)/shard_map/factor/pallas_call | solution.py:433
  82.3 0.8 collective-permute-start.19
  83.1 1.4 %collective-permute-start.18 = (bf16[128,512]{1,0:T(8,128)(2,1)S(1)}, bf16[128,512]{1,0:T(8,128)(2,1)S(1)}, u32[]{:S(2)}, u32[]{:S(2)}) collective-permute-start(bf16[128,512]{1,0:T(8,128)(2,1)S(1)} %pad_maximum_fusion.6), channel_id=1, source_target_pairs={{0,4},{1,5},{2,6},{3,7},{4,0},{5,1},{6,2},{7,3},{8,12},{9,13},{10,... | collective-permute-start | bytes 393224 | tf_op jit(solution)/shard_map/ppermute | solution.py:64
  84.6 1.3 %collective-permute-start.17 = (bf16[128,512]{1,0:T(8,128)(2,1)S(1)}, bf16[128,512]{1,0:T(8,128)(2,1)S(1)}, u32[]{:S(2)}, u32[]{:S(2)}) collective-permute-start(bf16[128,512]{1,0:T(8,128)(2,1)S(1)} %pad_maximum_fusion.6), channel_id=1, source_target_pairs={{0,1},{1,0},{2,3},{3,2},{4,5},{5,4},{6,7},{7,6},{8,9},{9,8},{10,11... | collective-permute-start | bytes 393224 | tf_op jit(solution)/shard_map/ppermute | solution.py:64
  85.9 5.4 %factor.7 = f32[256,512]{1,0:T(8,128)S(1)} custom-call(f32[128,512]{1,0:T(8,128)S(1)} %get-tuple-element.56.refs_0_, bf16[512,4096]{1,0:T(8,128)(2,1)S(1)} %get-tuple-element.40.refs_6_.slab0_ref.refs_1_, bf16[512,4096]{1,0:T(8,128)(2,1)S(1)} %get-tuple-element.43.slab1_ref.refs_2_, f32[256,512]{1,0:T(8,128)S(1)} %get-tuple-element.57.refs_3_), custom_call_target="tpu_custom_call" | custom-call | flops 6000000000 | bytes 4194304 | tf_op jit(solution)/shard_map/factor/pallas_call | solution.py:433
  94.9 7.4 %finish.1 = (f32[4096,128]{1,0:T(8,128)}, f32[4096,128]{1,0:T(8,128)}) custom-call(s32[2]{0:T(128)S(1)} %copy-done.6, s32[2,4]{1,0:T(2,128)S(1)} %copy-done.5, s32[1]{0:T(128)} %bitcast.me_ref, s32[1]{0:T(128)} %bitcast.1.core_ref.refs_5_, bf16[8,128,512]{2,1,0:T(8,128)(2,1)S(1)} %bitcast.71, ...), custom_call_target="tpu_custom_call", output_to_operand_aliasing={{1}: (10, {})} | custom-call | flops 1073741824 | bytes 16777216 | tf_op jit(solution)/shard_map/finish/pallas_call | solution.py:562
  (98 shorter events, 9.8 us)
Async XLA Ops:
  0.6 2.6 %copy-start.6 = (s32[2]{0:T(128)S(1)}, s32[2]{0:T(128)}, u32[]{:S(2)}) copy-start(s32[2]{0:T(128)} %owner_ref.1) | copy-start | bytes 28
  2.7 2.1 %collective-permute-start = (bf16[2,256,512]{2,1,0:T(8,128)(2,1)S(1)}, bf16[2,256,512]{2,1,0:T(8,128)(2,1)S(1)}, u32[]{:S(2)}, u32[]{:S(2)}) collective-permute-start(bf16[2,256,512]{2,1,0:T(8,128)(2,1)S(1)} %get-tuple-element.33), channel_id=1, source_target_pairs={{0,2},{1,3},{2,0},{3,1},{4,6},{5,7},{6,4},{7,5},{8,10},{9,11},{10,... | collective-permute-start | bytes 1572872 | tf_op jit(solution)/shard_map/ppermute | solution.py:64
  4.9 31.5 %copy-start.2 = (f32[4096,128]{1,0:T(8,128)S(1)}, f32[4096,128]{1,0:T(8,128)}, u32[]{:S(2)}) copy-start(f32[4096,128]{1,0:T(8,128)} %res_ref.1) | copy-start | bytes 6291460
  4.9 7.6 %collective-permute-start.2 = (bf16[2,64,512]{2,1,0:T(8,128)(2,1)S(1)}, bf16[2,64,512]{2,1,0:T(8,128)(2,1)S(1)}, u32[]{:S(2)}, u32[]{:S(2)}) collective-permute-start(bf16[2,64,512]{2,1,0:T(8,128)(2,1)S(1)} %get-tuple-element.93), channel_id=1, source_target_pairs={{0,4},{1,5},{2,6},{3,7},{4,0},{5,1},{6,2},{7,3},{8,12},{9,13},{10,... | collective-permute-start | bytes 393224 | tf_op jit(solution)/shard_map/ppermute | solution.py:64
  7.9 6.4 %collective-permute-start.3 = (bf16[2,64,512]{2,1,0:T(8,128)(2,1)S(1)}, bf16[2,64,512]{2,1,0:T(8,128)(2,1)S(1)}, u32[]{:S(2)}, u32[]{:S(2)}) collective-permute-start(bf16[2,64,512]{2,1,0:T(8,128)(2,1)S(1)} %get-tuple-element.94), channel_id=1, source_target_pairs={{0,1},{1,0},{2,3},{3,2},{4,5},{5,4},{6,7},{7,6},{8,9},{9,8},{10,11... | collective-permute-start | bytes 393224 | tf_op jit(solution)/shard_map/ppermute | solution.py:64
  9.4 6.4 %collective-permute-start.1 = (bf16[2,64,512]{2,1,0:T(8,128)(2,1)S(1)}, bf16[2,64,512]{2,1,0:T(8,128)(2,1)S(1)}, u32[]{:S(2)}, u32[]{:S(2)}) collective-permute-start(bf16[2,64,512]{2,1,0:T(8,128)(2,1)S(1)} %get-tuple-element.95), channel_id=1, source_target_pairs={{0,5},{1,4},{2,7},{3,6},{4,1},{5,0},{6,3},{7,2},{8,13},{9,12},{10,... | collective-permute-start | bytes 393224 | tf_op jit(solution)/shard_map/ppermute | solution.py:64
  15.8 5.5 %collective-permute-start.4 = (bf16[2,64,512]{2,1,0:T(8,128)(2,1)S(1)}, bf16[2,64,512]{2,1,0:T(8,128)(2,1)S(1)}, u32[]{:S(2)}, u32[]{:S(2)}) collective-permute-start(bf16[2,64,512]{2,1,0:T(8,128)(2,1)S(1)} %fusion.5), channel_id=1, source_target_pairs={{0,8},{1,9},{2,18},{3,19},{4,12},{5,13},{6,22},{7,23},{8,0},{9,1},... | collective-permute-start | bytes 393224 | tf_op jit(solution)/shard_map/ppermute | solution.py:64
  21.5 5.9 %collective-permute-start.5 = (bf16[2,64,512]{2,1,0:T(8,128)(2,1)S(1)}, bf16[2,64,512]{2,1,0:T(8,128)(2,1)S(1)}, u32[]{:S(2)}, u32[]{:S(2)}) collective-permute-start(bf16[2,64,512]{2,1,0:T(8,128)(2,1)S(1)} %broadcast_select_fusion.9), channel_id=1, source_target_pairs={{0,16},{1,17},{2,10},{3,11},{4,20},{5,21},{6,14},{7,15},{8,24},{9,... | collective-permute-start | bytes 393224 | tf_op jit(solution)/shard_map/ppermute | solution.py:64
  27.5 5.6 %collective-permute-start.8 = (bf16[2,64,512]{2,1,0:T(8,128)(2,1)S(1)}, bf16[2,64,512]{2,1,0:T(8,128)(2,1)S(1)}, u32[]{:S(2)}, u32[]{:S(2)}) collective-permute-start(bf16[2,64,512]{2,1,0:T(8,128)(2,1)S(1)} %broadcast_select_fusion.10), channel_id=1, source_target_pairs={{0,1},{1,0},{2,3},{3,2},{4,5},{5,4},{6,7},{7,6},{8,9},{9,8},{10,11... | collective-permute-start | bytes 393224 | tf_op jit(solution)/shard_map/ppermute | solution.py:64
  28.7 5.6 %collective-permute-start.7 = (bf16[2,64,512]{2,1,0:T(8,128)(2,1)S(1)}, bf16[2,64,512]{2,1,0:T(8,128)(2,1)S(1)}, u32[]{:S(2)}, u32[]{:S(2)}) collective-permute-start(bf16[2,64,512]{2,1,0:T(8,128)(2,1)S(1)} %broadcast_select_fusion.10), channel_id=1, source_target_pairs={{0,4},{1,5},{2,6},{3,7},{4,0},{5,1},{6,2},{7,3},{8,12},{9,13},{10,... | collective-permute-start | bytes 393224 | tf_op jit(solution)/shard_map/ppermute | solution.py:64
  30.3 5.9 %collective-permute-start.6 = (bf16[2,64,512]{2,1,0:T(8,128)(2,1)S(1)}, bf16[2,64,512]{2,1,0:T(8,128)(2,1)S(1)}, u32[]{:S(2)}, u32[]{:S(2)}) collective-permute-start(bf16[2,64,512]{2,1,0:T(8,128)(2,1)S(1)} %broadcast_select_fusion.10), channel_id=1, source_target_pairs={{0,5},{1,4},{2,7},{3,6},{4,1},{5,0},{6,3},{7,2},{8,13},{9,12},{10,... | collective-permute-start | bytes 393224 | tf_op jit(solution)/shard_map/ppermute | solution.py:64
  36.3 7.8 %collective-permute-start.9 = (bf16[512,512]{1,0:T(8,128)(2,1)S(1)}, bf16[512,512]{1,0:T(8,128)(2,1)S(1)}, u32[]{:S(2)}, u32[]{:S(2)}) collective-permute-start(bf16[512,512]{1,0:T(8,128)(2,1)S(1)} %bitcast.74), channel_id=1, source_target_pairs={{0,2},{1,3},{2,0},{3,1},{4,6},{5,7},{6,4},{7,5},{8,10},{9,11},{10,... | collective-permute-start | bytes 1572872 | tf_op jit(solution)/shard_map/ppermute | solution.py:64
  36.3 2.2 %copy-start = (bf16[4096,512]{1,0:T(8,128)(2,1)S(1)}, bf16[4096,512]{1,0:T(8,128)(2,1)}, u32[]{:S(2)}) copy-start(bf16[4096,512]{1,0:T(8,128)(2,1)} %refs_1_.3) | copy-start | bytes 12582916
  38.5 1.6 %copy-start.3 = (f32[4096,128]{1,0:T(8,128)S(1)}, f32[4096,128]{1,0:T(8,128)}, u32[]{:S(2)}) copy-start(f32[4096,128]{1,0:T(8,128)} %coef_ref.1) | copy-start | bytes 6291460
  40.1 4.0 %copy-start.1 = (bf16[4096,512]{1,0:T(8,128)(2,1)S(1)}, bf16[4096,512]{1,0:T(8,128)(2,1)}, u32[]{:S(2)}) copy-start(bf16[4096,512]{1,0:T(8,128)(2,1)} %refs_1_.3) | copy-start | bytes 12582916
  40.1 4.0 %copy-start.4 = (f32[4096,128]{1,0:T(8,128)S(1)}, f32[4096,128]{1,0:T(8,128)}, u32[]{:S(2)}) copy-start(f32[4096,128]{1,0:T(8,128)} %coef_ref.1) | copy-start | bytes 6291460
  51.6 2.1 %collective-permute-start.10 = (bf16[2,2,128,512]{3,2,1,0:T(8,128)(2,1)S(1)}, bf16[2,2,128,512]{3,2,1,0:T(8,128)(2,1)S(1)}, u32[]{:S(2)}, u32[]{:S(2)}) collective-permute-start(bf16[2,2,128,512]{3,2,1,0:T(8,128)(2,1)S(1)} %get-tuple-element.78), channel_id=1, source_target_pairs={{0,2},{1,3},{2,0},{3,1},{4,6},{5,7},{6,4},{7,5},{8,10},{9,11},{10,... | collective-permute-start | bytes 1572872 | tf_op jit(solution)/shard_map/ppermute | solution.py:64
  54.3 9.4 %collective-permute-start.13 = (bf16[128,512]{1,0:T(8,128)(2,1)S(1)}, bf16[128,512]{1,0:T(8,128)(2,1)S(1)}, u32[]{:S(2)}, u32[]{:S(2)}) collective-permute-start(bf16[128,512]{1,0:T(8,128)(2,1)S(1)} %get-tuple-element.86), channel_id=1, source_target_pairs={{0,5},{1,4},{2,7},{3,6},{4,1},{5,0},{6,3},{7,2},{8,13},{9,12},{10,... | collective-permute-start | bytes 393224 | tf_op jit(solution)/shard_map/ppermute | solution.py:64
  55.1 8.5 %collective-permute-start.12 = (bf16[128,512]{1,0:T(8,128)(2,1)S(1)}, bf16[128,512]{1,0:T(8,128)(2,1)S(1)}, u32[]{:S(2)}, u32[]{:S(2)}) collective-permute-start(bf16[128,512]{1,0:T(8,128)(2,1)S(1)} %get-tuple-element.87), channel_id=1, source_target_pairs={{0,4},{1,5},{2,6},{3,7},{4,0},{5,1},{6,2},{7,3},{8,12},{9,13},{10,... | collective-permute-start | bytes 393224 | tf_op jit(solution)/shard_map/ppermute | solution.py:64
  56.3 7.3 %collective-permute-start.11 = (bf16[128,512]{1,0:T(8,128)(2,1)S(1)}, bf16[128,512]{1,0:T(8,128)(2,1)S(1)}, u32[]{:S(2)}, u32[]{:S(2)}) collective-permute-start(bf16[128,512]{1,0:T(8,128)(2,1)S(1)} %get-tuple-element.88), channel_id=1, source_target_pairs={{0,1},{1,0},{2,3},{3,2},{4,5},{5,4},{6,7},{7,6},{8,9},{9,8},{10,11... | collective-permute-start | bytes 393224 | tf_op jit(solution)/shard_map/ppermute | solution.py:64
  64.0 18.0 %collective-permute-start.16 = (bf16[128,512]{1,0:T(8,128)(2,1)S(1)}, bf16[128,512]{1,0:T(8,128)(2,1)S(1)}, u32[]{:S(2)}, u32[]{:S(2)}) collective-permute-start(bf16[128,512]{1,0:T(8,128)(2,1)S(1)} %pad_maximum_fusion.5), channel_id=1, source_target_pairs={{0,24},{1,25},{2,26},{3,27},{4,28},{5,29},{6,30},{7,31},{8,16},{9,... | collective-permute-start | bytes 393224 | tf_op jit(solution)/shard_map/ppermute | solution.py:64
  69.3 12.7 %collective-permute-start.15 = (bf16[128,512]{1,0:T(8,128)(2,1)S(1)}, bf16[128,512]{1,0:T(8,128)(2,1)S(1)}, u32[]{:S(2)}, u32[]{:S(2)}) collective-permute-start(bf16[128,512]{1,0:T(8,128)(2,1)S(1)} %pad_maximum_fusion.5), channel_id=1, source_target_pairs={{0,16},{1,17},{2,18},{3,19},{4,20},{5,21},{6,22},{7,23},{8,24},{9,... | collective-permute-start | bytes 393224 | tf_op jit(solution)/shard_map/ppermute | solution.py:64
  69.3 12.7 %collective-permute-start.14 = (bf16[128,512]{1,0:T(8,128)(2,1)S(1)}, bf16[128,512]{1,0:T(8,128)(2,1)S(1)}, u32[]{:S(2)}, u32[]{:S(2)}) collective-permute-start(bf16[128,512]{1,0:T(8,128)(2,1)S(1)} %pad_maximum_fusion.5), channel_id=1, source_target_pairs={{0,8},{1,9},{2,10},{3,11},{4,12},{5,13},{6,14},{7,15},{8,0},{9,1},... | collective-permute-start | bytes 393224 | tf_op jit(solution)/shard_map/ppermute | solution.py:64
  75.7 16.6 %collective-permute-start.21 = (f32[256,512]{1,0:T(8,128)S(1)}, f32[256,512]{1,0:T(8,128)S(1)}, u32[]{:S(2)}, u32[]{:S(2)}) collective-permute-start(f32[256,512]{1,0:T(8,128)S(1)} %get-tuple-element.48.refs_3_), channel_id=1, source_target_pairs={{0,2},{1,3},{2,0},{3,1},{4,6},{5,7},{6,4},{7,5},{8,10},{9,11},{10,... | collective-permute-start | bytes 1572872 | tf_op jit(solution)/shard_map/ppermute | solution.py:64
  75.8 16.4 %collective-permute-start.22 = (f32[256,512]{1,0:T(8,128)S(1)}, f32[256,512]{1,0:T(8,128)S(1)}, u32[]{:S(2)}, u32[]{:S(2)}) collective-permute-start(f32[256,512]{1,0:T(8,128)S(1)} %get-tuple-element.50.refs_3_), channel_id=1, source_target_pairs={{0,2},{1,3},{2,0},{3,1},{4,6},{5,7},{6,4},{7,5},{8,10},{9,11},{10,... | collective-permute-start | bytes 1572872 | tf_op jit(solution)/shard_map/ppermute | solution.py:64
  82.3 9.0 %collective-permute-start.19 = (bf16[128,512]{1,0:T(8,128)(2,1)S(1)}, bf16[128,512]{1,0:T(8,128)(2,1)S(1)}, u32[]{:S(2)}, u32[]{:S(2)}) collective-permute-start(bf16[128,512]{1,0:T(8,128)(2,1)S(1)} %pad_maximum_fusion.6), channel_id=1, source_target_pairs={{0,5},{1,4},{2,7},{3,6},{4,1},{5,0},{6,3},{7,2},{8,13},{9,12},{10,... | collective-permute-start | bytes 393224 | tf_op jit(solution)/shard_map/ppermute | solution.py:64
  83.1 8.3 %collective-permute-start.18 = (bf16[128,512]{1,0:T(8,128)(2,1)S(1)}, bf16[128,512]{1,0:T(8,128)(2,1)S(1)}, u32[]{:S(2)}, u32[]{:S(2)}) collective-permute-start(bf16[128,512]{1,0:T(8,128)(2,1)S(1)} %pad_maximum_fusion.6), channel_id=1, source_target_pairs={{0,4},{1,5},{2,6},{3,7},{4,0},{5,1},{6,2},{7,3},{8,12},{9,13},{10,... | collective-permute-start | bytes 393224 | tf_op jit(solution)/shard_map/ppermute | solution.py:64
  84.6 6.8 %collective-permute-start.17 = (bf16[128,512]{1,0:T(8,128)(2,1)S(1)}, bf16[128,512]{1,0:T(8,128)(2,1)S(1)}, u32[]{:S(2)}, u32[]{:S(2)}) collective-permute-start(bf16[128,512]{1,0:T(8,128)(2,1)S(1)} %pad_maximum_fusion.6), channel_id=1, source_target_pairs={{0,1},{1,0},{2,3},{3,2},{4,5},{5,4},{6,7},{7,6},{8,9},{9,8},{10,11... | collective-permute-start | bytes 393224 | tf_op jit(solution)/shard_map/ppermute | solution.py:64
  91.3 2.0 %collective-permute-start.23 = (f32[256,512]{1,0:T(8,128)S(1)}, f32[256,512]{1,0:T(8,128)S(1)}, u32[]{:S(2)}, u32[]{:S(2)}) collective-permute-start(f32[256,512]{1,0:T(8,128)S(1)} %get-tuple-element.57.refs_3_), channel_id=1, source_target_pairs={{0,2},{1,3},{2,0},{3,1},{4,6},{5,7},{6,4},{7,5},{8,10},{9,11},{10,... | collective-permute-start | bytes 1572872 | tf_op jit(solution)/shard_map/ppermute | solution.py:64
  91.6 2.4 %collective-permute-start.20 = (bf16[2,2,128,512]{3,2,1,0:T(8,128)(2,1)S(1)}, bf16[2,2,128,512]{3,2,1,0:T(8,128)(2,1)S(1)}, u32[]{:S(2)}, u32[]{:S(2)}) collective-permute-start(bf16[2,2,128,512]{3,2,1,0:T(8,128)(2,1)S(1)} %bitcast.81), channel_id=1, source_target_pairs={{0,2},{1,3},{2,0},{3,1},{4,6},{5,7},{6,4},{7,5},{8,10},{9,11},{10,... | collective-permute-start | bytes 1572872 | tf_op jit(solution)/shard_map/ppermute | solution.py:64
  92.2 2.6 %collective-permute-start.24 = (f32[256,512]{1,0:T(8,128)S(1)}, f32[256,512]{1,0:T(8,128)S(1)}, u32[]{:S(2)}, u32[]{:S(2)}) collective-permute-start(f32[256,512]{1,0:T(8,128)S(1)} %factor.7), channel_id=1, source_target_pairs={{0,2},{1,3},{2,0},{3,1},{4,6},{5,7},{6,4},{7,5},{8,10},{9,11},{10,... | collective-permute-start | bytes 1572872 | tf_op jit(solution)/shard_map/ppermute | solution.py:64
  92.5 2.4 %copy-start.5 = (s32[2,4]{1,0:T(2,128)S(1)}, s32[2,4]{1,0:T(2,128)}, u32[]{:S(2)}) copy-start(s32[2,4]{1,0:T(2,128)} %tiles_ref.3) | copy-start | bytes 100

commit v4 on v3

--- a/solution.py
+++ b/solution.py
@@ -3,6 +3,7 @@
 
 import jax
 import jax.numpy as jnp
+import numpy as np
 from jax import lax
 from jax.experimental import pallas as pl
 from jax.experimental.pallas import tpu as pltpu
@@ -69,9 +70,9 @@
 
 
 def swap_among(pick, me, axes, low, high):
-    place = bit_of(me, low) + 2 * bit_of(me, high)
+    place = (bit_of(me, low) + 2 * bit_of(me, high)).astype(jnp.uint32)
     flips = [0, low, high, low | high]
-    return place, [swap(pick(place ^ c), axes, flips[c]) for c in (1, 2, 3)]
+    return place, [swap(pick(place ^ np.uint32(c)), axes, flips[c]) for c in (1, 2, 3)]
 
 
 def ordered(parts, me, low, high, axis):
@@ -90,6 +91,7 @@
     quarters = half.reshape(STEPS, 4, BLOCK // 8, width)
     pick = lambda place: lax.dynamic_index_in_dim(quarters, place, 1, False)
     place, got = swap_among(pick, me, AXES, low, high)
+    got, prepared = lax.optimization_barrier((got, prepared))
     part = jnp.where(
         differs(high),
         jnp.where(differs(low), got[2], got[1]),
@@ -103,10 +105,8 @@
             hops.append((flip, jnp.where(on_core, second, first)))
     if len(far) % 2:
         hops.append((far[-1], far[-1]))
-    for hop, (flip, mask) in enumerate(hops):
+    for flip, mask in hops:
         other = swap(part, AXES, flip)
-        if hop == len(hops) - 2:
-            other, prepared = lax.optimization_barrier((other, prepared))
         part = jnp.where(differs(mask), other, part)
     _, got = swap_among(lambda place: part, me, AXES, low, high)
     half = ordered([part] + got, me, low, high, 1)
@@ -201,6 +201,55 @@
         ),
         name="gram",
     )(core, block, *map(in_vmem, slab))
+
+
+def load_kernel(scale, chunk, feat_in, res_in, coef_in, norm_ref, feat_ref, res_ref, coef_ref, sems, more_sems):
+    chunks = feat_in.shape[0] // chunk
+    rows_of = lambda i: pl.ds(pl.multiple_of(i * chunk, chunk), chunk)
+
+    def load(i):
+        return pltpu.make_async_copy(feat_in.at[rows_of(i), :], feat_ref.at[rows_of(i), :], sems.at[i])
+
+    others = [
+        pltpu.make_async_copy(source, target, more_sems.at[i])
+        for i, (source, target) in enumerate(((res_in, res_ref), (coef_in, coef_ref)))
+    ]
+    for i in range(chunks):
+        load(i).start()
+    for copy in others:
+        copy.start()
+    ones = jnp.ones((16, feat_in.shape[1]), jnp.bfloat16)
+
+    def body(i, _):
+        load(i).wait()
+        wide = feat_ref[rows_of(i), :].astype(jnp.float32)
+        square = wide * wide
+        high = square.astype(jnp.bfloat16)
+        low = (square - high.astype(jnp.float32)).astype(jnp.bfloat16)
+        sums = [lax.dot_general(ones, part, NT, preferred_element_type=jnp.float32) for part in (high, low)]
+        norm_ref[:, rows_of(i)] = (sums[0] + sums[1])[:1] * scale
+        return 0
+
+    lax.fori_loop(0, chunks, body, 0)
+    for copy in others:
+        copy.wait()
+
+
+def load_all(features, residual, coefficients, scale, chunk=512):
+    rows = features.shape[0]
+    arrays = (features, residual, coefficients)
+    vmem, hbm = pl.BlockSpec(memory_space=pltpu.VMEM), pl.BlockSpec(memory_space=pltpu.HBM)
+    return pl.pallas_call(
+        functools.partial(load_kernel, scale, chunk),
+        in_specs=[hbm] * 3,
+        out_specs=(vmem,) * 4,
+        out_shape=(jax.ShapeDtypeStruct((1, rows), jnp.float32),)
+        + tuple(pltpu.VMEM(value.shape, value.dtype) for value in arrays),
+        scratch_shapes=[pltpu.SemaphoreType.DMA((rows // chunk,)), pltpu.SemaphoreType.DMA((2,))],
+        compiler_params=pltpu.CompilerParams(vmem_limit_bytes=SMALL_LIMIT),
+        cost_estimate=pl.CostEstimate(flops=3 * 10**9, bytes_accessed=8 * 1024 * 1024, transcendentals=0),
+        name="load",
+    )(*(pltpu.with_memory_space_constraint(value, pltpu.HBM) for value in arrays))
 
 
 def slab_kernel(scale, chunk, *refs):
@@ -598,9 +647,9 @@
     groups = spread.count
     own = targets // groups
 
-    wide = features.astype(jnp.float32)
-    norms = (jnp.sum(wide * wide, axis=1) * scale).reshape(1, rows_dev)
-    half, other, norms = fetch_blocks(features, norms, block_owner, block_tiles, me, devices, sub_count)
+    loaded = load_all(features, residual, coefficients, scale)
+    half, other, loaded = fetch_blocks(features, loaded, block_owner, block_tiles, me, devices, sub_count)
+    norms, features, residual, coefficients = loaded
     core, on_core = bit_of(me, sub_count).reshape(1), (me & sub_count) != 0
     first = slabs(half, features, norms, residual, coefficients, scale)
     other, first = lax.optimization_barrier((other, first))

time: 103 us -> 98.1 us (0.952)
  Pallas kernels: 44 us -> 48.7 us
  local copies, waits for them, and re-layouts: 4.08 us -> 0.29 us
  other arithmetic: 5.42 us -> 2.32 us
  starting transfers between devices: 28 us -> 25.8 us
    pallas_call x0 -> x1, Pallas kernels: none -> 4.58 us  [load_all(): pl.pallas_call(functools.partial(load_kernel, scale, chunk), in_specs=[hb...]
    unnamed x14 -> x4, local copies, waits for them, and re-layouts: 3.8 us -> 0.01 us
    reduce_sum x1 -> x0, other arithmetic: 3.08 us -> none  [local(): norms = (jnp.sum(wide * wide, axis=1) * scale).reshape(1, rows_dev)]
    ppermute x25, starting transfers between devices: 28 us -> 25.8 us  [swap(): lax.ppermute(value, axes, [(i, i ^ flip_of(i)) for i in range(lax.axis_si...]
  transfers between devices with their start and end apart: 25 -> 25, of which waited for: 12 -> 15; matrix products, arithmetic and copies ran while one was open for 4% -> 1% of each run, Pallas kernels for 27% -> 33%
where the time goes in v4:
time: 98.1 us; the launch traced here: 97.9 us
  Pallas kernels  48.7 us (50%)
  starting transfers between devices  25.8 us (26%)
  waiting for transfers between devices  19.4 us (20%)
  other arithmetic  2.32 us (2%)
  between operations  1.4 us (1%)
    ppermute x25, starting transfers between devices, swap(): lax.ppermute(value, axes, [(i, i ^ flip_of(i)) for i in range(lax.axis_si...  25.8 us
    pallas_call x4, Pallas kernels, factor_step(): pl.pallas_call(functools.partial(factor_kernel, index, copied is not None...  22.7 us
    ppermute x25, waiting for transfers between devices, swap(): lax.ppermute(value, axes, [(i, i ^ flip_of(i)) for i in range(lax.axis_si...  19.4 us
    pallas_call x2, Pallas kernels, slabs(): pl.pallas_call(functools.partial(slab_kernel, scale, chunk), in_specs=in_...  11.3 us
    pallas_call x1, Pallas kernels, finish(): pl.pallas_call(functools.partial(final_kernel, step_size, chunk), in_spec...  7.37 us
    pallas_call x1, Pallas kernels, load_all(): pl.pallas_call(functools.partial(load_kernel, scale, chunk), in_specs=[hb...  4.58 us
    pallas_call x1, Pallas kernels, pick_halves(): pl.pallas_call(pick_kernel, grid_spec=pltpu.PrefetchScalarGridSpec(num_sc...  2.18 us
  transfers between devices with their start and end apart: 25, of which 15 were waited for; matrix products, arithmetic and copies ran while one was open for 1% of the time, Pallas kernels for 33%

profile of v4, /device:TPU:0, one launch (start us, length us, event | category | flops | bytes accessed | tf_op | source)
XLA Modules:
  0.0 97.9 jit_solution(8455672609702553935)
XLA Ops:
  0.6 2.2 %pick.1 = (bf16[2,256,512]{2,1,0:T(8,128)(2,1)S(1)}, bf16[2,256,512]{2,1,0:T(8,128)(2,1)S(1)}) custom-call(s32[2,4]{1,0:T(2,128)} %tiles_ref.3, s32[1]{0:T(128)} %bitcast.1.core_ref.refs_5_, bf16[4096,512]{1,0:T(8,128)(2,1)} %feat_in.1), custom_call_target="tpu_custom_call" | custom-call | tf_op jit(solution)/shard_map/pick/pallas_call | solution.py:48
  3.4 1.5 %collective-permute-done = bf16[2,256,512]{2,1,0:T(8,128)(2,1)S(1)} collective-permute-done((bf16[2,256,512]{2,1,0:T(8,128)(2,1)S(1)}, bf16[2,256,512]{2,1,0:T(8,128)(2,1)S(1)}, u32[]{:S(2)}, u32[]{:S(2)}) %collective-permute-start) | collective-permute-done | bytes 524320 | tf_op jit(solution)/shard_map/ppermute | solution.py:65
  5.1 3.9 %collective-permute-start.3 = (bf16[2,64,512]{2,1,0:T(8,128)(2,1)S(1)}, bf16[2,64,512]{2,1,0:T(8,128)(2,1)S(1)}, u32[]{:S(2)}, u32[]{:S(2)}) collective-permute-start(bf16[2,64,512]{2,1,0:T(8,128)(2,1)S(1)} %get-tuple-element.111), channel_id=1, source_target_pairs={{0,5},{1,4},{2,7},{3,6},{4,1},{5,0},{6,3},{7,2},{8,13},{9,12},{10,... | collective-permute-start | bytes 393224 | tf_op jit(solution)/shard_map/ppermute | solution.py:65
  9.6 4.6 %load.1 = (f32[1,4096]{1,0:T(1,128)S(1)}, bf16[4096,512]{1,0:T(8,128)(2,1)S(1)}, f32[4096,128]{1,0:T(8,128)S(1)}, f32[4096,128]{1,0:T(8,128)S(1)}) custom-call(bf16[4096,512]{1,0:T(8,128)(2,1)} %feat_in.1, f32[4096,128]{1,0:T(8,128)} %res_in.1, f32[4096,128]{1,0:T(8,128)} %coef_in.1), custom_call_target="tpu_custom_call" | custom-call | flops 3000000000 | bytes 8388608 | tf_op jit(solution)/shard_map/load/pallas_call | solution.py:242
  14.2 1.4 %collective-permute-done.2 = bf16[2,64,512]{2,1,0:T(8,128)(2,1)S(1)} collective-permute-done((bf16[2,64,512]{2,1,0:T(8,128)(2,1)S(1)}, bf16[2,64,512]{2,1,0:T(8,128)(2,1)S(1)}, u32[]{:S(2)}, u32[]{:S(2)}) %collective-permute-start.2) | collective-permute-done | bytes 131104 | tf_op jit(solution)/shard_map/ppermute | solution.py:65
  15.9 1.6 %collective-permute-start.4 = (bf16[2,64,512]{2,1,0:T(8,128)(2,1)S(1)}, bf16[2,64,512]{2,1,0:T(8,128)(2,1)S(1)}, u32[]{:S(2)}, u32[]{:S(2)}) collective-permute-start(bf16[2,64,512]{2,1,0:T(8,128)(2,1)S(1)} %fusion.5), channel_id=1, source_target_pairs={{0,8},{1,9},{2,18},{3,19},{4,12},{5,13},{6,22},{7,23},{8,0},{9,1},... | collective-permute-start | bytes 393224 | tf_op jit(solution)/shard_map/ppermute | solution.py:65
  17.6 4.6 %collective-permute-done.4 = bf16[2,64,512]{2,1,0:T(8,128)(2,1)S(1)} collective-permute-done((bf16[2,64,512]{2,1,0:T(8,128)(2,1)S(1)}, bf16[2,64,512]{2,1,0:T(8,128)(2,1)S(1)}, u32[]{:S(2)}, u32[]{:S(2)}) %collective-permute-start.4) | collective-permute-done | bytes 131104 | tf_op jit(solution)/shard_map/ppermute | solution.py:65
  22.2 1.8 %collective-permute-start.5 = (bf16[2,64,512]{2,1,0:T(8,128)(2,1)S(1)}, bf16[2,64,512]{2,1,0:T(8,128)(2,1)S(1)}, u32[]{:S(2)}, u32[]{:S(2)}) collective-permute-start(bf16[2,64,512]{2,1,0:T(8,128)(2,1)S(1)} %broadcast_select_fusion.9), channel_id=1, source_target_pairs={{0,16},{1,17},{2,10},{3,11},{4,20},{5,21},{6,14},{7,15},{8,24},{9,... | collective-permute-start | bytes 393224 | tf_op jit(solution)/shard_map/ppermute | solution.py:65
  24.0 4.3 %collective-permute-done.5 = bf16[2,64,512]{2,1,0:T(8,128)(2,1)S(1)} collective-permute-done((bf16[2,64,512]{2,1,0:T(8,128)(2,1)S(1)}, bf16[2,64,512]{2,1,0:T(8,128)(2,1)S(1)}, u32[]{:S(2)}, u32[]{:S(2)}) %collective-permute-start.5) | collective-permute-done | bytes 131104 | tf_op jit(solution)/shard_map/ppermute | solution.py:65
  28.5 1.5 %collective-permute-start.8 = (bf16[2,64,512]{2,1,0:T(8,128)(2,1)S(1)}, bf16[2,64,512]{2,1,0:T(8,128)(2,1)S(1)}, u32[]{:S(2)}, u32[]{:S(2)}) collective-permute-start(bf16[2,64,512]{2,1,0:T(8,128)(2,1)S(1)} %broadcast_select_fusion.10), channel_id=1, source_target_pairs={{0,1},{1,0},{2,3},{3,2},{4,5},{5,4},{6,7},{7,6},{8,9},{9,8},{10,11... | collective-permute-start | bytes 393224 | tf_op jit(solution)/shard_map/ppermute | solution.py:65
  30.4 1.6 %collective-permute-start.6 = (bf16[2,64,512]{2,1,0:T(8,128)(2,1)S(1)}, bf16[2,64,512]{2,1,0:T(8,128)(2,1)S(1)}, u32[]{:S(2)}, u32[]{:S(2)}) collective-permute-start(bf16[2,64,512]{2,1,0:T(8,128)(2,1)S(1)} %broadcast_select_fusion.10), channel_id=1, source_target_pairs={{0,5},{1,4},{2,7},{3,6},{4,1},{5,0},{6,3},{7,2},{8,13},{9,12},{10,... | collective-permute-start | bytes 393224 | tf_op jit(solution)/shard_map/ppermute | solution.py:65
  32.0 1.9 %collective-permute-done.8 = bf16[2,64,512]{2,1,0:T(8,128)(2,1)S(1)} collective-permute-done((bf16[2,64,512]{2,1,0:T(8,128)(2,1)S(1)}, bf16[2,64,512]{2,1,0:T(8,128)(2,1)S(1)}, u32[]{:S(2)}, u32[]{:S(2)}) %collective-permute-start.8) | collective-permute-done | bytes 131104 | tf_op jit(solution)/shard_map/ppermute | solution.py:65
  34.0 1.0 collective-permute-done.7
  34.9 1.4 %collective-permute-done.6 = bf16[2,64,512]{2,1,0:T(8,128)(2,1)S(1)} collective-permute-done((bf16[2,64,512]{2,1,0:T(8,128)(2,1)S(1)}, bf16[2,64,512]{2,1,0:T(8,128)(2,1)S(1)}, u32[]{:S(2)}, u32[]{:S(2)}) %collective-permute-start.6) | collective-permute-done | bytes 131104 | tf_op jit(solution)/shard_map/ppermute | solution.py:65
  36.5 4.0 %slabs.2 = (bf16[512,4096]{1,0:T(8,128)(2,1)S(1)}, f32[256,128]{1,0:T(8,128)S(1)}) custom-call(bf16[512,512]{1,0:T(8,128)(2,1)S(1)} %bitcast.74, bf16[4096,512]{1,0:T(8,128)(2,1)S(1)} %get-tuple-element.51.refs_1_, f32[1,4096]{1,0:T(1,128)S(1)} %get-tuple-element.52.refs_2_, f32[4096,128]{1,0:T(8,128)S(1)} %get-tuple-element.53.refs_3_.res_ref, ...), custom_call_target="tpu_custom_call" | custom-call | flops 2684354560 | bytes 12582912 | tf_op jit(solution)/shard_map/slabs/pallas_call | solution.py:354
  40.5 7.3 %slabs.3 = (bf16[512,4096]{1,0:T(8,128)(2,1)S(1)}, bf16[8,128,512]{2,1,0:T(8,128)(2,1)S(1)}) custom-call(bf16[512,512]{1,0:T(8,128)(2,1)S(1)} %collective-permute-done.9.refs_0_, bf16[4096,512]{1,0:T(8,128)(2,1)S(1)} %get-tuple-element.51.refs_1_, f32[1,4096]{1,0:T(1,128)S(1)} %get-tuple-element.52.refs_2_, ...), custom_call_target="tpu_custom_call" | custom-call | flops 4831838208 | bytes 12582912 | tf_op jit(solution)/shard_map/slabs/pallas_call | solution.py:354
  48.8 0.6 gram.1.refs_0_
  49.4 0.7 collective-permute-done.10
  50.6 1.9 %collective-permute-start.13 = (bf16[128,512]{1,0:T(8,128)(2,1)S(1)}, bf16[128,512]{1,0:T(8,128)(2,1)S(1)}, u32[]{:S(2)}, u32[]{:S(2)}) collective-permute-start(bf16[128,512]{1,0:T(8,128)(2,1)S(1)} %get-tuple-element.104), channel_id=1, source_target_pairs={{0,5},{1,4},{2,7},{3,6},{4,1},{5,0},{6,3},{7,2},{8,13},{9,12},{10,... | collective-permute-start | bytes 393224 | tf_op jit(solution)/shard_map/ppermute | solution.py:65
  52.5 1.5 %collective-permute-start.12 = (bf16[128,512]{1,0:T(8,128)(2,1)S(1)}, bf16[128,512]{1,0:T(8,128)(2,1)S(1)}, u32[]{:S(2)}, u32[]{:S(2)}) collective-permute-start(bf16[128,512]{1,0:T(8,128)(2,1)S(1)} %get-tuple-element.105), channel_id=1, source_target_pairs={{0,4},{1,5},{2,6},{3,7},{4,0},{5,1},{6,2},{7,3},{8,12},{9,13},{10,... | collective-permute-start | bytes 393224 | tf_op jit(solution)/shard_map/ppermute | solution.py:65
  54.2 5.8 %factor.4 = (f32[256,512]{1,0:T(8,128)S(1)}, f32[4096,128]{1,0:T(8,128)}) custom-call(f32[512,512]{1,0:T(8,128)S(1)} %gram.1.refs_0_, bf16[512,4096]{1,0:T(8,128)(2,1)S(1)} %get-tuple-element.58.refs_6_.slab0_ref.refs_1_, bf16[512,4096]{1,0:T(8,128)(2,1)S(1)} %get-tuple-element.61.slab1_ref.refs_2_, f32[4096,128]{1,0:T(8,128)S(1)} %get-tuple-element.54.refs_4_.refs_3_.coef_ref), custom_call_target="tpu_custom_call" | custom-call | flops 6000000000 | bytes 4194304 | tf_op jit(solution)/shard_map/factor/pallas_call | solution.py:482
  60.6 4.1 %collective-permute-start.16 = (bf16[128,512]{1,0:T(8,128)(2,1)S(1)}, bf16[128,512]{1,0:T(8,128)(2,1)S(1)}, u32[]{:S(2)}, u32[]{:S(2)}) collective-permute-start(bf16[128,512]{1,0:T(8,128)(2,1)S(1)} %pad_maximum_fusion.5), channel_id=1, source_target_pairs={{0,24},{1,25},{2,26},{3,27},{4,28},{5,29},{6,30},{7,31},{8,16},{9,... | collective-permute-start | bytes 393224 | tf_op jit(solution)/shard_map/ppermute | solution.py:65
  64.7 0.6 collective-permute-start.14
  65.3 5.8 %factor.5 = (f32[256,512]{1,0:T(8,128)S(1)}, f32[256,512]{1,0:T(8,128)S(1)}, bf16[512,512]{1,0:T(8,128)(2,1)S(1)}) custom-call(f32[512,512]{1,0:T(8,128)S(1)} %gram.1.refs_0_, bf16[512,4096]{1,0:T(8,128)(2,1)S(1)} %get-tuple-element.58.refs_6_.slab0_ref.refs_1_, bf16[512,4096]{1,0:T(8,128)(2,1)S(1)} %get-tuple-element.61.slab1_ref.refs_2_, ...), custom_call_target="tpu_custom_call" | custom-call | flops 6000000000 | bytes 4194304 | tf_op jit(solution)/shard_map/factor/pallas_call | solution.py:482
  71.7 5.7 %factor.6 = (f32[256,512]{1,0:T(8,128)S(1)}, f32[128,512]{1,0:T(8,128)S(1)}) custom-call(f32[256,512]{1,0:T(8,128)S(1)} %get-tuple-element.67.refs_0_, bf16[512,4096]{1,0:T(8,128)(2,1)S(1)} %get-tuple-element.58.refs_6_.slab0_ref.refs_1_, bf16[512,4096]{1,0:T(8,128)(2,1)S(1)} %get-tuple-element.61.slab1_ref.refs_2_, f32[256,512]{1,0:T(8,128)S(1)} %get-tuple-element.68.refs_3_), custom_call_target="tpu_custom_call" | custom-call | flops 6000000000 | bytes 4194304 | tf_op jit(solution)/shard_map/factor/pallas_call | solution.py:482
  77.8 1.6 %collective-permute-start.19 = (bf16[128,512]{1,0:T(8,128)(2,1)S(1)}, bf16[128,512]{1,0:T(8,128)(2,1)S(1)}, u32[]{:S(2)}, u32[]{:S(2)}) collective-permute-start(bf16[128,512]{1,0:T(8,128)(2,1)S(1)} %pad_maximum_fusion.6), channel_id=1, source_target_pairs={{0,5},{1,4},{2,7},{3,6},{4,1},{5,0},{6,3},{7,2},{8,13},{9,12},{10,... | collective-permute-start | bytes 393224 | tf_op jit(solution)/shard_map/ppermute | solution.py:65
  79.4 1.4 %collective-permute-start.18 = (bf16[128,512]{1,0:T(8,128)(2,1)S(1)}, bf16[128,512]{1,0:T(8,128)(2,1)S(1)}, u32[]{:S(2)}, u32[]{:S(2)}) collective-permute-start(bf16[128,512]{1,0:T(8,128)(2,1)S(1)} %pad_maximum_fusion.6), channel_id=1, source_target_pairs={{0,4},{1,5},{2,6},{3,7},{4,0},{5,1},{6,2},{7,3},{8,12},{9,13},{10,... | collective-permute-start | bytes 393224 | tf_op jit(solution)/shard_map/ppermute | solution.py:65
  80.7 0.6 collective-permute-start.17
  81.3 5.4 %factor.7 = f32[256,512]{1,0:T(8,128)S(1)} custom-call(f32[128,512]{1,0:T(8,128)S(1)} %get-tuple-element.74.refs_0_, bf16[512,4096]{1,0:T(8,128)(2,1)S(1)} %get-tuple-element.58.refs_6_.slab0_ref.refs_1_, bf16[512,4096]{1,0:T(8,128)(2,1)S(1)} %get-tuple-element.61.slab1_ref.refs_2_, f32[256,512]{1,0:T(8,128)S(1)} %get-tuple-element.75.refs_3_), custom_call_target="tpu_custom_call" | custom-call | flops 6000000000 | bytes 4194304 | tf_op jit(solution)/shard_map/factor/pallas_call | solution.py:482
  88.1 0.7 collective-permute-done.23
  88.8 0.7 collective-permute-done.20
  90.4 7.4 %finish.1 = (f32[4096,128]{1,0:T(8,128)}, f32[4096,128]{1,0:T(8,128)}) custom-call(s32[2]{0:T(128)S(1)} %copy-done.1, s32[2,4]{1,0:T(2,128)S(1)} %copy-done, s32[1]{0:T(128)} %bitcast.me_ref, s32[1]{0:T(128)} %bitcast.1.core_ref.refs_5_, bf16[8,128,512]{2,1,0:T(8,128)(2,1)S(1)} %bitcast.70, ...), custom_call_target="tpu_custom_call", output_to_operand_aliasing={{1}: (10, {})} | custom-call | flops 1073741824 | bytes 16777216 | tf_op jit(solution)/shard_map/finish/pallas_call | solution.py:611
  (87 shorter events, 7.5 us)
Async XLA Ops:
  0.6 2.7 %copy-start.1 = (s32[2]{0:T(128)S(1)}, s32[2]{0:T(128)}, u32[]{:S(2)}) copy-start(s32[2]{0:T(128)} %owner_ref.1) | copy-start | bytes 28
  2.8 2.1 %collective-permute-start = (bf16[2,256,512]{2,1,0:T(8,128)(2,1)S(1)}, bf16[2,256,512]{2,1,0:T(8,128)(2,1)S(1)}, u32[]{:S(2)}, u32[]{:S(2)}) collective-permute-start(bf16[2,256,512]{2,1,0:T(8,128)(2,1)S(1)} %get-tuple-element.42), channel_id=1, source_target_pairs={{0,2},{1,3},{2,0},{3,1},{4,6},{5,7},{6,4},{7,5},{8,10},{9,11},{10,... | collective-permute-start | bytes 1572872 | tf_op jit(solution)/shard_map/ppermute | solution.py:65
  5.1 9.1 %collective-permute-start.3 = (bf16[2,64,512]{2,1,0:T(8,128)(2,1)S(1)}, bf16[2,64,512]{2,1,0:T(8,128)(2,1)S(1)}, u32[]{:S(2)}, u32[]{:S(2)}) collective-permute-start(bf16[2,64,512]{2,1,0:T(8,128)(2,1)S(1)} %get-tuple-element.111), channel_id=1, source_target_pairs={{0,5},{1,4},{2,7},{3,6},{4,1},{5,0},{6,3},{7,2},{8,13},{9,12},{10,... | collective-permute-start | bytes 393224 | tf_op jit(solution)/shard_map/ppermute | solution.py:65
  8.9 6.6 %collective-permute-start.2 = (bf16[2,64,512]{2,1,0:T(8,128)(2,1)S(1)}, bf16[2,64,512]{2,1,0:T(8,128)(2,1)S(1)}, u32[]{:S(2)}, u32[]{:S(2)}) collective-permute-start(bf16[2,64,512]{2,1,0:T(8,128)(2,1)S(1)} %get-tuple-element.112), channel_id=1, source_target_pairs={{0,4},{1,5},{2,6},{3,7},{4,0},{5,1},{6,2},{7,3},{8,12},{9,13},{10,... | collective-permute-start | bytes 393224 | tf_op jit(solution)/shard_map/ppermute | solution.py:65
  9.4 6.4 %collective-permute-start.1 = (bf16[2,64,512]{2,1,0:T(8,128)(2,1)S(1)}, bf16[2,64,512]{2,1,0:T(8,128)(2,1)S(1)}, u32[]{:S(2)}, u32[]{:S(2)}) collective-permute-start(bf16[2,64,512]{2,1,0:T(8,128)(2,1)S(1)} %get-tuple-element.113), channel_id=1, source_target_pairs={{0,1},{1,0},{2,3},{3,2},{4,5},{5,4},{6,7},{7,6},{8,9},{9,8},{10,11... | collective-permute-start | bytes 393224 | tf_op jit(solution)/shard_map/ppermute | solution.py:65
  15.9 6.2 %collective-permute-start.4 = (bf16[2,64,512]{2,1,0:T(8,128)(2,1)S(1)}, bf16[2,64,512]{2,1,0:T(8,128)(2,1)S(1)}, u32[]{:S(2)}, u32[]{:S(2)}) collective-permute-start(bf16[2,64,512]{2,1,0:T(8,128)(2,1)S(1)} %fusion.5), channel_id=1, source_target_pairs={{0,8},{1,9},{2,18},{3,19},{4,12},{5,13},{6,22},{7,23},{8,0},{9,1},... | collective-permute-start | bytes 393224 | tf_op jit(solution)/shard_map/ppermute | solution.py:65
  22.2 6.1 %collective-permute-start.5 = (bf16[2,64,512]{2,1,0:T(8,128)(2,1)S(1)}, bf16[2,64,512]{2,1,0:T(8,128)(2,1)S(1)}, u32[]{:S(2)}, u32[]{:S(2)}) collective-permute-start(bf16[2,64,512]{2,1,0:T(8,128)(2,1)S(1)} %broadcast_select_fusion.9), channel_id=1, source_target_pairs={{0,16},{1,17},{2,10},{3,11},{4,20},{5,21},{6,14},{7,15},{8,24},{9,... | collective-permute-start | bytes 393224 | tf_op jit(solution)/shard_map/ppermute | solution.py:65
  28.5 5.5 %collective-permute-start.8 = (bf16[2,64,512]{2,1,0:T(8,128)(2,1)S(1)}, bf16[2,64,512]{2,1,0:T(8,128)(2,1)S(1)}, u32[]{:S(2)}, u32[]{:S(2)}) collective-permute-start(bf16[2,64,512]{2,1,0:T(8,128)(2,1)S(1)} %broadcast_select_fusion.10), channel_id=1, source_target_pairs={{0,1},{1,0},{2,3},{3,2},{4,5},{5,4},{6,7},{7,6},{8,9},{9,8},{10,11... | collective-permute-start | bytes 393224 | tf_op jit(solution)/shard_map/ppermute | solution.py:65
  30.0 5.0 %collective-permute-start.7 = (bf16[2,64,512]{2,1,0:T(8,128)(2,1)S(1)}, bf16[2,64,512]{2,1,0:T(8,128)(2,1)S(1)}, u32[]{:S(2)}, u32[]{:S(2)}) collective-permute-start(bf16[2,64,512]{2,1,0:T(8,128)(2,1)S(1)} %broadcast_select_fusion.10), channel_id=1, source_target_pairs={{0,4},{1,5},{2,6},{3,7},{4,0},{5,1},{6,2},{7,3},{8,12},{9,13},{10,... | collective-permute-start | bytes 393224 | tf_op jit(solution)/shard_map/ppermute | solution.py:65
  30.4 5.9 %collective-permute-start.6 = (bf16[2,64,512]{2,1,0:T(8,128)(2,1)S(1)}, bf16[2,64,512]{2,1,0:T(8,128)(2,1)S(1)}, u32[]{:S(2)}, u32[]{:S(2)}) collective-permute-start(bf16[2,64,512]{2,1,0:T(8,128)(2,1)S(1)} %broadcast_select_fusion.10), channel_id=1, source_target_pairs={{0,5},{1,4},{2,7},{3,6},{4,1},{5,0},{6,3},{7,2},{8,13},{9,12},{10,... | collective-permute-start | bytes 393224 | tf_op jit(solution)/shard_map/ppermute | solution.py:65
  36.5 4.1 %collective-permute-start.9 = (bf16[512,512]{1,0:T(8,128)(2,1)S(1)}, bf16[512,512]{1,0:T(8,128)(2,1)S(1)}, u32[]{:S(2)}, u32[]{:S(2)}) collective-permute-start(bf16[512,512]{1,0:T(8,128)(2,1)S(1)} %bitcast.73), channel_id=1, source_target_pairs={{0,2},{1,3},{2,0},{3,1},{4,6},{5,7},{6,4},{7,5},{8,10},{9,11},{10,... | collective-permute-start | bytes 1572872 | tf_op jit(solution)/shard_map/ppermute | solution.py:65
  48.0 2.1 %collective-permute-start.10 = (bf16[2,2,128,512]{3,2,1,0:T(8,128)(2,1)S(1)}, bf16[2,2,128,512]{3,2,1,0:T(8,128)(2,1)S(1)}, u32[]{:S(2)}, u32[]{:S(2)}) collective-permute-start(bf16[2,2,128,512]{3,2,1,0:T(8,128)(2,1)S(1)} %get-tuple-element.96), channel_id=1, source_target_pairs={{0,2},{1,3},{2,0},{3,1},{4,6},{5,7},{6,4},{7,5},{8,10},{9,11},{10,... | collective-permute-start | bytes 1572872 | tf_op jit(solution)/shard_map/ppermute | solution.py:65
  50.6 9.4 %collective-permute-start.13 = (bf16[128,512]{1,0:T(8,128)(2,1)S(1)}, bf16[128,512]{1,0:T(8,128)(2,1)S(1)}, u32[]{:S(2)}, u32[]{:S(2)}) collective-permute-start(bf16[128,512]{1,0:T(8,128)(2,1)S(1)} %get-tuple-element.104), channel_id=1, source_target_pairs={{0,5},{1,4},{2,7},{3,6},{4,1},{5,0},{6,3},{7,2},{8,13},{9,12},{10,... | collective-permute-start | bytes 393224 | tf_op jit(solution)/shard_map/ppermute | solution.py:65
  52.5 7.7 %collective-permute-start.12 = (bf16[128,512]{1,0:T(8,128)(2,1)S(1)}, bf16[128,512]{1,0:T(8,128)(2,1)S(1)}, u32[]{:S(2)}, u32[]{:S(2)}) collective-permute-start(bf16[128,512]{1,0:T(8,128)(2,1)S(1)} %get-tuple-element.105), channel_id=1, source_target_pairs={{0,4},{1,5},{2,6},{3,7},{4,0},{5,1},{6,2},{7,3},{8,12},{9,13},{10,... | collective-permute-start | bytes 393224 | tf_op jit(solution)/shard_map/ppermute | solution.py:65
  54.0 6.2 %collective-permute-start.11 = (bf16[128,512]{1,0:T(8,128)(2,1)S(1)}, bf16[128,512]{1,0:T(8,128)(2,1)S(1)}, u32[]{:S(2)}, u32[]{:S(2)}) collective-permute-start(bf16[128,512]{1,0:T(8,128)(2,1)S(1)} %get-tuple-element.106), channel_id=1, source_target_pairs={{0,1},{1,0},{2,3},{3,2},{4,5},{5,4},{6,7},{7,6},{8,9},{9,8},{10,11... | collective-permute-start | bytes 393224 | tf_op jit(solution)/shard_map/ppermute | solution.py:65
  60.6 16.9 %collective-permute-start.16 = (bf16[128,512]{1,0:T(8,128)(2,1)S(1)}, bf16[128,512]{1,0:T(8,128)(2,1)S(1)}, u32[]{:S(2)}, u32[]{:S(2)}) collective-permute-start(bf16[128,512]{1,0:T(8,128)(2,1)S(1)} %pad_maximum_fusion.5), channel_id=1, source_target_pairs={{0,24},{1,25},{2,26},{3,27},{4,28},{5,29},{6,30},{7,31},{8,16},{9,... | collective-permute-start | bytes 393224 | tf_op jit(solution)/shard_map/ppermute | solution.py:65
  64.7 12.7 %collective-permute-start.15 = (bf16[128,512]{1,0:T(8,128)(2,1)S(1)}, bf16[128,512]{1,0:T(8,128)(2,1)S(1)}, u32[]{:S(2)}, u32[]{:S(2)}) collective-permute-start(bf16[128,512]{1,0:T(8,128)(2,1)S(1)} %pad_maximum_fusion.5), channel_id=1, source_target_pairs={{0,16},{1,17},{2,18},{3,19},{4,20},{5,21},{6,22},{7,23},{8,24},{9,... | collective-permute-start | bytes 393224 | tf_op jit(solution)/shard_map/ppermute | solution.py:65
  64.7 12.7 %collective-permute-start.14 = (bf16[128,512]{1,0:T(8,128)(2,1)S(1)}, bf16[128,512]{1,0:T(8,128)(2,1)S(1)}, u32[]{:S(2)}, u32[]{:S(2)}) collective-permute-start(bf16[128,512]{1,0:T(8,128)(2,1)S(1)} %pad_maximum_fusion.5), channel_id=1, source_target_pairs={{0,8},{1,9},{2,10},{3,11},{4,12},{5,13},{6,14},{7,15},{8,0},{9,1},... | collective-permute-start | bytes 393224 | tf_op jit(solution)/shard_map/ppermute | solution.py:65
  71.2 16.8 %collective-permute-start.21 = (f32[256,512]{1,0:T(8,128)S(1)}, f32[256,512]{1,0:T(8,128)S(1)}, u32[]{:S(2)}, u32[]{:S(2)}) collective-permute-start(f32[256,512]{1,0:T(8,128)S(1)} %get-tuple-element.66.refs_3_), channel_id=1, source_target_pairs={{0,2},{1,3},{2,0},{3,1},{4,6},{5,7},{6,4},{7,5},{8,10},{9,11},{10,... | collective-permute-start | bytes 1572872 | tf_op jit(solution)/shard_map/ppermute | solution.py:65
  71.3 16.6 %collective-permute-start.22 = (f32[256,512]{1,0:T(8,128)S(1)}, f32[256,512]{1,0:T(8,128)S(1)}, u32[]{:S(2)}, u32[]{:S(2)}) collective-permute-start(f32[256,512]{1,0:T(8,128)S(1)} %get-tuple-element.68.refs_3_), channel_id=1, source_target_pairs={{0,2},{1,3},{2,0},{3,1},{4,6},{5,7},{6,4},{7,5},{8,10},{9,11},{10,... | collective-permute-start | bytes 1572872 | tf_op jit(solution)/shard_map/ppermute | solution.py:65
  77.8 9.0 %collective-permute-start.19 = (bf16[128,512]{1,0:T(8,128)(2,1)S(1)}, bf16[128,512]{1,0:T(8,128)(2,1)S(1)}, u32[]{:S(2)}, u32[]{:S(2)}) collective-permute-start(bf16[128,512]{1,0:T(8,128)(2,1)S(1)} %pad_maximum_fusion.6), channel_id=1, source_target_pairs={{0,5},{1,4},{2,7},{3,6},{4,1},{5,0},{6,3},{7,2},{8,13},{9,12},{10,... | collective-permute-start | bytes 393224 | tf_op jit(solution)/shard_map/ppermute | solution.py:65
  79.4 7.7 %collective-permute-start.18 = (bf16[128,512]{1,0:T(8,128)(2,1)S(1)}, bf16[128,512]{1,0:T(8,128)(2,1)S(1)}, u32[]{:S(2)}, u32[]{:S(2)}) collective-permute-start(bf16[128,512]{1,0:T(8,128)(2,1)S(1)} %pad_maximum_fusion.6), channel_id=1, source_target_pairs={{0,4},{1,5},{2,6},{3,7},{4,0},{5,1},{6,2},{7,3},{8,12},{9,13},{10,... | collective-permute-start | bytes 393224 | tf_op jit(solution)/shard_map/ppermute | solution.py:65
  80.7 6.3 %collective-permute-start.17 = (bf16[128,512]{1,0:T(8,128)(2,1)S(1)}, bf16[128,512]{1,0:T(8,128)(2,1)S(1)}, u32[]{:S(2)}, u32[]{:S(2)}) collective-permute-start(bf16[128,512]{1,0:T(8,128)(2,1)S(1)} %pad_maximum_fusion.6), channel_id=1, source_target_pairs={{0,1},{1,0},{2,3},{3,2},{4,5},{5,4},{6,7},{7,6},{8,9},{9,8},{10,11... | collective-permute-start | bytes 393224 | tf_op jit(solution)/shard_map/ppermute | solution.py:65
  86.8 2.0 %collective-permute-start.23 = (f32[256,512]{1,0:T(8,128)S(1)}, f32[256,512]{1,0:T(8,128)S(1)}, u32[]{:S(2)}, u32[]{:S(2)}) collective-permute-start(f32[256,512]{1,0:T(8,128)S(1)} %get-tuple-element.75.refs_3_), channel_id=1, source_target_pairs={{0,2},{1,3},{2,0},{3,1},{4,6},{5,7},{6,4},{7,5},{8,10},{9,11},{10,... | collective-permute-start | bytes 1572872 | tf_op jit(solution)/shard_map/ppermute | solution.py:65
  87.2 2.2 %collective-permute-start.20 = (bf16[2,2,128,512]{3,2,1,0:T(8,128)(2,1)S(1)}, bf16[2,2,128,512]{3,2,1,0:T(8,128)(2,1)S(1)}, u32[]{:S(2)}, u32[]{:S(2)}) collective-permute-start(bf16[2,2,128,512]{3,2,1,0:T(8,128)(2,1)S(1)} %bitcast.78), channel_id=1, source_target_pairs={{0,2},{1,3},{2,0},{3,1},{4,6},{5,7},{6,4},{7,5},{8,10},{9,11},{10,... | collective-permute-start | bytes 1572872 | tf_op jit(solution)/shard_map/ppermute | solution.py:65
  87.6 2.6 %collective-permute-start.24 = (f32[256,512]{1,0:T(8,128)S(1)}, f32[256,512]{1,0:T(8,128)S(1)}, u32[]{:S(2)}, u32[]{:S(2)}) collective-permute-start(f32[256,512]{1,0:T(8,128)S(1)} %factor.7), channel_id=1, source_target_pairs={{0,2},{1,3},{2,0},{3,1},{4,6},{5,7},{6,4},{7,5},{8,10},{9,11},{10,... | collective-permute-start | bytes 1572872 | tf_op jit(solution)/shard_map/ppermute | solution.py:65
  89.6 0.8 copy-start

commit v5 on v4

--- a/solution.py
+++ b/solution.py
@@ -660,10 +660,10 @@
     if spread.axes != AXES:
         pieces = pack(lax.psum(unpack(pieces, exact), "sub"), exact)
     rest = gram(block, core, scale, slab)
-    factors, before, extra = ([], []), None, []
+    kept, sent, before, extra = [], [], None, []
 
     def beside(hop, indices):
-        nonlocal before, rest
+        nonlocal before, rest, sent
         then, got = hop
         for index in indices:
             args = {0: {"copied": coefficients}, 1: {"block": block, "scale": scale}}.get(index, {})
@@ -671,11 +671,10 @@
             if args:
                 extra.append(given.pop())
             if index == indices[-1]:
-                got, mine, given = lax.optimization_barrier((got, mine, given))
+                got, mine, given, sent = lax.optimization_barrier((got, mine, given, sent))
             before, rest = mine, given[0] if given else rest
-            other = swap(mine, AXES, sub_count)
-            factors[0].append(jnp.where(on_core, other, mine))
-            factors[1].append(jnp.where(on_core, mine, other))
+            sent = sent + [swap(mine, AXES, sub_count)]
+            kept.append(mine)
         return then(got)
 
     value = spread.core_sum(pieces, exact)
@@ -683,10 +682,12 @@
     value = beside(spread.far_sum(value, exact), [1, 2])
     packed = beside(spread.near_gather(pack(value, exact)), [3])
     base, gram12 = extra
+    factors = [jnp.where(on_core, other, mine) for mine, other in zip(kept, sent)]
+    factors += [jnp.where(on_core, mine, other) for mine, other in zip(kept, sent)]
     packed = spread.core_gather(packed)
     return finish(
         block_owner, block_tiles, me.reshape(1), core, packed, gram12, slab, residual, coefficients, base,
-        factors[0] + factors[1], step_size,
+        factors, step_size,
     )
 
 

time: 98.1 us -> 97.8 us (level)
  transfers between devices with their start and end apart: 25 -> 25, of which waited for: 15 -> 14; matrix products, arithmetic and copies ran while one was open for 1% -> 1% of each run, Pallas kernels for 33% -> 33%
where the time goes in v5:
time: 97.8 us; the launch traced here: 97.7 us
  Pallas kernels  48.7 us (50%)
  starting transfers between devices  25.7 us (26%)
  waiting for transfers between devices  19.1 us (20%)
  other arithmetic  2.5 us (3%)
  between operations  1.4 us (1%)
    ppermute x25, starting transfers between devices, swap(): lax.ppermute(value, axes, [(i, i ^ flip_of(i)) for i in range(lax.axis_si...  25.7 us
    pallas_call x4, Pallas kernels, factor_step(): pl.pallas_call(functools.partial(factor_kernel, index, copied is not None...  22.7 us
    ppermute x25, waiting for transfers between devices, swap(): lax.ppermute(value, axes, [(i, i ^ flip_of(i)) for i in range(lax.axis_si...  19.1 us
    pallas_call x2, Pallas kernels, slabs(): pl.pallas_call(functools.partial(slab_kernel, scale, chunk), in_specs=in_...  11.3 us
    pallas_call x1, Pallas kernels, finish(): pl.pallas_call(functools.partial(final_kernel, step_size, chunk), in_spec...  7.37 us
    pallas_call x1, Pallas kernels, load_all(): pl.pallas_call(functools.partial(load_kernel, scale, chunk), in_specs=[hb...  4.58 us
    pallas_call x1, Pallas kernels, pick_halves(): pl.pallas_call(pick_kernel, grid_spec=pltpu.PrefetchScalarGridSpec(num_sc...  2.18 us
  transfers between devices with their start and end apart: 25, of which 14 were waited for; matrix products, arithmetic and copies ran while one was open for 1% of the time, Pallas kernels for 33%

profile of v5, /device:TPU:0, one launch (start us, length us, event | category | flops | bytes accessed | tf_op | source)
XLA Modules:
  0.0 97.7 jit_solution(14274786623059747165)
XLA Ops:
  0.6 2.2 %pick.1 = (bf16[2,256,512]{2,1,0:T(8,128)(2,1)S(1)}, bf16[2,256,512]{2,1,0:T(8,128)(2,1)S(1)}) custom-call(s32[2,4]{1,0:T(2,128)} %tiles_ref.3, s32[1]{0:T(128)} %bitcast.1.core_ref.refs_5_, bf16[4096,512]{1,0:T(8,128)(2,1)} %feat_in.1), custom_call_target="tpu_custom_call" | custom-call | tf_op jit(solution)/shard_map/pick/pallas_call | solution.py:48
  3.4 1.5 %collective-permute-done = bf16[2,256,512]{2,1,0:T(8,128)(2,1)S(1)} collective-permute-done((bf16[2,256,512]{2,1,0:T(8,128)(2,1)S(1)}, bf16[2,256,512]{2,1,0:T(8,128)(2,1)S(1)}, u32[]{:S(2)}, u32[]{:S(2)}) %collective-permute-start) | collective-permute-done | bytes 524320 | tf_op jit(solution)/shard_map/ppermute | solution.py:65
  5.1 3.9 %collective-permute-start.3 = (bf16[2,64,512]{2,1,0:T(8,128)(2,1)S(1)}, bf16[2,64,512]{2,1,0:T(8,128)(2,1)S(1)}, u32[]{:S(2)}, u32[]{:S(2)}) collective-permute-start(bf16[2,64,512]{2,1,0:T(8,128)(2,1)S(1)} %get-tuple-element.121), channel_id=1, source_target_pairs={{0,5},{1,4},{2,7},{3,6},{4,1},{5,0},{6,3},{7,2},{8,13},{9,12},{10,... | collective-permute-start | bytes 393224 | tf_op jit(solution)/shard_map/ppermute | solution.py:65
  9.6 4.6 %load.1 = (f32[1,4096]{1,0:T(1,128)S(1)}, bf16[4096,512]{1,0:T(8,128)(2,1)S(1)}, f32[4096,128]{1,0:T(8,128)S(1)}, f32[4096,128]{1,0:T(8,128)S(1)}) custom-call(bf16[4096,512]{1,0:T(8,128)(2,1)} %feat_in.1, f32[4096,128]{1,0:T(8,128)} %res_in.1, f32[4096,128]{1,0:T(8,128)} %coef_in.1), custom_call_target="tpu_custom_call" | custom-call | flops 3000000000 | bytes 8388608 | tf_op jit(solution)/shard_map/load/pallas_call | solution.py:242
  14.2 1.4 %collective-permute-done.2 = bf16[2,64,512]{2,1,0:T(8,128)(2,1)S(1)} collective-permute-done((bf16[2,64,512]{2,1,0:T(8,128)(2,1)S(1)}, bf16[2,64,512]{2,1,0:T(8,128)(2,1)S(1)}, u32[]{:S(2)}, u32[]{:S(2)}) %collective-permute-start.2) | collective-permute-done | bytes 131104 | tf_op jit(solution)/shard_map/ppermute | solution.py:65
  15.9 1.6 %collective-permute-start.4 = (bf16[2,64,512]{2,1,0:T(8,128)(2,1)S(1)}, bf16[2,64,512]{2,1,0:T(8,128)(2,1)S(1)}, u32[]{:S(2)}, u32[]{:S(2)}) collective-permute-start(bf16[2,64,512]{2,1,0:T(8,128)(2,1)S(1)} %fusion.5), channel_id=1, source_target_pairs={{0,8},{1,9},{2,18},{3,19},{4,12},{5,13},{6,22},{7,23},{8,0},{9,1},... | collective-permute-start | bytes 393224 | tf_op jit(solution)/shard_map/ppermute | solution.py:65
  17.6 4.6 %collective-permute-done.4 = bf16[2,64,512]{2,1,0:T(8,128)(2,1)S(1)} collective-permute-done((bf16[2,64,512]{2,1,0:T(8,128)(2,1)S(1)}, bf16[2,64,512]{2,1,0:T(8,128)(2,1)S(1)}, u32[]{:S(2)}, u32[]{:S(2)}) %collective-permute-start.4) | collective-permute-done | bytes 131104 | tf_op jit(solution)/shard_map/ppermute | solution.py:65
  22.2 1.8 %collective-permute-start.5 = (bf16[2,64,512]{2,1,0:T(8,128)(2,1)S(1)}, bf16[2,64,512]{2,1,0:T(8,128)(2,1)S(1)}, u32[]{:S(2)}, u32[]{:S(2)}) collective-permute-start(bf16[2,64,512]{2,1,0:T(8,128)(2,1)S(1)} %broadcast_select_fusion.9), channel_id=1, source_target_pairs={{0,16},{1,17},{2,10},{3,11},{4,20},{5,21},{6,14},{7,15},{8,24},{9,... | collective-permute-start | bytes 393224 | tf_op jit(solution)/shard_map/ppermute | solution.py:65
  24.0 4.3 %collective-permute-done.5 = bf16[2,64,512]{2,1,0:T(8,128)(2,1)S(1)} collective-permute-done((bf16[2,64,512]{2,1,0:T(8,128)(2,1)S(1)}, bf16[2,64,512]{2,1,0:T(8,128)(2,1)S(1)}, u32[]{:S(2)}, u32[]{:S(2)}) %collective-permute-start.5) | collective-permute-done | bytes 131104 | tf_op jit(solution)/shard_map/ppermute | solution.py:65
  28.5 1.5 %collective-permute-start.8 = (bf16[2,64,512]{2,1,0:T(8,128)(2,1)S(1)}, bf16[2,64,512]{2,1,0:T(8,128)(2,1)S(1)}, u32[]{:S(2)}, u32[]{:S(2)}) collective-permute-start(bf16[2,64,512]{2,1,0:T(8,128)(2,1)S(1)} %broadcast_select_fusion.10), channel_id=1, source_target_pairs={{0,1},{1,0},{2,3},{3,2},{4,5},{5,4},{6,7},{7,6},{8,9},{9,8},{10,11... | collective-permute-start | bytes 393224 | tf_op jit(solution)/shard_map/ppermute | solution.py:65
  30.4 1.6 %collective-permute-start.6 = (bf16[2,64,512]{2,1,0:T(8,128)(2,1)S(1)}, bf16[2,64,512]{2,1,0:T(8,128)(2,1)S(1)}, u32[]{:S(2)}, u32[]{:S(2)}) collective-permute-start(bf16[2,64,512]{2,1,0:T(8,128)(2,1)S(1)} %broadcast_select_fusion.10), channel_id=1, source_target_pairs={{0,5},{1,4},{2,7},{3,6},{4,1},{5,0},{6,3},{7,2},{8,13},{9,12},{10,... | collective-permute-start | bytes 393224 | tf_op jit(solution)/shard_map/ppermute | solution.py:65
  32.0 1.9 %collective-permute-done.8 = bf16[2,64,512]{2,1,0:T(8,128)(2,1)S(1)} collective-permute-done((bf16[2,64,512]{2,1,0:T(8,128)(2,1)S(1)}, bf16[2,64,512]{2,1,0:T(8,128)(2,1)S(1)}, u32[]{:S(2)}, u32[]{:S(2)}) %collective-permute-start.8) | collective-permute-done | bytes 131104 | tf_op jit(solution)/shard_map/ppermute | solution.py:65
  34.0 1.0 %collective-permute-done.7 = bf16[2,64,512]{2,1,0:T(8,128)(2,1)S(1)} collective-permute-done((bf16[2,64,512]{2,1,0:T(8,128)(2,1)S(1)}, bf16[2,64,512]{2,1,0:T(8,128)(2,1)S(1)}, u32[]{:S(2)}, u32[]{:S(2)}) %collective-permute-start.7) | collective-permute-done | bytes 131104 | tf_op jit(solution)/shard_map/ppermute | solution.py:65
  34.9 1.4 %collective-permute-done.6 = bf16[2,64,512]{2,1,0:T(8,128)(2,1)S(1)} collective-permute-done((bf16[2,64,512]{2,1,0:T(8,128)(2,1)S(1)}, bf16[2,64,512]{2,1,0:T(8,128)(2,1)S(1)}, u32[]{:S(2)}, u32[]{:S(2)}) %collective-permute-start.6) | collective-permute-done | bytes 131104 | tf_op jit(solution)/shard_map/ppermute | solution.py:65
  36.5 4.0 %slabs.2 = (bf16[512,4096]{1,0:T(8,128)(2,1)S(1)}, f32[256,128]{1,0:T(8,128)S(1)}) custom-call(bf16[512,512]{1,0:T(8,128)(2,1)S(1)} %bitcast.74, bf16[4096,512]{1,0:T(8,128)(2,1)S(1)} %get-tuple-element.56.refs_1_, f32[1,4096]{1,0:T(1,128)S(1)} %get-tuple-element.57.refs_2_, f32[4096,128]{1,0:T(8,128)S(1)} %get-tuple-element.58.refs_3_.res_ref, ...), custom_call_target="tpu_custom_call" | custom-call | flops 2684354560 | bytes 12582912 | tf_op jit(solution)/shard_map/slabs/pallas_call | solution.py:354
  40.5 7.3 %slabs.3 = (bf16[512,4096]{1,0:T(8,128)(2,1)S(1)}, bf16[8,128,512]{2,1,0:T(8,128)(2,1)S(1)}) custom-call(bf16[512,512]{1,0:T(8,128)(2,1)S(1)} %collective-permute-done.9.refs_0_, bf16[4096,512]{1,0:T(8,128)(2,1)S(1)} %get-tuple-element.56.refs_1_, f32[1,4096]{1,0:T(1,128)S(1)} %get-tuple-element.57.refs_2_, ...), custom_call_target="tpu_custom_call" | custom-call | flops 4831838208 | bytes 12582912 | tf_op jit(solution)/shard_map/slabs/pallas_call | solution.py:354
  48.0 0.6 collective-permute-start.10
  48.8 0.6 gram.1.refs_0_
  49.4 0.7 collective-permute-done.10
  50.6 1.9 %collective-permute-start.13 = (bf16[128,512]{1,0:T(8,128)(2,1)S(1)}, bf16[128,512]{1,0:T(8,128)(2,1)S(1)}, u32[]{:S(2)}, u32[]{:S(2)}) collective-permute-start(bf16[128,512]{1,0:T(8,128)(2,1)S(1)} %get-tuple-element.114), channel_id=1, source_target_pairs={{0,5},{1,4},{2,7},{3,6},{4,1},{5,0},{6,3},{7,2},{8,13},{9,12},{10,... | collective-permute-start | bytes 393224 | tf_op jit(solution)/shard_map/ppermute | solution.py:65
  52.5 1.5 %collective-permute-start.12 = (bf16[128,512]{1,0:T(8,128)(2,1)S(1)}, bf16[128,512]{1,0:T(8,128)(2,1)S(1)}, u32[]{:S(2)}, u32[]{:S(2)}) collective-permute-start(bf16[128,512]{1,0:T(8,128)(2,1)S(1)} %get-tuple-element.115), channel_id=1, source_target_pairs={{0,4},{1,5},{2,6},{3,7},{4,0},{5,1},{6,2},{7,3},{8,12},{9,13},{10,... | collective-permute-start | bytes 393224 | tf_op jit(solution)/shard_map/ppermute | solution.py:65
  54.2 5.8 %factor.4 = (f32[256,512]{1,0:T(8,128)S(1)}, f32[4096,128]{1,0:T(8,128)}) custom-call(f32[512,512]{1,0:T(8,128)S(1)} %gram.1.refs_0_, bf16[512,4096]{1,0:T(8,128)(2,1)S(1)} %get-tuple-element.63.refs_6_.slab0_ref.refs_1_, bf16[512,4096]{1,0:T(8,128)(2,1)S(1)} %get-tuple-element.66.slab1_ref.refs_2_, f32[4096,128]{1,0:T(8,128)S(1)} %get-tuple-element.59.refs_4_.refs_3_.coef_ref), custom_call_target="tpu_custom_call" | custom-call | flops 6000000000 | bytes 4194304 | tf_op jit(solution)/shard_map/factor/pallas_call | solution.py:482
  60.6 4.1 %collective-permute-start.16 = (bf16[128,512]{1,0:T(8,128)(2,1)S(1)}, bf16[128,512]{1,0:T(8,128)(2,1)S(1)}, u32[]{:S(2)}, u32[]{:S(2)}) collective-permute-start(bf16[128,512]{1,0:T(8,128)(2,1)S(1)} %pad_maximum_fusion.5), channel_id=1, source_target_pairs={{0,24},{1,25},{2,26},{3,27},{4,28},{5,29},{6,30},{7,31},{8,16},{9,... | collective-permute-start | bytes 393224 | tf_op jit(solution)/shard_map/ppermute | solution.py:65
  64.7 0.6 collective-permute-start.14
  65.4 5.8 %factor.5 = (f32[256,512]{1,0:T(8,128)S(1)}, f32[256,512]{1,0:T(8,128)S(1)}, bf16[512,512]{1,0:T(8,128)(2,1)S(1)}) custom-call(f32[512,512]{1,0:T(8,128)S(1)} %gram.1.refs_0_, bf16[512,4096]{1,0:T(8,128)(2,1)S(1)} %get-tuple-element.63.refs_6_.slab0_ref.refs_1_, bf16[512,4096]{1,0:T(8,128)(2,1)S(1)} %get-tuple-element.66.slab1_ref.refs_2_, ...), custom_call_target="tpu_custom_call" | custom-call | flops 6000000000 | bytes 4194304 | tf_op jit(solution)/shard_map/factor/pallas_call | solution.py:482
  71.8 5.7 %factor.6 = (f32[256,512]{1,0:T(8,128)S(1)}, f32[128,512]{1,0:T(8,128)S(1)}) custom-call(f32[256,512]{1,0:T(8,128)S(1)} %get-tuple-element.72.refs_0_, bf16[512,4096]{1,0:T(8,128)(2,1)S(1)} %get-tuple-element.63.refs_6_.slab0_ref.refs_1_, bf16[512,4096]{1,0:T(8,128)(2,1)S(1)} %get-tuple-element.66.slab1_ref.refs_2_, f32[256,512]{1,0:T(8,128)S(1)} %get-tuple-element.73.refs_3_), custom_call_target="tpu_custom_call" | custom-call | flops 6000000000 | bytes 4194304 | tf_op jit(solution)/shard_map/factor/pallas_call | solution.py:482
  77.8 1.6 %collective-permute-start.21 = (bf16[128,512]{1,0:T(8,128)(2,1)S(1)}, bf16[128,512]{1,0:T(8,128)(2,1)S(1)}, u32[]{:S(2)}, u32[]{:S(2)}) collective-permute-start(bf16[128,512]{1,0:T(8,128)(2,1)S(1)} %pad_maximum_fusion.6), channel_id=1, source_target_pairs={{0,5},{1,4},{2,7},{3,6},{4,1},{5,0},{6,3},{7,2},{8,13},{9,12},{10,... | collective-permute-start | bytes 393224 | tf_op jit(solution)/shard_map/ppermute | solution.py:65
  79.4 1.4 %collective-permute-start.20 = (bf16[128,512]{1,0:T(8,128)(2,1)S(1)}, bf16[128,512]{1,0:T(8,128)(2,1)S(1)}, u32[]{:S(2)}, u32[]{:S(2)}) collective-permute-start(bf16[128,512]{1,0:T(8,128)(2,1)S(1)} %pad_maximum_fusion.6), channel_id=1, source_target_pairs={{0,4},{1,5},{2,6},{3,7},{4,0},{5,1},{6,2},{7,3},{8,12},{9,13},{10,... | collective-permute-start | bytes 393224 | tf_op jit(solution)/shard_map/ppermute | solution.py:65
  80.7 0.6 collective-permute-start.19
  81.4 5.4 %factor.7 = f32[256,512]{1,0:T(8,128)S(1)} custom-call(f32[128,512]{1,0:T(8,128)S(1)} %get-tuple-element.79.refs_0_, bf16[512,4096]{1,0:T(8,128)(2,1)S(1)} %get-tuple-element.63.refs_6_.slab0_ref.refs_1_, bf16[512,4096]{1,0:T(8,128)(2,1)S(1)} %get-tuple-element.66.slab1_ref.refs_2_, f32[256,512]{1,0:T(8,128)S(1)} %get-tuple-element.80.refs_3_), custom_call_target="tpu_custom_call" | custom-call | flops 6000000000 | bytes 4194304 | tf_op jit(solution)/shard_map/factor/pallas_call | solution.py:482
  88.3 0.9 collective-permute-done.23
  90.1 7.4 %finish.1 = (f32[4096,128]{1,0:T(8,128)}, f32[4096,128]{1,0:T(8,128)}) custom-call(s32[2]{0:T(128)S(1)} %copy-done.1, s32[2,4]{1,0:T(2,128)S(1)} %copy-done, s32[1]{0:T(128)} %bitcast.me_ref, s32[1]{0:T(128)} %bitcast.1.core_ref.refs_5_, bf16[8,128,512]{2,1,0:T(8,128)(2,1)S(1)} %bitcast.70, ...), custom_call_target="tpu_custom_call", output_to_operand_aliasing={{1}: (10, {})} | custom-call | flops 1073741824 | bytes 16777216 | tf_op jit(solution)/shard_map/finish/pallas_call | solution.py:611
  (87 shorter events, 7.1 us)
Async XLA Ops:
  0.6 2.7 %copy-start.1 = (s32[2]{0:T(128)S(1)}, s32[2]{0:T(128)}, u32[]{:S(2)}) copy-start(s32[2]{0:T(128)} %owner_ref.1) | copy-start | bytes 28
  2.8 2.1 %collective-permute-start = (bf16[2,256,512]{2,1,0:T(8,128)(2,1)S(1)}, bf16[2,256,512]{2,1,0:T(8,128)(2,1)S(1)}, u32[]{:S(2)}, u32[]{:S(2)}) collective-permute-start(bf16[2,256,512]{2,1,0:T(8,128)(2,1)S(1)} %get-tuple-element.47), channel_id=1, source_target_pairs={{0,2},{1,3},{2,0},{3,1},{4,6},{5,7},{6,4},{7,5},{8,10},{9,11},{10,... | collective-permute-start | bytes 1572872 | tf_op jit(solution)/shard_map/ppermute | solution.py:65
  5.1 9.1 %collective-permute-start.3 = (bf16[2,64,512]{2,1,0:T(8,128)(2,1)S(1)}, bf16[2,64,512]{2,1,0:T(8,128)(2,1)S(1)}, u32[]{:S(2)}, u32[]{:S(2)}) collective-permute-start(bf16[2,64,512]{2,1,0:T(8,128)(2,1)S(1)} %get-tuple-element.121), channel_id=1, source_target_pairs={{0,5},{1,4},{2,7},{3,6},{4,1},{5,0},{6,3},{7,2},{8,13},{9,12},{10,... | collective-permute-start | bytes 393224 | tf_op jit(solution)/shard_map/ppermute | solution.py:65
  8.9 6.6 %collective-permute-start.2 = (bf16[2,64,512]{2,1,0:T(8,128)(2,1)S(1)}, bf16[2,64,512]{2,1,0:T(8,128)(2,1)S(1)}, u32[]{:S(2)}, u32[]{:S(2)}) collective-permute-start(bf16[2,64,512]{2,1,0:T(8,128)(2,1)S(1)} %get-tuple-element.122), channel_id=1, source_target_pairs={{0,4},{1,5},{2,6},{3,7},{4,0},{5,1},{6,2},{7,3},{8,12},{9,13},{10,... | collective-permute-start | bytes 393224 | tf_op jit(solution)/shard_map/ppermute | solution.py:65
  9.4 6.4 %collective-permute-start.1 = (bf16[2,64,512]{2,1,0:T(8,128)(2,1)S(1)}, bf16[2,64,512]{2,1,0:T(8,128)(2,1)S(1)}, u32[]{:S(2)}, u32[]{:S(2)}) collective-permute-start(bf16[2,64,512]{2,1,0:T(8,128)(2,1)S(1)} %get-tuple-element.123), channel_id=1, source_target_pairs={{0,1},{1,0},{2,3},{3,2},{4,5},{5,4},{6,7},{7,6},{8,9},{9,8},{10,11... | collective-permute-start | bytes 393224 | tf_op jit(solution)/shard_map/ppermute | solution.py:65
  15.9 6.2 %collective-permute-start.4 = (bf16[2,64,512]{2,1,0:T(8,128)(2,1)S(1)}, bf16[2,64,512]{2,1,0:T(8,128)(2,1)S(1)}, u32[]{:S(2)}, u32[]{:S(2)}) collective-permute-start(bf16[2,64,512]{2,1,0:T(8,128)(2,1)S(1)} %fusion.5), channel_id=1, source_target_pairs={{0,8},{1,9},{2,18},{3,19},{4,12},{5,13},{6,22},{7,23},{8,0},{9,1},... | collective-permute-start | bytes 393224 | tf_op jit(solution)/shard_map/ppermute | solution.py:65
  22.2 6.1 %collective-permute-start.5 = (bf16[2,64,512]{2,1,0:T(8,128)(2,1)S(1)}, bf16[2,64,512]{2,1,0:T(8,128)(2,1)S(1)}, u32[]{:S(2)}, u32[]{:S(2)}) collective-permute-start(bf16[2,64,512]{2,1,0:T(8,128)(2,1)S(1)} %broadcast_select_fusion.9), channel_id=1, source_target_pairs={{0,16},{1,17},{2,10},{3,11},{4,20},{5,21},{6,14},{7,15},{8,24},{9,... | collective-permute-start | bytes 393224 | tf_op jit(solution)/shard_map/ppermute | solution.py:65
  28.5 5.5 %collective-permute-start.8 = (bf16[2,64,512]{2,1,0:T(8,128)(2,1)S(1)}, bf16[2,64,512]{2,1,0:T(8,128)(2,1)S(1)}, u32[]{:S(2)}, u32[]{:S(2)}) collective-permute-start(bf16[2,64,512]{2,1,0:T(8,128)(2,1)S(1)} %broadcast_select_fusion.10), channel_id=1, source_target_pairs={{0,1},{1,0},{2,3},{3,2},{4,5},{5,4},{6,7},{7,6},{8,9},{9,8},{10,11... | collective-permute-start | bytes 393224 | tf_op jit(solution)/shard_map/ppermute | solution.py:65
  30.0 5.0 %collective-permute-start.7 = (bf16[2,64,512]{2,1,0:T(8,128)(2,1)S(1)}, bf16[2,64,512]{2,1,0:T(8,128)(2,1)S(1)}, u32[]{:S(2)}, u32[]{:S(2)}) collective-permute-start(bf16[2,64,512]{2,1,0:T(8,128)(2,1)S(1)} %broadcast_select_fusion.10), channel_id=1, source_target_pairs={{0,4},{1,5},{2,6},{3,7},{4,0},{5,1},{6,2},{7,3},{8,12},{9,13},{10,... | collective-permute-start | bytes 393224 | tf_op jit(solution)/shard_map/ppermute | solution.py:65
  30.4 5.9 %collective-permute-start.6 = (bf16[2,64,512]{2,1,0:T(8,128)(2,1)S(1)}, bf16[2,64,512]{2,1,0:T(8,128)(2,1)S(1)}, u32[]{:S(2)}, u32[]{:S(2)}) collective-permute-start(bf16[2,64,512]{2,1,0:T(8,128)(2,1)S(1)} %broadcast_select_fusion.10), channel_id=1, source_target_pairs={{0,5},{1,4},{2,7},{3,6},{4,1},{5,0},{6,3},{7,2},{8,13},{9,12},{10,... | collective-permute-start | bytes 393224 | tf_op jit(solution)/shard_map/ppermute | solution.py:65
  36.5 4.1 %collective-permute-start.9 = (bf16[512,512]{1,0:T(8,128)(2,1)S(1)}, bf16[512,512]{1,0:T(8,128)(2,1)S(1)}, u32[]{:S(2)}, u32[]{:S(2)}) collective-permute-start(bf16[512,512]{1,0:T(8,128)(2,1)S(1)} %bitcast.73), channel_id=1, source_target_pairs={{0,2},{1,3},{2,0},{3,1},{4,6},{5,7},{6,4},{7,5},{8,10},{9,11},{10,... | collective-permute-start | bytes 1572872 | tf_op jit(solution)/shard_map/ppermute | solution.py:65
  48.0 2.1 %collective-permute-start.10 = (bf16[2,2,128,512]{3,2,1,0:T(8,128)(2,1)S(1)}, bf16[2,2,128,512]{3,2,1,0:T(8,128)(2,1)S(1)}, u32[]{:S(2)}, u32[]{:S(2)}) collective-permute-start(bf16[2,2,128,512]{3,2,1,0:T(8,128)(2,1)S(1)} %get-tuple-element.106), channel_id=1, source_target_pairs={{0,2},{1,3},{2,0},{3,1},{4,6},{5,7},{6,4},{7,5},{8,10},{9,11},{10,... | collective-permute-start | bytes 1572872 | tf_op jit(solution)/shard_map/ppermute | solution.py:65
  50.6 9.4 %collective-permute-start.13 = (bf16[128,512]{1,0:T(8,128)(2,1)S(1)}, bf16[128,512]{1,0:T(8,128)(2,1)S(1)}, u32[]{:S(2)}, u32[]{:S(2)}) collective-permute-start(bf16[128,512]{1,0:T(8,128)(2,1)S(1)} %get-tuple-element.114), channel_id=1, source_target_pairs={{0,5},{1,4},{2,7},{3,6},{4,1},{5,0},{6,3},{7,2},{8,13},{9,12},{10,... | collective-permute-start | bytes 393224 | tf_op jit(solution)/shard_map/ppermute | solution.py:65
  52.5 7.7 %collective-permute-start.12 = (bf16[128,512]{1,0:T(8,128)(2,1)S(1)}, bf16[128,512]{1,0:T(8,128)(2,1)S(1)}, u32[]{:S(2)}, u32[]{:S(2)}) collective-permute-start(bf16[128,512]{1,0:T(8,128)(2,1)S(1)} %get-tuple-element.115), channel_id=1, source_target_pairs={{0,4},{1,5},{2,6},{3,7},{4,0},{5,1},{6,2},{7,3},{8,12},{9,13},{10,... | collective-permute-start | bytes 393224 | tf_op jit(solution)/shard_map/ppermute | solution.py:65
  54.0 6.2 %collective-permute-start.11 = (bf16[128,512]{1,0:T(8,128)(2,1)S(1)}, bf16[128,512]{1,0:T(8,128)(2,1)S(1)}, u32[]{:S(2)}, u32[]{:S(2)}) collective-permute-start(bf16[128,512]{1,0:T(8,128)(2,1)S(1)} %get-tuple-element.116), channel_id=1, source_target_pairs={{0,1},{1,0},{2,3},{3,2},{4,5},{5,4},{6,7},{7,6},{8,9},{9,8},{10,11... | collective-permute-start | bytes 393224 | tf_op jit(solution)/shard_map/ppermute | solution.py:65
  60.6 16.8 %collective-permute-start.16 = (bf16[128,512]{1,0:T(8,128)(2,1)S(1)}, bf16[128,512]{1,0:T(8,128)(2,1)S(1)}, u32[]{:S(2)}, u32[]{:S(2)}) collective-permute-start(bf16[128,512]{1,0:T(8,128)(2,1)S(1)} %pad_maximum_fusion.5), channel_id=1, source_target_pairs={{0,24},{1,25},{2,26},{3,27},{4,28},{5,29},{6,30},{7,31},{8,16},{9,... | collective-permute-start | bytes 393224 | tf_op jit(solution)/shard_map/ppermute | solution.py:65
  64.7 12.7 %collective-permute-start.15 = (bf16[128,512]{1,0:T(8,128)(2,1)S(1)}, bf16[128,512]{1,0:T(8,128)(2,1)S(1)}, u32[]{:S(2)}, u32[]{:S(2)}) collective-permute-start(bf16[128,512]{1,0:T(8,128)(2,1)S(1)} %pad_maximum_fusion.5), channel_id=1, source_target_pairs={{0,16},{1,17},{2,18},{3,19},{4,20},{5,21},{6,22},{7,23},{8,24},{9,... | collective-permute-start | bytes 393224 | tf_op jit(solution)/shard_map/ppermute | solution.py:65
  64.7 12.7 %collective-permute-start.14 = (bf16[128,512]{1,0:T(8,128)(2,1)S(1)}, bf16[128,512]{1,0:T(8,128)(2,1)S(1)}, u32[]{:S(2)}, u32[]{:S(2)}) collective-permute-start(bf16[128,512]{1,0:T(8,128)(2,1)S(1)} %pad_maximum_fusion.5), channel_id=1, source_target_pairs={{0,8},{1,9},{2,10},{3,11},{4,12},{5,13},{6,14},{7,15},{8,0},{9,1},... | collective-permute-start | bytes 393224 | tf_op jit(solution)/shard_map/ppermute | solution.py:65
  71.2 6.3 %collective-permute-start.17 = (f32[256,512]{1,0:T(8,128)S(1)}, f32[256,512]{1,0:T(8,128)S(1)}, u32[]{:S(2)}, u32[]{:S(2)}) collective-permute-start(f32[256,512]{1,0:T(8,128)S(1)} %get-tuple-element.71.refs_3_), channel_id=1, source_target_pairs={{0,2},{1,3},{2,0},{3,1},{4,6},{5,7},{6,4},{7,5},{8,10},{9,11},{10,... | collective-permute-start | bytes 1572872 | tf_op jit(solution)/shard_map/ppermute | solution.py:65
  71.3 6.2 %collective-permute-start.18 = (f32[256,512]{1,0:T(8,128)S(1)}, f32[256,512]{1,0:T(8,128)S(1)}, u32[]{:S(2)}, u32[]{:S(2)}) collective-permute-start(f32[256,512]{1,0:T(8,128)S(1)} %get-tuple-element.73.refs_3_), channel_id=1, source_target_pairs={{0,2},{1,3},{2,0},{3,1},{4,6},{5,7},{6,4},{7,5},{8,10},{9,11},{10,... | collective-permute-start | bytes 1572872 | tf_op jit(solution)/shard_map/ppermute | solution.py:65
  77.8 9.0 %collective-permute-start.21 = (bf16[128,512]{1,0:T(8,128)(2,1)S(1)}, bf16[128,512]{1,0:T(8,128)(2,1)S(1)}, u32[]{:S(2)}, u32[]{:S(2)}) collective-permute-start(bf16[128,512]{1,0:T(8,128)(2,1)S(1)} %pad_maximum_fusion.6), channel_id=1, source_target_pairs={{0,5},{1,4},{2,7},{3,6},{4,1},{5,0},{6,3},{7,2},{8,13},{9,12},{10,... | collective-permute-start | bytes 393224 | tf_op jit(solution)/shard_map/ppermute | solution.py:65
  79.4 7.7 %collective-permute-start.20 = (bf16[128,512]{1,0:T(8,128)(2,1)S(1)}, bf16[128,512]{1,0:T(8,128)(2,1)S(1)}, u32[]{:S(2)}, u32[]{:S(2)}) collective-permute-start(bf16[128,512]{1,0:T(8,128)(2,1)S(1)} %pad_maximum_fusion.6), channel_id=1, source_target_pairs={{0,4},{1,5},{2,6},{3,7},{4,0},{5,1},{6,2},{7,3},{8,12},{9,13},{10,... | collective-permute-start | bytes 393224 | tf_op jit(solution)/shard_map/ppermute | solution.py:65
  80.7 6.3 %collective-permute-start.19 = (bf16[128,512]{1,0:T(8,128)(2,1)S(1)}, bf16[128,512]{1,0:T(8,128)(2,1)S(1)}, u32[]{:S(2)}, u32[]{:S(2)}) collective-permute-start(bf16[128,512]{1,0:T(8,128)(2,1)S(1)} %pad_maximum_fusion.6), channel_id=1, source_target_pairs={{0,1},{1,0},{2,3},{3,2},{4,5},{5,4},{6,7},{7,6},{8,9},{9,8},{10,11... | collective-permute-start | bytes 393224 | tf_op jit(solution)/shard_map/ppermute | solution.py:65
  81.3 5.7 %collective-permute-start.22 = (f32[256,512]{1,0:T(8,128)S(1)}, f32[256,512]{1,0:T(8,128)S(1)}, u32[]{:S(2)}, u32[]{:S(2)}) collective-permute-start(f32[256,512]{1,0:T(8,128)S(1)} %get-tuple-element.80.refs_3_), channel_id=1, source_target_pairs={{0,2},{1,3},{2,0},{3,1},{4,6},{5,7},{6,4},{7,5},{8,10},{9,11},{10,... | collective-permute-start | bytes 1572872 | tf_op jit(solution)/shard_map/ppermute | solution.py:65
  87.3 2.0 %collective-permute-start.23 = (bf16[2,2,128,512]{3,2,1,0:T(8,128)(2,1)S(1)}, bf16[2,2,128,512]{3,2,1,0:T(8,128)(2,1)S(1)}, u32[]{:S(2)}, u32[]{:S(2)}) collective-permute-start(bf16[2,2,128,512]{3,2,1,0:T(8,128)(2,1)S(1)} %bitcast.78), channel_id=1, source_target_pairs={{0,2},{1,3},{2,0},{3,1},{4,6},{5,7},{6,4},{7,5},{8,10},{9,11},{10,... | collective-permute-start | bytes 1572872 | tf_op jit(solution)/shard_map/ppermute | solution.py:65
  87.6 2.4 %collective-permute-start.24 = (f32[256,512]{1,0:T(8,128)S(1)}, f32[256,512]{1,0:T(8,128)S(1)}, u32[]{:S(2)}, u32[]{:S(2)}) collective-permute-start(f32[256,512]{1,0:T(8,128)S(1)} %factor.7), channel_id=1, source_target_pairs={{0,2},{1,3},{2,0},{3,1},{4,6},{5,7},{6,4},{7,5},{8,10},{9,11},{10,... | collective-permute-start | bytes 1572872 | tf_op jit(solution)/shard_map/ppermute | solution.py:65
  89.4 0.7 copy-start

commit v6 on v5

--- a/solution.py
+++ b/solution.py
@@ -297,7 +297,7 @@
             )
         return 0
 
-    lax.fori_loop(0, chunks, body, 0, unroll=2)
+    lax.fori_loop(0, chunks, body, 0, unroll=4)
     if not second:
         refs[6][...] = grad[...]
         return
@@ -592,7 +592,7 @@
         res_copy(i).start()
         return 0
 
-    lax.fori_loop(0, chunks, body, 0)
+    lax.fori_loop(0, chunks, body, 0, unroll=2)
     for i in range(rows // chunk):
         res_copy(i).wait()
     for s in range(STEPS):

time: 97.8 us -> 96.6 us (0.988)
  Pallas kernels: 48.7 us -> 47.5 us
where the time goes in v6:
time: 96.6 us; the launch traced here: 96.5 us
  Pallas kernels  47.5 us (49%)
  starting transfers between devices  25.7 us (27%)
  waiting for transfers between devices  19.1 us (20%)
  other arithmetic  2.5 us (3%)
  between operations  1.4 us (1%)
    ppermute x25, starting transfers between devices, swap(): lax.ppermute(value, axes, [(i, i ^ flip_of(i)) for i in range(lax.axis_si...  25.7 us
    pallas_call x4, Pallas kernels, factor_step(): pl.pallas_call(functools.partial(factor_kernel, index, copied is not None...  22.7 us
    ppermute x25, waiting for transfers between devices, swap(): lax.ppermute(value, axes, [(i, i ^ flip_of(i)) for i in range(lax.axis_si...  19.1 us
    pallas_call x2, Pallas kernels, slabs(): pl.pallas_call(functools.partial(slab_kernel, scale, chunk), in_specs=in_...  10.6 us
    pallas_call x1, Pallas kernels, finish(): pl.pallas_call(functools.partial(final_kernel, step_size, chunk), in_spec...  6.85 us
    pallas_call x1, Pallas kernels, load_all(): pl.pallas_call(functools.partial(load_kernel, scale, chunk), in_specs=[hb...  4.58 us
    pallas_call x1, Pallas kernels, pick_halves(): pl.pallas_call(pick_kernel, grid_spec=pltpu.PrefetchScalarGridSpec(num_sc...  2.18 us
  transfers between devices with their start and end apart: 25, of which 14 were waited for; matrix products, arithmetic and copies ran while one was open for 1% of the time, Pallas kernels for 33%

profile of v6, /device:TPU:0, one launch (start us, length us, event | category | flops | bytes accessed | tf_op | source)
XLA Modules:
  0.0 96.5 jit_solution(9397087794753321088)
XLA Ops:
  0.6 2.2 %pick.1 = (bf16[2,256,512]{2,1,0:T(8,128)(2,1)S(1)}, bf16[2,256,512]{2,1,0:T(8,128)(2,1)S(1)}) custom-call(s32[2,4]{1,0:T(2,128)} %tiles_ref.3, s32[1]{0:T(128)} %bitcast.1.core_ref.refs_5_, bf16[4096,512]{1,0:T(8,128)(2,1)} %feat_in.1), custom_call_target="tpu_custom_call" | custom-call | tf_op jit(solution)/shard_map/pick/pallas_call | solution.py:48
  3.4 1.5 %collective-permute-done = bf16[2,256,512]{2,1,0:T(8,128)(2,1)S(1)} collective-permute-done((bf16[2,256,512]{2,1,0:T(8,128)(2,1)S(1)}, bf16[2,256,512]{2,1,0:T(8,128)(2,1)S(1)}, u32[]{:S(2)}, u32[]{:S(2)}) %collective-permute-start) | collective-permute-done | bytes 524320 | tf_op jit(solution)/shard_map/ppermute | solution.py:65
  5.1 3.9 %collective-permute-start.3 = (bf16[2,64,512]{2,1,0:T(8,128)(2,1)S(1)}, bf16[2,64,512]{2,1,0:T(8,128)(2,1)S(1)}, u32[]{:S(2)}, u32[]{:S(2)}) collective-permute-start(bf16[2,64,512]{2,1,0:T(8,128)(2,1)S(1)} %get-tuple-element.121), channel_id=1, source_target_pairs={{0,5},{1,4},{2,7},{3,6},{4,1},{5,0},{6,3},{7,2},{8,13},{9,12},{10,... | collective-permute-start | bytes 393224 | tf_op jit(solution)/shard_map/ppermute | solution.py:65
  9.6 4.6 %load.1 = (f32[1,4096]{1,0:T(1,128)S(1)}, bf16[4096,512]{1,0:T(8,128)(2,1)S(1)}, f32[4096,128]{1,0:T(8,128)S(1)}, f32[4096,128]{1,0:T(8,128)S(1)}) custom-call(bf16[4096,512]{1,0:T(8,128)(2,1)} %feat_in.1, f32[4096,128]{1,0:T(8,128)} %res_in.1, f32[4096,128]{1,0:T(8,128)} %coef_in.1), custom_call_target="tpu_custom_call" | custom-call | flops 3000000000 | bytes 8388608 | tf_op jit(solution)/shard_map/load/pallas_call | solution.py:242
  14.2 1.4 %collective-permute-done.2 = bf16[2,64,512]{2,1,0:T(8,128)(2,1)S(1)} collective-permute-done((bf16[2,64,512]{2,1,0:T(8,128)(2,1)S(1)}, bf16[2,64,512]{2,1,0:T(8,128)(2,1)S(1)}, u32[]{:S(2)}, u32[]{:S(2)}) %collective-permute-start.2) | collective-permute-done | bytes 131104 | tf_op jit(solution)/shard_map/ppermute | solution.py:65
  15.9 1.6 %collective-permute-start.4 = (bf16[2,64,512]{2,1,0:T(8,128)(2,1)S(1)}, bf16[2,64,512]{2,1,0:T(8,128)(2,1)S(1)}, u32[]{:S(2)}, u32[]{:S(2)}) collective-permute-start(bf16[2,64,512]{2,1,0:T(8,128)(2,1)S(1)} %fusion.5), channel_id=1, source_target_pairs={{0,8},{1,9},{2,18},{3,19},{4,12},{5,13},{6,22},{7,23},{8,0},{9,1},... | collective-permute-start | bytes 393224 | tf_op jit(solution)/shard_map/ppermute | solution.py:65
  17.6 4.6 %collective-permute-done.4 = bf16[2,64,512]{2,1,0:T(8,128)(2,1)S(1)} collective-permute-done((bf16[2,64,512]{2,1,0:T(8,128)(2,1)S(1)}, bf16[2,64,512]{2,1,0:T(8,128)(2,1)S(1)}, u32[]{:S(2)}, u32[]{:S(2)}) %collective-permute-start.4) | collective-permute-done | bytes 131104 | tf_op jit(solution)/shard_map/ppermute | solution.py:65
  22.2 1.8 %collective-permute-start.5 = (bf16[2,64,512]{2,1,0:T(8,128)(2,1)S(1)}, bf16[2,64,512]{2,1,0:T(8,128)(2,1)S(1)}, u32[]{:S(2)}, u32[]{:S(2)}) collective-permute-start(bf16[2,64,512]{2,1,0:T(8,128)(2,1)S(1)} %broadcast_select_fusion.9), channel_id=1, source_target_pairs={{0,16},{1,17},{2,10},{3,11},{4,20},{5,21},{6,14},{7,15},{8,24},{9,... | collective-permute-start | bytes 393224 | tf_op jit(solution)/shard_map/ppermute | solution.py:65
  24.0 4.3 %collective-permute-done.5 = bf16[2,64,512]{2,1,0:T(8,128)(2,1)S(1)} collective-permute-done((bf16[2,64,512]{2,1,0:T(8,128)(2,1)S(1)}, bf16[2,64,512]{2,1,0:T(8,128)(2,1)S(1)}, u32[]{:S(2)}, u32[]{:S(2)}) %collective-permute-start.5) | collective-permute-done | bytes 131104 | tf_op jit(solution)/shard_map/ppermute | solution.py:65
  28.5 1.5 %collective-permute-start.8 = (bf16[2,64,512]{2,1,0:T(8,128)(2,1)S(1)}, bf16[2,64,512]{2,1,0:T(8,128)(2,1)S(1)}, u32[]{:S(2)}, u32[]{:S(2)}) collective-permute-start(bf16[2,64,512]{2,1,0:T(8,128)(2,1)S(1)} %broadcast_select_fusion.10), channel_id=1, source_target_pairs={{0,1},{1,0},{2,3},{3,2},{4,5},{5,4},{6,7},{7,6},{8,9},{9,8},{10,11... | collective-permute-start | bytes 393224 | tf_op jit(solution)/shard_map/ppermute | solution.py:65
  30.4 1.6 %collective-permute-start.6 = (bf16[2,64,512]{2,1,0:T(8,128)(2,1)S(1)}, bf16[2,64,512]{2,1,0:T(8,128)(2,1)S(1)}, u32[]{:S(2)}, u32[]{:S(2)}) collective-permute-start(bf16[2,64,512]{2,1,0:T(8,128)(2,1)S(1)} %broadcast_select_fusion.10), channel_id=1, source_target_pairs={{0,5},{1,4},{2,7},{3,6},{4,1},{5,0},{6,3},{7,2},{8,13},{9,12},{10,... | collective-permute-start | bytes 393224 | tf_op jit(solution)/shard_map/ppermute | solution.py:65
  32.0 1.9 %collective-permute-done.8 = bf16[2,64,512]{2,1,0:T(8,128)(2,1)S(1)} collective-permute-done((bf16[2,64,512]{2,1,0:T(8,128)(2,1)S(1)}, bf16[2,64,512]{2,1,0:T(8,128)(2,1)S(1)}, u32[]{:S(2)}, u32[]{:S(2)}) %collective-permute-start.8) | collective-permute-done | bytes 131104 | tf_op jit(solution)/shard_map/ppermute | solution.py:65
  34.0 1.0 %collective-permute-done.7 = bf16[2,64,512]{2,1,0:T(8,128)(2,1)S(1)} collective-permute-done((bf16[2,64,512]{2,1,0:T(8,128)(2,1)S(1)}, bf16[2,64,512]{2,1,0:T(8,128)(2,1)S(1)}, u32[]{:S(2)}, u32[]{:S(2)}) %collective-permute-start.7) | collective-permute-done | bytes 131104 | tf_op jit(solution)/shard_map/ppermute | solution.py:65
  34.9 1.4 %collective-permute-done.6 = bf16[2,64,512]{2,1,0:T(8,128)(2,1)S(1)} collective-permute-done((bf16[2,64,512]{2,1,0:T(8,128)(2,1)S(1)}, bf16[2,64,512]{2,1,0:T(8,128)(2,1)S(1)}, u32[]{:S(2)}, u32[]{:S(2)}) %collective-permute-start.6) | collective-permute-done | bytes 131104 | tf_op jit(solution)/shard_map/ppermute | solution.py:65
  36.5 3.6 %slabs.2 = (bf16[512,4096]{1,0:T(8,128)(2,1)S(1)}, f32[256,128]{1,0:T(8,128)S(1)}) custom-call(bf16[512,512]{1,0:T(8,128)(2,1)S(1)} %bitcast.74, bf16[4096,512]{1,0:T(8,128)(2,1)S(1)} %get-tuple-element.56.refs_1_, f32[1,4096]{1,0:T(1,128)S(1)} %get-tuple-element.57.refs_2_, f32[4096,128]{1,0:T(8,128)S(1)} %get-tuple-element.58.refs_3_.res_ref, ...), custom_call_target="tpu_custom_call" | custom-call | flops 2684354560 | bytes 12582912 | tf_op jit(solution)/shard_map/slabs/pallas_call | solution.py:354
  40.2 7.0 %slabs.3 = (bf16[512,4096]{1,0:T(8,128)(2,1)S(1)}, bf16[8,128,512]{2,1,0:T(8,128)(2,1)S(1)}) custom-call(bf16[512,512]{1,0:T(8,128)(2,1)S(1)} %collective-permute-done.9.refs_0_, bf16[4096,512]{1,0:T(8,128)(2,1)S(1)} %get-tuple-element.56.refs_1_, f32[1,4096]{1,0:T(1,128)S(1)} %get-tuple-element.57.refs_2_, ...), custom_call_target="tpu_custom_call" | custom-call | flops 4831838208 | bytes 12582912 | tf_op jit(solution)/shard_map/slabs/pallas_call | solution.py:354
  47.3 0.6 collective-permute-start.10
  48.1 0.6 gram.1.refs_0_
  48.7 0.7 collective-permute-done.10
  49.9 1.9 %collective-permute-start.13 = (bf16[128,512]{1,0:T(8,128)(2,1)S(1)}, bf16[128,512]{1,0:T(8,128)(2,1)S(1)}, u32[]{:S(2)}, u32[]{:S(2)}) collective-permute-start(bf16[128,512]{1,0:T(8,128)(2,1)S(1)} %get-tuple-element.114), channel_id=1, source_target_pairs={{0,5},{1,4},{2,7},{3,6},{4,1},{5,0},{6,3},{7,2},{8,13},{9,12},{10,... | collective-permute-start | bytes 393224 | tf_op jit(solution)/shard_map/ppermute | solution.py:65
  51.8 1.5 %collective-permute-start.12 = (bf16[128,512]{1,0:T(8,128)(2,1)S(1)}, bf16[128,512]{1,0:T(8,128)(2,1)S(1)}, u32[]{:S(2)}, u32[]{:S(2)}) collective-permute-start(bf16[128,512]{1,0:T(8,128)(2,1)S(1)} %get-tuple-element.115), channel_id=1, source_target_pairs={{0,4},{1,5},{2,6},{3,7},{4,0},{5,1},{6,2},{7,3},{8,12},{9,13},{10,... | collective-permute-start | bytes 393224 | tf_op jit(solution)/shard_map/ppermute | solution.py:65
  53.5 5.8 %factor.4 = (f32[256,512]{1,0:T(8,128)S(1)}, f32[4096,128]{1,0:T(8,128)}) custom-call(f32[512,512]{1,0:T(8,128)S(1)} %gram.1.refs_0_, bf16[512,4096]{1,0:T(8,128)(2,1)S(1)} %get-tuple-element.63.refs_6_.slab0_ref.refs_1_, bf16[512,4096]{1,0:T(8,128)(2,1)S(1)} %get-tuple-element.66.slab1_ref.refs_2_, f32[4096,128]{1,0:T(8,128)S(1)} %get-tuple-element.59.refs_4_.refs_3_.coef_ref), custom_call_target="tpu_custom_call" | custom-call | flops 6000000000 | bytes 4194304 | tf_op jit(solution)/shard_map/factor/pallas_call | solution.py:482
  59.9 4.1 %collective-permute-start.16 = (bf16[128,512]{1,0:T(8,128)(2,1)S(1)}, bf16[128,512]{1,0:T(8,128)(2,1)S(1)}, u32[]{:S(2)}, u32[]{:S(2)}) collective-permute-start(bf16[128,512]{1,0:T(8,128)(2,1)S(1)} %pad_maximum_fusion.5), channel_id=1, source_target_pairs={{0,24},{1,25},{2,26},{3,27},{4,28},{5,29},{6,30},{7,31},{8,16},{9,... | collective-permute-start | bytes 393224 | tf_op jit(solution)/shard_map/ppermute | solution.py:65
  64.0 0.6 collective-permute-start.14
  64.7 5.8 %factor.5 = (f32[256,512]{1,0:T(8,128)S(1)}, f32[256,512]{1,0:T(8,128)S(1)}, bf16[512,512]{1,0:T(8,128)(2,1)S(1)}) custom-call(f32[512,512]{1,0:T(8,128)S(1)} %gram.1.refs_0_, bf16[512,4096]{1,0:T(8,128)(2,1)S(1)} %get-tuple-element.63.refs_6_.slab0_ref.refs_1_, bf16[512,4096]{1,0:T(8,128)(2,1)S(1)} %get-tuple-element.66.slab1_ref.refs_2_, ...), custom_call_target="tpu_custom_call" | custom-call | flops 6000000000 | bytes 4194304 | tf_op jit(solution)/shard_map/factor/pallas_call | solution.py:482
  71.1 5.7 %factor.6 = (f32[256,512]{1,0:T(8,128)S(1)}, f32[128,512]{1,0:T(8,128)S(1)}) custom-call(f32[256,512]{1,0:T(8,128)S(1)} %get-tuple-element.72.refs_0_, bf16[512,4096]{1,0:T(8,128)(2,1)S(1)} %get-tuple-element.63.refs_6_.slab0_ref.refs_1_, bf16[512,4096]{1,0:T(8,128)(2,1)S(1)} %get-tuple-element.66.slab1_ref.refs_2_, f32[256,512]{1,0:T(8,128)S(1)} %get-tuple-element.73.refs_3_), custom_call_target="tpu_custom_call" | custom-call | flops 6000000000 | bytes 4194304 | tf_op jit(solution)/shard_map/factor/pallas_call | solution.py:482
  77.1 1.6 %collective-permute-start.21 = (bf16[128,512]{1,0:T(8,128)(2,1)S(1)}, bf16[128,512]{1,0:T(8,128)(2,1)S(1)}, u32[]{:S(2)}, u32[]{:S(2)}) collective-permute-start(bf16[128,512]{1,0:T(8,128)(2,1)S(1)} %pad_maximum_fusion.6), channel_id=1, source_target_pairs={{0,5},{1,4},{2,7},{3,6},{4,1},{5,0},{6,3},{7,2},{8,13},{9,12},{10,... | collective-permute-start | bytes 393224 | tf_op jit(solution)/shard_map/ppermute | solution.py:65
  78.7 1.4 %collective-permute-start.20 = (bf16[128,512]{1,0:T(8,128)(2,1)S(1)}, bf16[128,512]{1,0:T(8,128)(2,1)S(1)}, u32[]{:S(2)}, u32[]{:S(2)}) collective-permute-start(bf16[128,512]{1,0:T(8,128)(2,1)S(1)} %pad_maximum_fusion.6), channel_id=1, source_target_pairs={{0,4},{1,5},{2,6},{3,7},{4,0},{5,1},{6,2},{7,3},{8,12},{9,13},{10,... | collective-permute-start | bytes 393224 | tf_op jit(solution)/shard_map/ppermute | solution.py:65
  80.0 0.6 collective-permute-start.19
  80.7 5.4 %factor.7 = f32[256,512]{1,0:T(8,128)S(1)} custom-call(f32[128,512]{1,0:T(8,128)S(1)} %get-tuple-element.79.refs_0_, bf16[512,4096]{1,0:T(8,128)(2,1)S(1)} %get-tuple-element.63.refs_6_.slab0_ref.refs_1_, bf16[512,4096]{1,0:T(8,128)(2,1)S(1)} %get-tuple-element.66.slab1_ref.refs_2_, f32[256,512]{1,0:T(8,128)S(1)} %get-tuple-element.80.refs_3_), custom_call_target="tpu_custom_call" | custom-call | flops 6000000000 | bytes 4194304 | tf_op jit(solution)/shard_map/factor/pallas_call | solution.py:482
  87.6 0.9 collective-permute-done.23
  89.4 6.9 %finish.1 = (f32[4096,128]{1,0:T(8,128)}, f32[4096,128]{1,0:T(8,128)}) custom-call(s32[2]{0:T(128)S(1)} %copy-done.1, s32[2,4]{1,0:T(2,128)S(1)} %copy-done, s32[1]{0:T(128)} %bitcast.me_ref, s32[1]{0:T(128)} %bitcast.1.core_ref.refs_5_, bf16[8,128,512]{2,1,0:T(8,128)(2,1)S(1)} %bitcast.70, ...), custom_call_target="tpu_custom_call", output_to_operand_aliasing={{1}: (10, {})} | custom-call | flops 1073741824 | bytes 16777216 | tf_op jit(solution)/shard_map/finish/pallas_call | solution.py:611
  (87 shorter events, 7.1 us)
Async XLA Ops:
  0.6 2.7 %copy-start.1 = (s32[2]{0:T(128)S(1)}, s32[2]{0:T(128)}, u32[]{:S(2)}) copy-start(s32[2]{0:T(128)} %owner_ref.1) | copy-start | bytes 28
  2.8 2.1 %collective-permute-start = (bf16[2,256,512]{2,1,0:T(8,128)(2,1)S(1)}, bf16[2,256,512]{2,1,0:T(8,128)(2,1)S(1)}, u32[]{:S(2)}, u32[]{:S(2)}) collective-permute-start(bf16[2,256,512]{2,1,0:T(8,128)(2,1)S(1)} %get-tuple-element.47), channel_id=1, source_target_pairs={{0,2},{1,3},{2,0},{3,1},{4,6},{5,7},{6,4},{7,5},{8,10},{9,11},{10,... | collective-permute-start | bytes 1572872 | tf_op jit(solution)/shard_map/ppermute | solution.py:65
  5.1 9.1 %collective-permute-start.3 = (bf16[2,64,512]{2,1,0:T(8,128)(2,1)S(1)}, bf16[2,64,512]{2,1,0:T(8,128)(2,1)S(1)}, u32[]{:S(2)}, u32[]{:S(2)}) collective-permute-start(bf16[2,64,512]{2,1,0:T(8,128)(2,1)S(1)} %get-tuple-element.121), channel_id=1, source_target_pairs={{0,5},{1,4},{2,7},{3,6},{4,1},{5,0},{6,3},{7,2},{8,13},{9,12},{10,... | collective-permute-start | bytes 393224 | tf_op jit(solution)/shard_map/ppermute | solution.py:65
  8.9 6.6 %collective-permute-start.2 = (bf16[2,64,512]{2,1,0:T(8,128)(2,1)S(1)}, bf16[2,64,512]{2,1,0:T(8,128)(2,1)S(1)}, u32[]{:S(2)}, u32[]{:S(2)}) collective-permute-start(bf16[2,64,512]{2,1,0:T(8,128)(2,1)S(1)} %get-tuple-element.122), channel_id=1, source_target_pairs={{0,4},{1,5},{2,6},{3,7},{4,0},{5,1},{6,2},{7,3},{8,12},{9,13},{10,... | collective-permute-start | bytes 393224 | tf_op jit(solution)/shard_map/ppermute | solution.py:65
  9.4 6.4 %collective-permute-start.1 = (bf16[2,64,512]{2,1,0:T(8,128)(2,1)S(1)}, bf16[2,64,512]{2,1,0:T(8,128)(2,1)S(1)}, u32[]{:S(2)}, u32[]{:S(2)}) collective-permute-start(bf16[2,64,512]{2,1,0:T(8,128)(2,1)S(1)} %get-tuple-element.123), channel_id=1, source_target_pairs={{0,1},{1,0},{2,3},{3,2},{4,5},{5,4},{6,7},{7,6},{8,9},{9,8},{10,11... | collective-permute-start | bytes 393224 | tf_op jit(solution)/shard_map/ppermute | solution.py:65
  15.9 6.2 %collective-permute-start.4 = (bf16[2,64,512]{2,1,0:T(8,128)(2,1)S(1)}, bf16[2,64,512]{2,1,0:T(8,128)(2,1)S(1)}, u32[]{:S(2)}, u32[]{:S(2)}) collective-permute-start(bf16[2,64,512]{2,1,0:T(8,128)(2,1)S(1)} %fusion.5), channel_id=1, source_target_pairs={{0,8},{1,9},{2,18},{3,19},{4,12},{5,13},{6,22},{7,23},{8,0},{9,1},... | collective-permute-start | bytes 393224 | tf_op jit(solution)/shard_map/ppermute | solution.py:65
  22.2 6.1 %collective-permute-start.5 = (bf16[2,64,512]{2,1,0:T(8,128)(2,1)S(1)}, bf16[2,64,512]{2,1,0:T(8,128)(2,1)S(1)}, u32[]{:S(2)}, u32[]{:S(2)}) collective-permute-start(bf16[2,64,512]{2,1,0:T(8,128)(2,1)S(1)} %broadcast_select_fusion.9), channel_id=1, source_target_pairs={{0,16},{1,17},{2,10},{3,11},{4,20},{5,21},{6,14},{7,15},{8,24},{9,... | collective-permute-start | bytes 393224 | tf_op jit(solution)/shard_map/ppermute | solution.py:65
  28.5 5.5 %collective-permute-start.8 = (bf16[2,64,512]{2,1,0:T(8,128)(2,1)S(1)}, bf16[2,64,512]{2,1,0:T(8,128)(2,1)S(1)}, u32[]{:S(2)}, u32[]{:S(2)}) collective-permute-start(bf16[2,64,512]{2,1,0:T(8,128)(2,1)S(1)} %broadcast_select_fusion.10), channel_id=1, source_target_pairs={{0,1},{1,0},{2,3},{3,2},{4,5},{5,4},{6,7},{7,6},{8,9},{9,8},{10,11... | collective-permute-start | bytes 393224 | tf_op jit(solution)/shard_map/ppermute | solution.py:65
  30.0 5.0 %collective-permute-start.7 = (bf16[2,64,512]{2,1,0:T(8,128)(2,1)S(1)}, bf16[2,64,512]{2,1,0:T(8,128)(2,1)S(1)}, u32[]{:S(2)}, u32[]{:S(2)}) collective-permute-start(bf16[2,64,512]{2,1,0:T(8,128)(2,1)S(1)} %broadcast_select_fusion.10), channel_id=1, source_target_pairs={{0,4},{1,5},{2,6},{3,7},{4,0},{5,1},{6,2},{7,3},{8,12},{9,13},{10,... | collective-permute-start | bytes 393224 | tf_op jit(solution)/shard_map/ppermute | solution.py:65
  30.4 5.9 %collective-permute-start.6 = (bf16[2,64,512]{2,1,0:T(8,128)(2,1)S(1)}, bf16[2,64,512]{2,1,0:T(8,128)(2,1)S(1)}, u32[]{:S(2)}, u32[]{:S(2)}) collective-permute-start(bf16[2,64,512]{2,1,0:T(8,128)(2,1)S(1)} %broadcast_select_fusion.10), channel_id=1, source_target_pairs={{0,5},{1,4},{2,7},{3,6},{4,1},{5,0},{6,3},{7,2},{8,13},{9,12},{10,... | collective-permute-start | bytes 393224 | tf_op jit(solution)/shard_map/ppermute | solution.py:65
  36.5 3.7 %collective-permute-start.9 = (bf16[512,512]{1,0:T(8,128)(2,1)S(1)}, bf16[512,512]{1,0:T(8,128)(2,1)S(1)}, u32[]{:S(2)}, u32[]{:S(2)}) collective-permute-start(bf16[512,512]{1,0:T(8,128)(2,1)S(1)} %bitcast.73), channel_id=1, source_target_pairs={{0,2},{1,3},{2,0},{3,1},{4,6},{5,7},{6,4},{7,5},{8,10},{9,11},{10,... | collective-permute-start | bytes 1572872 | tf_op jit(solution)/shard_map/ppermute | solution.py:65
  47.3 2.1 %collective-permute-start.10 = (bf16[2,2,128,512]{3,2,1,0:T(8,128)(2,1)S(1)}, bf16[2,2,128,512]{3,2,1,0:T(8,128)(2,1)S(1)}, u32[]{:S(2)}, u32[]{:S(2)}) collective-permute-start(bf16[2,2,128,512]{3,2,1,0:T(8,128)(2,1)S(1)} %get-tuple-element.106), channel_id=1, source_target_pairs={{0,2},{1,3},{2,0},{3,1},{4,6},{5,7},{6,4},{7,5},{8,10},{9,11},{10,... | collective-permute-start | bytes 1572872 | tf_op jit(solution)/shard_map/ppermute | solution.py:65
  49.9 9.4 %collective-permute-start.13 = (bf16[128,512]{1,0:T(8,128)(2,1)S(1)}, bf16[128,512]{1,0:T(8,128)(2,1)S(1)}, u32[]{:S(2)}, u32[]{:S(2)}) collective-permute-start(bf16[128,512]{1,0:T(8,128)(2,1)S(1)} %get-tuple-element.114), channel_id=1, source_target_pairs={{0,5},{1,4},{2,7},{3,6},{4,1},{5,0},{6,3},{7,2},{8,13},{9,12},{10,... | collective-permute-start | bytes 393224 | tf_op jit(solution)/shard_map/ppermute | solution.py:65
  51.8 7.7 %collective-permute-start.12 = (bf16[128,512]{1,0:T(8,128)(2,1)S(1)}, bf16[128,512]{1,0:T(8,128)(2,1)S(1)}, u32[]{:S(2)}, u32[]{:S(2)}) collective-permute-start(bf16[128,512]{1,0:T(8,128)(2,1)S(1)} %get-tuple-element.115), channel_id=1, source_target_pairs={{0,4},{1,5},{2,6},{3,7},{4,0},{5,1},{6,2},{7,3},{8,12},{9,13},{10,... | collective-permute-start | bytes 393224 | tf_op jit(solution)/shard_map/ppermute | solution.py:65
  53.4 6.2 %collective-permute-start.11 = (bf16[128,512]{1,0:T(8,128)(2,1)S(1)}, bf16[128,512]{1,0:T(8,128)(2,1)S(1)}, u32[]{:S(2)}, u32[]{:S(2)}) collective-permute-start(bf16[128,512]{1,0:T(8,128)(2,1)S(1)} %get-tuple-element.116), channel_id=1, source_target_pairs={{0,1},{1,0},{2,3},{3,2},{4,5},{5,4},{6,7},{7,6},{8,9},{9,8},{10,11... | collective-permute-start | bytes 393224 | tf_op jit(solution)/shard_map/ppermute | solution.py:65
  59.9 16.9 %collective-permute-start.16 = (bf16[128,512]{1,0:T(8,128)(2,1)S(1)}, bf16[128,512]{1,0:T(8,128)(2,1)S(1)}, u32[]{:S(2)}, u32[]{:S(2)}) collective-permute-start(bf16[128,512]{1,0:T(8,128)(2,1)S(1)} %pad_maximum_fusion.5), channel_id=1, source_target_pairs={{0,24},{1,25},{2,26},{3,27},{4,28},{5,29},{6,30},{7,31},{8,16},{9,... | collective-permute-start | bytes 393224 | tf_op jit(solution)/shard_map/ppermute | solution.py:65
  64.0 12.7 %collective-permute-start.15 = (bf16[128,512]{1,0:T(8,128)(2,1)S(1)}, bf16[128,512]{1,0:T(8,128)(2,1)S(1)}, u32[]{:S(2)}, u32[]{:S(2)}) collective-permute-start(bf16[128,512]{1,0:T(8,128)(2,1)S(1)} %pad_maximum_fusion.5), channel_id=1, source_target_pairs={{0,16},{1,17},{2,18},{3,19},{4,20},{5,21},{6,22},{7,23},{8,24},{9,... | collective-permute-start | bytes 393224 | tf_op jit(solution)/shard_map/ppermute | solution.py:65
  64.0 12.7 %collective-permute-start.14 = (bf16[128,512]{1,0:T(8,128)(2,1)S(1)}, bf16[128,512]{1,0:T(8,128)(2,1)S(1)}, u32[]{:S(2)}, u32[]{:S(2)}) collective-permute-start(bf16[128,512]{1,0:T(8,128)(2,1)S(1)} %pad_maximum_fusion.5), channel_id=1, source_target_pairs={{0,8},{1,9},{2,10},{3,11},{4,12},{5,13},{6,14},{7,15},{8,0},{9,1},... | collective-permute-start | bytes 393224 | tf_op jit(solution)/shard_map/ppermute | solution.py:65
  70.5 6.3 %collective-permute-start.17 = (f32[256,512]{1,0:T(8,128)S(1)}, f32[256,512]{1,0:T(8,128)S(1)}, u32[]{:S(2)}, u32[]{:S(2)}) collective-permute-start(f32[256,512]{1,0:T(8,128)S(1)} %get-tuple-element.71.refs_3_), channel_id=1, source_target_pairs={{0,2},{1,3},{2,0},{3,1},{4,6},{5,7},{6,4},{7,5},{8,10},{9,11},{10,... | collective-permute-start | bytes 1572872 | tf_op jit(solution)/shard_map/ppermute | solution.py:65
  70.6 6.2 %collective-permute-start.18 = (f32[256,512]{1,0:T(8,128)S(1)}, f32[256,512]{1,0:T(8,128)S(1)}, u32[]{:S(2)}, u32[]{:S(2)}) collective-permute-start(f32[256,512]{1,0:T(8,128)S(1)} %get-tuple-element.73.refs_3_), channel_id=1, source_target_pairs={{0,2},{1,3},{2,0},{3,1},{4,6},{5,7},{6,4},{7,5},{8,10},{9,11},{10,... | collective-permute-start | bytes 1572872 | tf_op jit(solution)/shard_map/ppermute | solution.py:65
  77.1 9.0 %collective-permute-start.21 = (bf16[128,512]{1,0:T(8,128)(2,1)S(1)}, bf16[128,512]{1,0:T(8,128)(2,1)S(1)}, u32[]{:S(2)}, u32[]{:S(2)}) collective-permute-start(bf16[128,512]{1,0:T(8,128)(2,1)S(1)} %pad_maximum_fusion.6), channel_id=1, source_target_pairs={{0,5},{1,4},{2,7},{3,6},{4,1},{5,0},{6,3},{7,2},{8,13},{9,12},{10,... | collective-permute-start | bytes 393224 | tf_op jit(solution)/shard_map/ppermute | solution.py:65
  78.7 7.7 %collective-permute-start.20 = (bf16[128,512]{1,0:T(8,128)(2,1)S(1)}, bf16[128,512]{1,0:T(8,128)(2,1)S(1)}, u32[]{:S(2)}, u32[]{:S(2)}) collective-permute-start(bf16[128,512]{1,0:T(8,128)(2,1)S(1)} %pad_maximum_fusion.6), channel_id=1, source_target_pairs={{0,4},{1,5},{2,6},{3,7},{4,0},{5,1},{6,2},{7,3},{8,12},{9,13},{10,... | collective-permute-start | bytes 393224 | tf_op jit(solution)/shard_map/ppermute | solution.py:65
  80.0 6.3 %collective-permute-start.19 = (bf16[128,512]{1,0:T(8,128)(2,1)S(1)}, bf16[128,512]{1,0:T(8,128)(2,1)S(1)}, u32[]{:S(2)}, u32[]{:S(2)}) collective-permute-start(bf16[128,512]{1,0:T(8,128)(2,1)S(1)} %pad_maximum_fusion.6), channel_id=1, source_target_pairs={{0,1},{1,0},{2,3},{3,2},{4,5},{5,4},{6,7},{7,6},{8,9},{9,8},{10,11... | collective-permute-start | bytes 393224 | tf_op jit(solution)/shard_map/ppermute | solution.py:65
  80.7 5.7 %collective-permute-start.22 = (f32[256,512]{1,0:T(8,128)S(1)}, f32[256,512]{1,0:T(8,128)S(1)}, u32[]{:S(2)}, u32[]{:S(2)}) collective-permute-start(f32[256,512]{1,0:T(8,128)S(1)} %get-tuple-element.80.refs_3_), channel_id=1, source_target_pairs={{0,2},{1,3},{2,0},{3,1},{4,6},{5,7},{6,4},{7,5},{8,10},{9,11},{10,... | collective-permute-start | bytes 1572872 | tf_op jit(solution)/shard_map/ppermute | solution.py:65
  86.6 2.0 %collective-permute-start.23 = (bf16[2,2,128,512]{3,2,1,0:T(8,128)(2,1)S(1)}, bf16[2,2,128,512]{3,2,1,0:T(8,128)(2,1)S(1)}, u32[]{:S(2)}, u32[]{:S(2)}) collective-permute-start(bf16[2,2,128,512]{3,2,1,0:T(8,128)(2,1)S(1)} %bitcast.78), channel_id=1, source_target_pairs={{0,2},{1,3},{2,0},{3,1},{4,6},{5,7},{6,4},{7,5},{8,10},{9,11},{10,... | collective-permute-start | bytes 1572872 | tf_op jit(solution)/shard_map/ppermute | solution.py:65
  86.9 2.4 %collective-permute-start.24 = (f32[256,512]{1,0:T(8,128)S(1)}, f32[256,512]{1,0:T(8,128)S(1)}, u32[]{:S(2)}, u32[]{:S(2)}) collective-permute-start(f32[256,512]{1,0:T(8,128)S(1)} %factor.7), channel_id=1, source_target_pairs={{0,2},{1,3},{2,0},{3,1},{4,6},{5,7},{6,4},{7,5},{8,10},{9,11},{10,... | collective-permute-start | bytes 1572872 | tf_op jit(solution)/shard_map/ppermute | solution.py:65
  88.7 0.7 copy-start

commit v7 on v6

--- a/solution.py
+++ b/solution.py
@@ -592,7 +592,7 @@
         res_copy(i).start()
         return 0
 
-    lax.fori_loop(0, chunks, body, 0, unroll=2)
+    lax.fori_loop(0, chunks, body, 0, unroll=4)
     for i in range(rows // chunk):
         res_copy(i).wait()
     for s in range(STEPS):

time: 96.6 us -> 96.3 us (level)
  no operation moved by 1% of the time
where the time goes in v7:
time: 96.3 us; the launch traced here: 96.1 us
  Pallas kernels  47.2 us (49%)
  starting transfers between devices  25.7 us (27%)
  waiting for transfers between devices  19.1 us (20%)
  other arithmetic  2.5 us (3%)
  between operations  1.4 us (1%)
    ppermute x25, starting transfers between devices, swap(): lax.ppermute(value, axes, [(i, i ^ flip_of(i)) for i in range(lax.axis_si...  25.7 us
    pallas_call x4, Pallas kernels, factor_step(): pl.pallas_call(functools.partial(factor_kernel, index, copied is not None...  22.7 us
    ppermute x25, waiting for transfers between devices, swap(): lax.ppermute(value, axes, [(i, i ^ flip_of(i)) for i in range(lax.axis_si...  19.1 us
    pallas_call x2, Pallas kernels, slabs(): pl.pallas_call(functools.partial(slab_kernel, scale, chunk), in_specs=in_...  10.6 us
    pallas_call x1, Pallas kernels, finish(): pl.pallas_call(functools.partial(final_kernel, step_size, chunk), in_spec...  6.52 us
    pallas_call x1, Pallas kernels, load_all(): pl.pallas_call(functools.partial(load_kernel, scale, chunk), in_specs=[hb...  4.58 us
    pallas_call x1, Pallas kernels, pick_halves(): pl.pallas_call(pick_kernel, grid_spec=pltpu.PrefetchScalarGridSpec(num_sc...  2.18 us
  transfers between devices with their start and end apart: 25, of which 14 were waited for; matrix products, arithmetic and copies ran while one was open for 1% of the time, Pallas kernels for 33%

profile of v7, /device:TPU:0, one launch (start us, length us, event | category | flops | bytes accessed | tf_op | source)
XLA Modules:
  0.0 96.1 jit_solution(17213196068166654162)
XLA Ops:
  0.6 2.2 %pick.1 = (bf16[2,256,512]{2,1,0:T(8,128)(2,1)S(1)}, bf16[2,256,512]{2,1,0:T(8,128)(2,1)S(1)}) custom-call(s32[2,4]{1,0:T(2,128)} %tiles_ref.3, s32[1]{0:T(128)} %bitcast.1.core_ref.refs_5_, bf16[4096,512]{1,0:T(8,128)(2,1)} %feat_in.1), custom_call_target="tpu_custom_call" | custom-call | tf_op jit(solution)/shard_map/pick/pallas_call | solution.py:48
  3.4 1.5 %collective-permute-done = bf16[2,256,512]{2,1,0:T(8,128)(2,1)S(1)} collective-permute-done((bf16[2,256,512]{2,1,0:T(8,128)(2,1)S(1)}, bf16[2,256,512]{2,1,0:T(8,128)(2,1)S(1)}, u32[]{:S(2)}, u32[]{:S(2)}) %collective-permute-start) | collective-permute-done | bytes 524320 | tf_op jit(solution)/shard_map/ppermute | solution.py:65
  5.1 3.9 %collective-permute-start.3 = (bf16[2,64,512]{2,1,0:T(8,128)(2,1)S(1)}, bf16[2,64,512]{2,1,0:T(8,128)(2,1)S(1)}, u32[]{:S(2)}, u32[]{:S(2)}) collective-permute-start(bf16[2,64,512]{2,1,0:T(8,128)(2,1)S(1)} %get-tuple-element.121), channel_id=1, source_target_pairs={{0,5},{1,4},{2,7},{3,6},{4,1},{5,0},{6,3},{7,2},{8,13},{9,12},{10,... | collective-permute-start | bytes 393224 | tf_op jit(solution)/shard_map/ppermute | solution.py:65
  9.6 4.6 %load.1 = (f32[1,4096]{1,0:T(1,128)S(1)}, bf16[4096,512]{1,0:T(8,128)(2,1)S(1)}, f32[4096,128]{1,0:T(8,128)S(1)}, f32[4096,128]{1,0:T(8,128)S(1)}) custom-call(bf16[4096,512]{1,0:T(8,128)(2,1)} %feat_in.1, f32[4096,128]{1,0:T(8,128)} %res_in.1, f32[4096,128]{1,0:T(8,128)} %coef_in.1), custom_call_target="tpu_custom_call" | custom-call | flops 3000000000 | bytes 8388608 | tf_op jit(solution)/shard_map/load/pallas_call | solution.py:242
  14.2 1.4 %collective-permute-done.2 = bf16[2,64,512]{2,1,0:T(8,128)(2,1)S(1)} collective-permute-done((bf16[2,64,512]{2,1,0:T(8,128)(2,1)S(1)}, bf16[2,64,512]{2,1,0:T(8,128)(2,1)S(1)}, u32[]{:S(2)}, u32[]{:S(2)}) %collective-permute-start.2) | collective-permute-done | bytes 131104 | tf_op jit(solution)/shard_map/ppermute | solution.py:65
  15.9 1.6 %collective-permute-start.4 = (bf16[2,64,512]{2,1,0:T(8,128)(2,1)S(1)}, bf16[2,64,512]{2,1,0:T(8,128)(2,1)S(1)}, u32[]{:S(2)}, u32[]{:S(2)}) collective-permute-start(bf16[2,64,512]{2,1,0:T(8,128)(2,1)S(1)} %fusion.5), channel_id=1, source_target_pairs={{0,8},{1,9},{2,18},{3,19},{4,12},{5,13},{6,22},{7,23},{8,0},{9,1},... | collective-permute-start | bytes 393224 | tf_op jit(solution)/shard_map/ppermute | solution.py:65
  17.6 4.6 %collective-permute-done.4 = bf16[2,64,512]{2,1,0:T(8,128)(2,1)S(1)} collective-permute-done((bf16[2,64,512]{2,1,0:T(8,128)(2,1)S(1)}, bf16[2,64,512]{2,1,0:T(8,128)(2,1)S(1)}, u32[]{:S(2)}, u32[]{:S(2)}) %collective-permute-start.4) | collective-permute-done | bytes 131104 | tf_op jit(solution)/shard_map/ppermute | solution.py:65
  22.2 1.8 %collective-permute-start.5 = (bf16[2,64,512]{2,1,0:T(8,128)(2,1)S(1)}, bf16[2,64,512]{2,1,0:T(8,128)(2,1)S(1)}, u32[]{:S(2)}, u32[]{:S(2)}) collective-permute-start(bf16[2,64,512]{2,1,0:T(8,128)(2,1)S(1)} %broadcast_select_fusion.9), channel_id=1, source_target_pairs={{0,16},{1,17},{2,10},{3,11},{4,20},{5,21},{6,14},{7,15},{8,24},{9,... | collective-permute-start | bytes 393224 | tf_op jit(solution)/shard_map/ppermute | solution.py:65
  24.0 4.3 %collective-permute-done.5 = bf16[2,64,512]{2,1,0:T(8,128)(2,1)S(1)} collective-permute-done((bf16[2,64,512]{2,1,0:T(8,128)(2,1)S(1)}, bf16[2,64,512]{2,1,0:T(8,128)(2,1)S(1)}, u32[]{:S(2)}, u32[]{:S(2)}) %collective-permute-start.5) | collective-permute-done | bytes 131104 | tf_op jit(solution)/shard_map/ppermute | solution.py:65
  28.5 1.5 %collective-permute-start.8 = (bf16[2,64,512]{2,1,0:T(8,128)(2,1)S(1)}, bf16[2,64,512]{2,1,0:T(8,128)(2,1)S(1)}, u32[]{:S(2)}, u32[]{:S(2)}) collective-permute-start(bf16[2,64,512]{2,1,0:T(8,128)(2,1)S(1)} %broadcast_select_fusion.10), channel_id=1, source_target_pairs={{0,1},{1,0},{2,3},{3,2},{4,5},{5,4},{6,7},{7,6},{8,9},{9,8},{10,11... | collective-permute-start | bytes 393224 | tf_op jit(solution)/shard_map/ppermute | solution.py:65
  30.4 1.6 %collective-permute-start.6 = (bf16[2,64,512]{2,1,0:T(8,128)(2,1)S(1)}, bf16[2,64,512]{2,1,0:T(8,128)(2,1)S(1)}, u32[]{:S(2)}, u32[]{:S(2)}) collective-permute-start(bf16[2,64,512]{2,1,0:T(8,128)(2,1)S(1)} %broadcast_select_fusion.10), channel_id=1, source_target_pairs={{0,5},{1,4},{2,7},{3,6},{4,1},{5,0},{6,3},{7,2},{8,13},{9,12},{10,... | collective-permute-start | bytes 393224 | tf_op jit(solution)/shard_map/ppermute | solution.py:65
  32.0 1.9 %collective-permute-done.8 = bf16[2,64,512]{2,1,0:T(8,128)(2,1)S(1)} collective-permute-done((bf16[2,64,512]{2,1,0:T(8,128)(2,1)S(1)}, bf16[2,64,512]{2,1,0:T(8,128)(2,1)S(1)}, u32[]{:S(2)}, u32[]{:S(2)}) %collective-permute-start.8) | collective-permute-done | bytes 131104 | tf_op jit(solution)/shard_map/ppermute | solution.py:65
  34.0 1.0 %collective-permute-done.7 = bf16[2,64,512]{2,1,0:T(8,128)(2,1)S(1)} collective-permute-done((bf16[2,64,512]{2,1,0:T(8,128)(2,1)S(1)}, bf16[2,64,512]{2,1,0:T(8,128)(2,1)S(1)}, u32[]{:S(2)}, u32[]{:S(2)}) %collective-permute-start.7) | collective-permute-done | bytes 131104 | tf_op jit(solution)/shard_map/ppermute | solution.py:65
  34.9 1.4 %collective-permute-done.6 = bf16[2,64,512]{2,1,0:T(8,128)(2,1)S(1)} collective-permute-done((bf16[2,64,512]{2,1,0:T(8,128)(2,1)S(1)}, bf16[2,64,512]{2,1,0:T(8,128)(2,1)S(1)}, u32[]{:S(2)}, u32[]{:S(2)}) %collective-permute-start.6) | collective-permute-done | bytes 131104 | tf_op jit(solution)/shard_map/ppermute | solution.py:65
  36.5 3.6 %slabs.2 = (bf16[512,4096]{1,0:T(8,128)(2,1)S(1)}, f32[256,128]{1,0:T(8,128)S(1)}) custom-call(bf16[512,512]{1,0:T(8,128)(2,1)S(1)} %bitcast.74, bf16[4096,512]{1,0:T(8,128)(2,1)S(1)} %get-tuple-element.56.refs_1_, f32[1,4096]{1,0:T(1,128)S(1)} %get-tuple-element.57.refs_2_, f32[4096,128]{1,0:T(8,128)S(1)} %get-tuple-element.58.refs_3_.res_ref, ...), custom_call_target="tpu_custom_call" | custom-call | flops 2684354560 | bytes 12582912 | tf_op jit(solution)/shard_map/slabs/pallas_call | solution.py:354
  40.2 7.0 %slabs.3 = (bf16[512,4096]{1,0:T(8,128)(2,1)S(1)}, bf16[8,128,512]{2,1,0:T(8,128)(2,1)S(1)}) custom-call(bf16[512,512]{1,0:T(8,128)(2,1)S(1)} %collective-permute-done.9.refs_0_, bf16[4096,512]{1,0:T(8,128)(2,1)S(1)} %get-tuple-element.56.refs_1_, f32[1,4096]{1,0:T(1,128)S(1)} %get-tuple-element.57.refs_2_, ...), custom_call_target="tpu_custom_call" | custom-call | flops 4831838208 | bytes 12582912 | tf_op jit(solution)/shard_map/slabs/pallas_call | solution.py:354
  47.3 0.6 collective-permute-start.10
  48.1 0.6 gram.1.refs_0_
  48.7 0.7 collective-permute-done.10
  49.9 1.9 %collective-permute-start.13 = (bf16[128,512]{1,0:T(8,128)(2,1)S(1)}, bf16[128,512]{1,0:T(8,128)(2,1)S(1)}, u32[]{:S(2)}, u32[]{:S(2)}) collective-permute-start(bf16[128,512]{1,0:T(8,128)(2,1)S(1)} %get-tuple-element.114), channel_id=1, source_target_pairs={{0,5},{1,4},{2,7},{3,6},{4,1},{5,0},{6,3},{7,2},{8,13},{9,12},{10,... | collective-permute-start | bytes 393224 | tf_op jit(solution)/shard_map/ppermute | solution.py:65
  51.8 1.5 %collective-permute-start.12 = (bf16[128,512]{1,0:T(8,128)(2,1)S(1)}, bf16[128,512]{1,0:T(8,128)(2,1)S(1)}, u32[]{:S(2)}, u32[]{:S(2)}) collective-permute-start(bf16[128,512]{1,0:T(8,128)(2,1)S(1)} %get-tuple-element.115), channel_id=1, source_target_pairs={{0,4},{1,5},{2,6},{3,7},{4,0},{5,1},{6,2},{7,3},{8,12},{9,13},{10,... | collective-permute-start | bytes 393224 | tf_op jit(solution)/shard_map/ppermute | solution.py:65
  53.5 5.8 %factor.4 = (f32[256,512]{1,0:T(8,128)S(1)}, f32[4096,128]{1,0:T(8,128)}) custom-call(f32[512,512]{1,0:T(8,128)S(1)} %gram.1.refs_0_, bf16[512,4096]{1,0:T(8,128)(2,1)S(1)} %get-tuple-element.63.refs_6_.slab0_ref.refs_1_, bf16[512,4096]{1,0:T(8,128)(2,1)S(1)} %get-tuple-element.66.slab1_ref.refs_2_, f32[4096,128]{1,0:T(8,128)S(1)} %get-tuple-element.59.refs_4_.refs_3_.coef_ref), custom_call_target="tpu_custom_call" | custom-call | flops 6000000000 | bytes 4194304 | tf_op jit(solution)/shard_map/factor/pallas_call | solution.py:482
  59.9 4.1 %collective-permute-start.16 = (bf16[128,512]{1,0:T(8,128)(2,1)S(1)}, bf16[128,512]{1,0:T(8,128)(2,1)S(1)}, u32[]{:S(2)}, u32[]{:S(2)}) collective-permute-start(bf16[128,512]{1,0:T(8,128)(2,1)S(1)} %pad_maximum_fusion.5), channel_id=1, source_target_pairs={{0,24},{1,25},{2,26},{3,27},{4,28},{5,29},{6,30},{7,31},{8,16},{9,... | collective-permute-start | bytes 393224 | tf_op jit(solution)/shard_map/ppermute | solution.py:65
  64.0 0.6 collective-permute-start.14
  64.7 5.8 %factor.5 = (f32[256,512]{1,0:T(8,128)S(1)}, f32[256,512]{1,0:T(8,128)S(1)}, bf16[512,512]{1,0:T(8,128)(2,1)S(1)}) custom-call(f32[512,512]{1,0:T(8,128)S(1)} %gram.1.refs_0_, bf16[512,4096]{1,0:T(8,128)(2,1)S(1)} %get-tuple-element.63.refs_6_.slab0_ref.refs_1_, bf16[512,4096]{1,0:T(8,128)(2,1)S(1)} %get-tuple-element.66.slab1_ref.refs_2_, ...), custom_call_target="tpu_custom_call" | custom-call | flops 6000000000 | bytes 4194304 | tf_op jit(solution)/shard_map/factor/pallas_call | solution.py:482
  71.1 5.7 %factor.6 = (f32[256,512]{1,0:T(8,128)S(1)}, f32[128,512]{1,0:T(8,128)S(1)}) custom-call(f32[256,512]{1,0:T(8,128)S(1)} %get-tuple-element.72.refs_0_, bf16[512,4096]{1,0:T(8,128)(2,1)S(1)} %get-tuple-element.63.refs_6_.slab0_ref.refs_1_, bf16[512,4096]{1,0:T(8,128)(2,1)S(1)} %get-tuple-element.66.slab1_ref.refs_2_, f32[256,512]{1,0:T(8,128)S(1)} %get-tuple-element.73.refs_3_), custom_call_target="tpu_custom_call" | custom-call | flops 6000000000 | bytes 4194304 | tf_op jit(solution)/shard_map/factor/pallas_call | solution.py:482
  77.1 1.6 %collective-permute-start.21 = (bf16[128,512]{1,0:T(8,128)(2,1)S(1)}, bf16[128,512]{1,0:T(8,128)(2,1)S(1)}, u32[]{:S(2)}, u32[]{:S(2)}) collective-permute-start(bf16[128,512]{1,0:T(8,128)(2,1)S(1)} %pad_maximum_fusion.6), channel_id=1, source_target_pairs={{0,5},{1,4},{2,7},{3,6},{4,1},{5,0},{6,3},{7,2},{8,13},{9,12},{10,... | collective-permute-start | bytes 393224 | tf_op jit(solution)/shard_map/ppermute | solution.py:65
  78.7 1.4 %collective-permute-start.20 = (bf16[128,512]{1,0:T(8,128)(2,1)S(1)}, bf16[128,512]{1,0:T(8,128)(2,1)S(1)}, u32[]{:S(2)}, u32[]{:S(2)}) collective-permute-start(bf16[128,512]{1,0:T(8,128)(2,1)S(1)} %pad_maximum_fusion.6), channel_id=1, source_target_pairs={{0,4},{1,5},{2,6},{3,7},{4,0},{5,1},{6,2},{7,3},{8,12},{9,13},{10,... | collective-permute-start | bytes 393224 | tf_op jit(solution)/shard_map/ppermute | solution.py:65
  80.0 0.6 collective-permute-start.19
  80.7 5.4 %factor.7 = f32[256,512]{1,0:T(8,128)S(1)} custom-call(f32[128,512]{1,0:T(8,128)S(1)} %get-tuple-element.79.refs_0_, bf16[512,4096]{1,0:T(8,128)(2,1)S(1)} %get-tuple-element.63.refs_6_.slab0_ref.refs_1_, bf16[512,4096]{1,0:T(8,128)(2,1)S(1)} %get-tuple-element.66.slab1_ref.refs_2_, f32[256,512]{1,0:T(8,128)S(1)} %get-tuple-element.80.refs_3_), custom_call_target="tpu_custom_call" | custom-call | flops 6000000000 | bytes 4194304 | tf_op jit(solution)/shard_map/factor/pallas_call | solution.py:482
  87.6 0.9 collective-permute-done.23
  89.4 6.5 %finish.1 = (f32[4096,128]{1,0:T(8,128)}, f32[4096,128]{1,0:T(8,128)}) custom-call(s32[2]{0:T(128)S(1)} %copy-done.1, s32[2,4]{1,0:T(2,128)S(1)} %copy-done, s32[1]{0:T(128)} %bitcast.me_ref, s32[1]{0:T(128)} %bitcast.1.core_ref.refs_5_, bf16[8,128,512]{2,1,0:T(8,128)(2,1)S(1)} %bitcast.70, ...), custom_call_target="tpu_custom_call", output_to_operand_aliasing={{1}: (10, {})} | custom-call | flops 1073741824 | bytes 16777216 | tf_op jit(solution)/shard_map/finish/pallas_call | solution.py:611
  (87 shorter events, 7.1 us)
Async XLA Ops:
  0.6 2.7 %copy-start.1 = (s32[2]{0:T(128)S(1)}, s32[2]{0:T(128)}, u32[]{:S(2)}) copy-start(s32[2]{0:T(128)} %owner_ref.1) | copy-start | bytes 28
  2.8 2.1 %collective-permute-start = (bf16[2,256,512]{2,1,0:T(8,128)(2,1)S(1)}, bf16[2,256,512]{2,1,0:T(8,128)(2,1)S(1)}, u32[]{:S(2)}, u32[]{:S(2)}) collective-permute-start(bf16[2,256,512]{2,1,0:T(8,128)(2,1)S(1)} %get-tuple-element.47), channel_id=1, source_target_pairs={{0,2},{1,3},{2,0},{3,1},{4,6},{5,7},{6,4},{7,5},{8,10},{9,11},{10,... | collective-permute-start | bytes 1572872 | tf_op jit(solution)/shard_map/ppermute | solution.py:65
  5.1 9.1 %collective-permute-start.3 = (bf16[2,64,512]{2,1,0:T(8,128)(2,1)S(1)}, bf16[2,64,512]{2,1,0:T(8,128)(2,1)S(1)}, u32[]{:S(2)}, u32[]{:S(2)}) collective-permute-start(bf16[2,64,512]{2,1,0:T(8,128)(2,1)S(1)} %get-tuple-element.121), channel_id=1, source_target_pairs={{0,5},{1,4},{2,7},{3,6},{4,1},{5,0},{6,3},{7,2},{8,13},{9,12},{10,... | collective-permute-start | bytes 393224 | tf_op jit(solution)/shard_map/ppermute | solution.py:65
  8.9 6.6 %collective-permute-start.2 = (bf16[2,64,512]{2,1,0:T(8,128)(2,1)S(1)}, bf16[2,64,512]{2,1,0:T(8,128)(2,1)S(1)}, u32[]{:S(2)}, u32[]{:S(2)}) collective-permute-start(bf16[2,64,512]{2,1,0:T(8,128)(2,1)S(1)} %get-tuple-element.122), channel_id=1, source_target_pairs={{0,4},{1,5},{2,6},{3,7},{4,0},{5,1},{6,2},{7,3},{8,12},{9,13},{10,... | collective-permute-start | bytes 393224 | tf_op jit(solution)/shard_map/ppermute | solution.py:65
  9.4 6.4 %collective-permute-start.1 = (bf16[2,64,512]{2,1,0:T(8,128)(2,1)S(1)}, bf16[2,64,512]{2,1,0:T(8,128)(2,1)S(1)}, u32[]{:S(2)}, u32[]{:S(2)}) collective-permute-start(bf16[2,64,512]{2,1,0:T(8,128)(2,1)S(1)} %get-tuple-element.123), channel_id=1, source_target_pairs={{0,1},{1,0},{2,3},{3,2},{4,5},{5,4},{6,7},{7,6},{8,9},{9,8},{10,11... | collective-permute-start | bytes 393224 | tf_op jit(solution)/shard_map/ppermute | solution.py:65
  15.9 6.2 %collective-permute-start.4 = (bf16[2,64,512]{2,1,0:T(8,128)(2,1)S(1)}, bf16[2,64,512]{2,1,0:T(8,128)(2,1)S(1)}, u32[]{:S(2)}, u32[]{:S(2)}) collective-permute-start(bf16[2,64,512]{2,1,0:T(8,128)(2,1)S(1)} %fusion.5), channel_id=1, source_target_pairs={{0,8},{1,9},{2,18},{3,19},{4,12},{5,13},{6,22},{7,23},{8,0},{9,1},... | collective-permute-start | bytes 393224 | tf_op jit(solution)/shard_map/ppermute | solution.py:65
  22.2 6.1 %collective-permute-start.5 = (bf16[2,64,512]{2,1,0:T(8,128)(2,1)S(1)}, bf16[2,64,512]{2,1,0:T(8,128)(2,1)S(1)}, u32[]{:S(2)}, u32[]{:S(2)}) collective-permute-start(bf16[2,64,512]{2,1,0:T(8,128)(2,1)S(1)} %broadcast_select_fusion.9), channel_id=1, source_target_pairs={{0,16},{1,17},{2,10},{3,11},{4,20},{5,21},{6,14},{7,15},{8,24},{9,... | collective-permute-start | bytes 393224 | tf_op jit(solution)/shard_map/ppermute | solution.py:65
  28.5 5.5 %collective-permute-start.8 = (bf16[2,64,512]{2,1,0:T(8,128)(2,1)S(1)}, bf16[2,64,512]{2,1,0:T(8,128)(2,1)S(1)}, u32[]{:S(2)}, u32[]{:S(2)}) collective-permute-start(bf16[2,64,512]{2,1,0:T(8,128)(2,1)S(1)} %broadcast_select_fusion.10), channel_id=1, source_target_pairs={{0,1},{1,0},{2,3},{3,2},{4,5},{5,4},{6,7},{7,6},{8,9},{9,8},{10,11... | collective-permute-start | bytes 393224 | tf_op jit(solution)/shard_map/ppermute | solution.py:65
  30.0 5.0 %collective-permute-start.7 = (bf16[2,64,512]{2,1,0:T(8,128)(2,1)S(1)}, bf16[2,64,512]{2,1,0:T(8,128)(2,1)S(1)}, u32[]{:S(2)}, u32[]{:S(2)}) collective-permute-start(bf16[2,64,512]{2,1,0:T(8,128)(2,1)S(1)} %broadcast_select_fusion.10), channel_id=1, source_target_pairs={{0,4},{1,5},{2,6},{3,7},{4,0},{5,1},{6,2},{7,3},{8,12},{9,13},{10,... | collective-permute-start | bytes 393224 | tf_op jit(solution)/shard_map/ppermute | solution.py:65
  30.4 5.9 %collective-permute-start.6 = (bf16[2,64,512]{2,1,0:T(8,128)(2,1)S(1)}, bf16[2,64,512]{2,1,0:T(8,128)(2,1)S(1)}, u32[]{:S(2)}, u32[]{:S(2)}) collective-permute-start(bf16[2,64,512]{2,1,0:T(8,128)(2,1)S(1)} %broadcast_select_fusion.10), channel_id=1, source_target_pairs={{0,5},{1,4},{2,7},{3,6},{4,1},{5,0},{6,3},{7,2},{8,13},{9,12},{10,... | collective-permute-start | bytes 393224 | tf_op jit(solution)/shard_map/ppermute | solution.py:65
  36.5 3.7 %collective-permute-start.9 = (bf16[512,512]{1,0:T(8,128)(2,1)S(1)}, bf16[512,512]{1,0:T(8,128)(2,1)S(1)}, u32[]{:S(2)}, u32[]{:S(2)}) collective-permute-start(bf16[512,512]{1,0:T(8,128)(2,1)S(1)} %bitcast.73), channel_id=1, source_target_pairs={{0,2},{1,3},{2,0},{3,1},{4,6},{5,7},{6,4},{7,5},{8,10},{9,11},{10,... | collective-permute-start | bytes 1572872 | tf_op jit(solution)/shard_map/ppermute | solution.py:65
  47.3 2.1 %collective-permute-start.10 = (bf16[2,2,128,512]{3,2,1,0:T(8,128)(2,1)S(1)}, bf16[2,2,128,512]{3,2,1,0:T(8,128)(2,1)S(1)}, u32[]{:S(2)}, u32[]{:S(2)}) collective-permute-start(bf16[2,2,128,512]{3,2,1,0:T(8,128)(2,1)S(1)} %get-tuple-element.106), channel_id=1, source_target_pairs={{0,2},{1,3},{2,0},{3,1},{4,6},{5,7},{6,4},{7,5},{8,10},{9,11},{10,... | collective-permute-start | bytes 1572872 | tf_op jit(solution)/shard_map/ppermute | solution.py:65
  49.9 9.4 %collective-permute-start.13 = (bf16[128,512]{1,0:T(8,128)(2,1)S(1)}, bf16[128,512]{1,0:T(8,128)(2,1)S(1)}, u32[]{:S(2)}, u32[]{:S(2)}) collective-permute-start(bf16[128,512]{1,0:T(8,128)(2,1)S(1)} %get-tuple-element.114), channel_id=1, source_target_pairs={{0,5},{1,4},{2,7},{3,6},{4,1},{5,0},{6,3},{7,2},{8,13},{9,12},{10,... | collective-permute-start | bytes 393224 | tf_op jit(solution)/shard_map/ppermute | solution.py:65
  51.8 7.7 %collective-permute-start.12 = (bf16[128,512]{1,0:T(8,128)(2,1)S(1)}, bf16[128,512]{1,0:T(8,128)(2,1)S(1)}, u32[]{:S(2)}, u32[]{:S(2)}) collective-permute-start(bf16[128,512]{1,0:T(8,128)(2,1)S(1)} %get-tuple-element.115), channel_id=1, source_target_pairs={{0,4},{1,5},{2,6},{3,7},{4,0},{5,1},{6,2},{7,3},{8,12},{9,13},{10,... | collective-permute-start | bytes 393224 | tf_op jit(solution)/shard_map/ppermute | solution.py:65
  53.4 6.2 %collective-permute-start.11 = (bf16[128,512]{1,0:T(8,128)(2,1)S(1)}, bf16[128,512]{1,0:T(8,128)(2,1)S(1)}, u32[]{:S(2)}, u32[]{:S(2)}) collective-permute-start(bf16[128,512]{1,0:T(8,128)(2,1)S(1)} %get-tuple-element.116), channel_id=1, source_target_pairs={{0,1},{1,0},{2,3},{3,2},{4,5},{5,4},{6,7},{7,6},{8,9},{9,8},{10,11... | collective-permute-start | bytes 393224 | tf_op jit(solution)/shard_map/ppermute | solution.py:65
  59.9 16.9 %collective-permute-start.16 = (bf16[128,512]{1,0:T(8,128)(2,1)S(1)}, bf16[128,512]{1,0:T(8,128)(2,1)S(1)}, u32[]{:S(2)}, u32[]{:S(2)}) collective-permute-start(bf16[128,512]{1,0:T(8,128)(2,1)S(1)} %pad_maximum_fusion.5), channel_id=1, source_target_pairs={{0,24},{1,25},{2,26},{3,27},{4,28},{5,29},{6,30},{7,31},{8,16},{9,... | collective-permute-start | bytes 393224 | tf_op jit(solution)/shard_map/ppermute | solution.py:65
  64.0 12.7 %collective-permute-start.15 = (bf16[128,512]{1,0:T(8,128)(2,1)S(1)}, bf16[128,512]{1,0:T(8,128)(2,1)S(1)}, u32[]{:S(2)}, u32[]{:S(2)}) collective-permute-start(bf16[128,512]{1,0:T(8,128)(2,1)S(1)} %pad_maximum_fusion.5), channel_id=1, source_target_pairs={{0,16},{1,17},{2,18},{3,19},{4,20},{5,21},{6,22},{7,23},{8,24},{9,... | collective-permute-start | bytes 393224 | tf_op jit(solution)/shard_map/ppermute | solution.py:65
  64.0 12.7 %collective-permute-start.14 = (bf16[128,512]{1,0:T(8,128)(2,1)S(1)}, bf16[128,512]{1,0:T(8,128)(2,1)S(1)}, u32[]{:S(2)}, u32[]{:S(2)}) collective-permute-start(bf16[128,512]{1,0:T(8,128)(2,1)S(1)} %pad_maximum_fusion.5), channel_id=1, source_target_pairs={{0,8},{1,9},{2,10},{3,11},{4,12},{5,13},{6,14},{7,15},{8,0},{9,1},... | collective-permute-start | bytes 393224 | tf_op jit(solution)/shard_map/ppermute | solution.py:65
  70.5 6.3 %collective-permute-start.17 = (f32[256,512]{1,0:T(8,128)S(1)}, f32[256,512]{1,0:T(8,128)S(1)}, u32[]{:S(2)}, u32[]{:S(2)}) collective-permute-start(f32[256,512]{1,0:T(8,128)S(1)} %get-tuple-element.71.refs_3_), channel_id=1, source_target_pairs={{0,2},{1,3},{2,0},{3,1},{4,6},{5,7},{6,4},{7,5},{8,10},{9,11},{10,... | collective-permute-start | bytes 1572872 | tf_op jit(solution)/shard_map/ppermute | solution.py:65
  70.6 6.2 %collective-permute-start.18 = (f32[256,512]{1,0:T(8,128)S(1)}, f32[256,512]{1,0:T(8,128)S(1)}, u32[]{:S(2)}, u32[]{:S(2)}) collective-permute-start(f32[256,512]{1,0:T(8,128)S(1)} %get-tuple-element.73.refs_3_), channel_id=1, source_target_pairs={{0,2},{1,3},{2,0},{3,1},{4,6},{5,7},{6,4},{7,5},{8,10},{9,11},{10,... | collective-permute-start | bytes 1572872 | tf_op jit(solution)/shard_map/ppermute | solution.py:65
  77.1 9.0 %collective-permute-start.21 = (bf16[128,512]{1,0:T(8,128)(2,1)S(1)}, bf16[128,512]{1,0:T(8,128)(2,1)S(1)}, u32[]{:S(2)}, u32[]{:S(2)}) collective-permute-start(bf16[128,512]{1,0:T(8,128)(2,1)S(1)} %pad_maximum_fusion.6), channel_id=1, source_target_pairs={{0,5},{1,4},{2,7},{3,6},{4,1},{5,0},{6,3},{7,2},{8,13},{9,12},{10,... | collective-permute-start | bytes 393224 | tf_op jit(solution)/shard_map/ppermute | solution.py:65
  78.7 7.7 %collective-permute-start.20 = (bf16[128,512]{1,0:T(8,128)(2,1)S(1)}, bf16[128,512]{1,0:T(8,128)(2,1)S(1)}, u32[]{:S(2)}, u32[]{:S(2)}) collective-permute-start(bf16[128,512]{1,0:T(8,128)(2,1)S(1)} %pad_maximum_fusion.6), channel_id=1, source_target_pairs={{0,4},{1,5},{2,6},{3,7},{4,0},{5,1},{6,2},{7,3},{8,12},{9,13},{10,... | collective-permute-start | bytes 393224 | tf_op jit(solution)/shard_map/ppermute | solution.py:65
  80.0 6.3 %collective-permute-start.19 = (bf16[128,512]{1,0:T(8,128)(2,1)S(1)}, bf16[128,512]{1,0:T(8,128)(2,1)S(1)}, u32[]{:S(2)}, u32[]{:S(2)}) collective-permute-start(bf16[128,512]{1,0:T(8,128)(2,1)S(1)} %pad_maximum_fusion.6), channel_id=1, source_target_pairs={{0,1},{1,0},{2,3},{3,2},{4,5},{5,4},{6,7},{7,6},{8,9},{9,8},{10,11... | collective-permute-start | bytes 393224 | tf_op jit(solution)/shard_map/ppermute | solution.py:65
  80.7 5.7 %collective-permute-start.22 = (f32[256,512]{1,0:T(8,128)S(1)}, f32[256,512]{1,0:T(8,128)S(1)}, u32[]{:S(2)}, u32[]{:S(2)}) collective-permute-start(f32[256,512]{1,0:T(8,128)S(1)} %get-tuple-element.80.refs_3_), channel_id=1, source_target_pairs={{0,2},{1,3},{2,0},{3,1},{4,6},{5,7},{6,4},{7,5},{8,10},{9,11},{10,... | collective-permute-start | bytes 1572872 | tf_op jit(solution)/shard_map/ppermute | solution.py:65
  86.6 2.0 %collective-permute-start.23 = (bf16[2,2,128,512]{3,2,1,0:T(8,128)(2,1)S(1)}, bf16[2,2,128,512]{3,2,1,0:T(8,128)(2,1)S(1)}, u32[]{:S(2)}, u32[]{:S(2)}) collective-permute-start(bf16[2,2,128,512]{3,2,1,0:T(8,128)(2,1)S(1)} %bitcast.78), channel_id=1, source_target_pairs={{0,2},{1,3},{2,0},{3,1},{4,6},{5,7},{6,4},{7,5},{8,10},{9,11},{10,... | collective-permute-start | bytes 1572872 | tf_op jit(solution)/shard_map/ppermute | solution.py:65
  86.9 2.4 %collective-permute-start.24 = (f32[256,512]{1,0:T(8,128)S(1)}, f32[256,512]{1,0:T(8,128)S(1)}, u32[]{:S(2)}, u32[]{:S(2)}) collective-permute-start(f32[256,512]{1,0:T(8,128)S(1)} %factor.7), channel_id=1, source_target_pairs={{0,2},{1,3},{2,0},{3,1},{4,6},{5,7},{6,4},{7,5},{8,10},{9,11},{10,... | collective-permute-start | bytes 1572872 | tf_op jit(solution)/shard_map/ppermute | solution.py:65
  88.7 0.7 copy-start
